TPU v7x, 32 devices: a whole 2x2x4 slice. The times are simulated.
32 devices in a mesh: lat: 4 (over y, core), lon: 8 (over z, x).
Axes of the slice: x: 2, y: 2, z: 4, core: 2. Of those that a mesh axis runs over, the one named last changes fastest.
Arguments:
- latent: bfloat16 [24, 2, 64, 640], P('lat', None, 'lon'), may hold values from -6 to 6
- norm_gain: float32 [640], replicated, may hold values from 0.25 to 1.75
- filters: bfloat16 [9, 24, 4, 8], P(None, 'lat'), may hold values from -1 to 1
- row_offsets: int32 [24, 4], P('lat'), may hold values from -2 to 2
- col_offsets: int32 [24, 4], P('lat'), may hold values from -6 to -2
- mix_weight: bfloat16 [9, 640, 640], P(None, 'lat', 'lon'), may hold values from -0.078125 to 0.078125
- up_weight: bfloat16 [640, 1280], P('lat', 'lon'), may hold values from -0.25 to 0.25
- up_bias: float32 [1280], replicated, may hold values from -3 to 3
- down_weight: bfloat16 [1280, 640], P('lat', 'lon'), may hold values from -0.15625 to 0.15625
Outputs:
- output: bfloat16 [24, 2, 64, 640], P('lat', None, 'lon')
All inputs are finite; a program needn't handle non-finite values.
Results may differ from a plain program's by a relative error of at most 0.0059.
Values may be sent and summed in bfloat16 or wider, within the bound.
No kernel may reach another device: no remote copies, remote signals or barrier semaphores. Data moves between devices by JAX's collectives and lax.ppermute only.
A program may use at most 64 MiB of HBM per device.

v0:
```python
import jax
import jax.numpy as jnp
from jax import lax
from jax.sharding import PartitionSpec as P

KB = 9
R = 4
BW = 8
HREACH = 2


EPSILON = 1e-05


def padded(shard, sides, width, wrap):
    for axis, dim in sides:
        size, length = (lax.axis_size(axis), shard.shape[dim])
        up = [(i, (i + 1) % size) for i in range(size if wrap else size - 1)]
        down = [(j, i) for i, j in up]
        last = lax.slice_in_dim(shard, length - width, length, axis=dim)
        leading = lax.slice_in_dim(shard, 0, width, axis=dim)
        before = lax.ppermute(last, axis, up)
        after = lax.ppermute(leading, axis, down)
        shard = jnp.concatenate([before, shard, after], axis=dim)
    return shard


def normalize(latent, norm_gain):
    widened = latent.astype(jnp.float32)
    channel_mean = jnp.mean(widened, axis=-1, keepdims=True)
    centered = widened - channel_mean
    variance = jnp.mean(centered * centered, axis=-1, keepdims=True)
    return (centered * lax.rsqrt(variance + EPSILON) * norm_gain).astype(jnp.bfloat16)


def contract_cycles(
    band_slab, filters, row_offsets, col_offsets, cycle_count, out_cells, shift_cells
):
    members = band_slab.shape[1]
    channel_share = band_slab.shape[3]

    def cycle_output(cycle_index):
        pieces = []
        for row_slot in range(R):
            where = cycle_index + HREACH + row_offsets[cycle_index, row_slot]
            source = lax.dynamic_index_in_dim(band_slab, where, 0, keepdims=False)
            start = col_offsets[cycle_index, row_slot] + shift_cells
            segment = lax.dynamic_slice_in_dim(source, start, out_cells + BW - 1, 1)
            for band_step in range(BW):
                pieces.append(segment[:, band_step : band_step + out_cells])
        stacked = jnp.stack(pieces).reshape(R * BW, members * out_cells * channel_share)
        cycle_filter = lax.dynamic_index_in_dim(filters, cycle_index, 1, keepdims=False).reshape(
            KB, R * BW
        )
        contracted = jnp.dot(cycle_filter, stacked, preferred_element_type=jnp.float32).astype(
            jnp.bfloat16
        )
        return contracted.reshape(KB, members, out_cells, channel_share)

    return lax.map(cycle_output, jnp.arange(cycle_count, dtype=jnp.int32))


def shards(
    latent,
    norm_gain,
    filters,
    row_offsets,
    col_offsets,
    mix_weight,
    up_weight,
    up_bias,
    down_weight,
):
    cycle_count = latent.shape[0]
    local_cells = latent.shape[2]
    width = latent.shape[3]
    partial_weights = (
        lax.all_gather(mix_weight, "lat", axis=1, tiled=True),
        lax.all_gather(up_weight, "lat", axis=0, tiled=True),
        lax.all_gather(down_weight, "lat", axis=0, tiled=True),
    )
    mix_full, up_full, down_full = (
        lax.all_gather(partial_weights[0], "lon", axis=2, tiled=True),
        lax.all_gather(partial_weights[1], "lon", axis=1, tiled=True),
        lax.all_gather(partial_weights[2], "lon", axis=1, tiled=True),
    )
    normalized = normalize(latent, norm_gain)
    side_reach = BW // 2 + 2
    cycle_rims = padded(normalized, (("lat", 0),), HREACH, False)
    band_slab = padded(cycle_rims, (("lon", 2),), side_reach, True)
    contracted = contract_cycles(
        band_slab, filters, row_offsets, col_offsets, cycle_count, local_cells, side_reach
    )
    convolved = jnp.einsum(
        "ikejc,kcd->iejd", contracted, mix_full, preferred_element_type=jnp.float32
    )
    hidden = (latent.astype(jnp.float32) + convolved).astype(jnp.bfloat16)
    flattened = hidden.reshape(-1, width)
    lifted = jnp.dot(flattened, up_full, preferred_element_type=jnp.float32) + up_bias
    activated = jax.nn.gelu(lifted, approximate=False).astype(jnp.bfloat16)
    result = flattened.astype(jnp.float32) + jnp.dot(
        activated, down_full, preferred_element_type=jnp.float32
    )
    return result.astype(jnp.bfloat16).reshape(latent.shape)


def solution(mesh):
    in_specs = (
        P("lat", None, "lon", None),
        P(),
        P(None, "lat", None, None),
        P("lat", None),
        P("lat", None),
        P(None, "lat", "lon"),
        P("lat", "lon"),
        P(),
        P("lat", "lon"),
    )
    out_specs = P("lat", None, "lon", None)
    return jax.shard_map(shards, mesh=mesh, in_specs=in_specs, out_specs=out_specs, check_vma=False)
```

profile of v0, /device:TPU:0, one launch (start us, length us, event | category | flops | bytes accessed | tf_op | source)
XLA Modules:
  0.0 250.1 jit_solution(8357053591402037838)
XLA Ops:
  6.5 1.2 copy.20
  7.7 20.1 %all_gather.18 = bf16[9,640,80]{2,0,1:T(8,128)(2,1)S(1)} all-gather(bf16[9,160,80]{2,0,1:T(8,128)(2,1)S(1)} %copy.20), channel_id=1, replica_groups=mesh['lat'=4,'lon'=8] {'lat'}, dimensions={1}, use_global_device_ids=true | all-gather | bytes 1152000 | tf_op jit(solution)/shard_map/all_gather | solution.py:78
  27.8 3.0 %copy.21 = bf16[9,640,80]{1,2,0:T(8,128)(2,1)} copy(bf16[9,640,80]{2,0,1:T(8,128)(2,1)S(1)} %all_gather.18) | data formatting | bytes 1843200 | tf_op jit(solution)/shard_map/all_gather | solution.py:78
  30.9 5.8 %all-gather = bf16[4,320,80]{1,2,0:T(8,128)(2,1)S(1)} all-gather(bf16[1,320,80]{1,2,0:T(8,128)(2,1)S(1)} %bitcast.99), channel_id=1, replica_groups=mesh['lat'=4,'lon'=8] {'lat'}, dimensions={0}, use_global_device_ids=true | all-gather | bytes 256000 | tf_op jit(solution)/shard_map/all_gather | solution.py:80
  36.8 0.9 reshape.262
  38.2 2.3 collective-permute-start
  40.5 1.3 collective-permute-start.1
  41.8 2.2 collective-permute-done.1
  44.1 1.5 collective-permute-start.2
  45.6 3.2 %collective-permute-start.3 = (bf16[10,2,6,640]{3,2,1,0:T(8,128)(2,1)S(1)}, bf16[10,2,6,640]{3,2,1,0:T(8,128)(2,1)S(1)}, u32[]{:S(2)}, u32[]{:S(2)}) collective-permute-start(bf16[10,2,6,640]{3,2,1,0:T(8,128)(2,1)S(1)} %get-tuple-element.192), channel_id=1, source_target_pairs={{1,0},{2,1},{3,2},{4,3},{5,4},{6,5},{7,6},{0,7},{9,8},{10,9},{11,1... | collective-permute-start | bytes 460808 | tf_op jit(solution)/shard_map/ppermute | solution.py:23
  48.8 7.7 %all_gather.20 = bf16[640,160]{1,0:T(8,128)(2,1)S(1)} all-gather(bf16[160,160]{1,0:T(8,128)(2,1)S(1)} %copy-done.1), channel_id=1, replica_groups=mesh['lat'=4,'lon'=8] {'lat'}, dimensions={0}, use_global_device_ids=true | all-gather | bytes 256000 | tf_op jit(solution)/shard_map/all_gather | solution.py:79
  56.6 0.8 copy.23
  57.4 0.9 collective-permute-done.2
  58.4 2.5 %collective-permute-done.3 = bf16[10,2,6,640]{3,2,1,0:T(8,128)(2,1)S(1)} collective-permute-done((bf16[10,2,6,640]{3,2,1,0:T(8,128)(2,1)S(1)}, bf16[10,2,6,640]{3,2,1,0:T(8,128)(2,1)S(1)}, u32[]{:S(2)}, u32[]{:S(2)}) %collective-permute-start.3) | collective-permute-done | bytes 153632 | tf_op jit(solution)/shard_map/ppermute | solution.py:23
  61.2 93.2 %while.13 = (s32[]{:T(128)}, bf16[6,9,2,8,640]{4,3,1,2,0:T(8,128)(2,1)}, s32[6]{0:T(128)S(1)}, bf16[9,6,4,8]{0,3,2,1:T(8,128)(2,1)}, s32[6,4]{0,1:T(4,128)S(1)},...) while((s32[]{:T(128)}, ...), condition=%wide.region_3.4_spmd, body=%wide.region_2.3_spmd.sunk | while | flops 5990446 | bytes 6112551 | solution.py:60
  72.8 2.2 stack.164
  75.0 1.0 convolution_convert_fusion.2
  76.1 0.7 copy_dynamic-update-slice_fusion.2
  88.4 2.2 stack.164
  90.6 1.0 convolution_convert_fusion.2
  103.9 2.2 stack.164
  106.1 1.0 convolution_convert_fusion.2
  119.4 2.2 stack.164
  121.6 1.0 convolution_convert_fusion.2
  134.9 2.2 stack.164
  137.2 1.0 convolution_convert_fusion.2
  150.5 2.2 stack.164
  152.7 1.0 convolution_convert_fusion.2
  154.4 5.8 %fusion.11 = bf16[6,2,8,640]{3,2,1,0:T(8,128)(2,1)S(1)} fusion(bf16[6,9,2,8,640]{4,3,1,2,0:T(8,128)(2,1)} %get-tuple-element.128, bf16[9,640,640]{1,2,0:T(8,128)(2,1)} %all-gather.5.cloned.1.call-done, bf16[6,2,8,640]{3,2,1,0:T(8,128)(2,1)S(1)} %copy-done), kind=kOutput, calls=%fused_computation.24 | convolution fusion | flops 707973120 | bytes 8724480 | tf_op jit(solution)/shard_map/ikejc,kcd->iejd/dot_general | solution.py:94
  160.2 33.4 %all-gather.9.cloned.1.call-done = bf16[1280,640]{0,1:T(8,128)(2,1)} async-done(((bf16[1280,80]{0,1:T(8,128)(2,1)}), bf16[1280,640]{0,1:T(8,128)(2,1)}) %all-gather.9.cloned.1.call-update) | async-done | bytes 1638416 | tf_op jit(solution)/shard_map/all_gather | solution.py:85
  193.6 45.6 %all-gather.7.cloned.1.call-done = bf16[640,1280]{0,1:T(8,128)(2,1)} async-done(((bf16[640,160]{0,1:T(8,128)(2,1)}), bf16[640,1280]{0,1:T(8,128)(2,1)}) %all-gather.7.cloned.1.call-update) | async-done | bytes 1638416 | tf_op jit(solution)/shard_map/all_gather | solution.py:84
  239.2 4.4 %fusion.14 = bf16[96,640]{1,0:T(8,128)(2,1)} fusion(bf16[1280,640]{0,1:T(8,128)(2,1)} %all-gather.9.cloned.1.call-done, bf16[96,640]{1,0:T(8,128)(2,1)S(1)} %bitcast.98, bf16[640,1280]{0,1:T(8,128)(2,1)} %all-gather.7.cloned.1.call-done, f32[1280]{0:T(1024)S(1)} %copy-done.6), kind=kOutput, calls=%fused_computation.25 | convolution fusion | flops 322867200 | bytes 3527680 | tf_op jit(solution)/shard_map/dot_general | solution.py:101
  (279 shorter events, 16.2 us)
Async XLA Ops:
  6.5 147.9 %all-gather.5.cloned.1.call-start = ((), (), s32[]{:S(2)}) async-start(), calls=%async_computation | async-start | bytes 8294400 | tf_op jit(solution)/shard_map/all_gather | solution.py:83
  27.8 3.1 %copy-start.2 = (bf16[320,80]{0,1:T(8,128)(2,1)S(1)}, bf16[320,80]{0,1:T(8,128)(2,1)}, u32[]{:S(2)}) copy-start(bf16[320,80]{0,1:T(8,128)(2,1)} %param.19) | copy-start | bytes 153604
  30.8 7.0 %copy-start = (bf16[6,2,8,640]{3,2,1,0:T(8,128)(2,1)S(1)}, bf16[6,2,8,640]{3,2,1,0:T(8,128)(2,1)}, u32[]{:S(2)}) copy-start(bf16[6,2,8,640]{3,2,1,0:T(8,128)(2,1)} %param.11) | copy-start | bytes 368644
  30.8 7.3 %copy-start.5 = (f32[640]{0:T(1024)S(1)}, f32[640]{0:T(1024)}, u32[]{:S(2)}) copy-start(f32[640]{0:T(1024)} %param.12) | copy-start | bytes 7684
  30.8 162.8 %all-gather.9.cloned.1.call-start = ((), (), s32[]{:S(2)}) async-start(), calls=%async_computation.2 | async-start | bytes 1843200 | tf_op jit(solution)/shard_map/all_gather | solution.py:85
  36.8 12.1 %copy-start.1 = (bf16[160,160]{1,0:T(8,128)(2,1)S(1)}, bf16[160,160]{1,0:T(8,128)(2,1)}, u32[]{:S(2)}) copy-start(bf16[160,160]{1,0:T(8,128)(2,1)} %param.17) | copy-start | bytes 153604
  37.7 201.5 %all-gather.7.cloned.1.call-start = ((), (), s32[]{:S(2)}) async-start(), calls=%async_computation.1 | async-start | bytes 1843200 | tf_op jit(solution)/shard_map/all_gather | solution.py:84
  38.2 3.6 %collective-permute-start = (bf16[2,2,8,640]{3,2,1,0:T(8,128)(2,1)S(1)}, bf16[2,2,8,640]{3,2,1,0:T(8,128)(2,1)S(1)}, u32[]{:S(2)}, u32[]{:S(2)}) collective-permute-start(bf16[2,2,8,640]{3,2,1,0:T(8,128)(2,1)S(1)} %get-tuple-element.193), channel_id=1, source_target_pairs={{0,8},{8,16},{16,24},{1,9},{9,17},{17,25},{2,10},{10,18},{18,26},{... | collective-permute-start | bytes 122888 | tf_op jit(solution)/shard_map/ppermute | solution.py:22
  40.5 3.5 %collective-permute-start.1 = (bf16[2,2,8,640]{3,2,1,0:T(8,128)(2,1)S(1)}, bf16[2,2,8,640]{3,2,1,0:T(8,128)(2,1)S(1)}, u32[]{:S(2)}, u32[]{:S(2)}) collective-permute-start(bf16[2,2,8,640]{3,2,1,0:T(8,128)(2,1)S(1)} %get-tuple-element.194), channel_id=1, source_target_pairs={{8,0},{16,8},{24,16},{9,1},{17,9},{25,17},{10,2},{18,10},{26,18},{... | collective-permute-start | bytes 122888 | tf_op jit(solution)/shard_map/ppermute | solution.py:23
  44.0 17.2 %copy-start.3 = (s32[6,4]{0,1:T(4,128)S(1)}, s32[6,4]{0,1:T(4,128)}, u32[]{:S(2)}) copy-start(s32[6,4]{0,1:T(4,128)} %param.14) | copy-start | bytes 292
  44.1 17.2 %copy-start.4 = (s32[6,4]{0,1:T(4,128)S(1)}, s32[6,4]{0,1:T(4,128)}, u32[]{:S(2)}) copy-start(s32[6,4]{0,1:T(4,128)} %param.15) | copy-start | bytes 292
  44.1 14.3 %collective-permute-start.2 = (bf16[10,2,6,640]{3,2,1,0:T(8,128)(2,1)S(1)}, bf16[10,2,6,640]{3,2,1,0:T(8,128)(2,1)S(1)}, u32[]{:S(2)}, u32[]{:S(2)}) collective-permute-start(bf16[10,2,6,640]{3,2,1,0:T(8,128)(2,1)S(1)} %get-tuple-element.191), channel_id=1, source_target_pairs={{0,1},{1,2},{2,3},{3,4},{4,5},{5,6},{6,7},{7,0},{8,9},{9,10},{10,1... | collective-permute-start | bytes 460808 | tf_op jit(solution)/shard_map/ppermute | solution.py:22
  45.6 15.3 %collective-permute-start.3 = (bf16[10,2,6,640]{3,2,1,0:T(8,128)(2,1)S(1)}, bf16[10,2,6,640]{3,2,1,0:T(8,128)(2,1)S(1)}, u32[]{:S(2)}, u32[]{:S(2)}) collective-permute-start(bf16[10,2,6,640]{3,2,1,0:T(8,128)(2,1)S(1)} %get-tuple-element.192), channel_id=1, source_target_pairs={{1,0},{2,1},{3,2},{4,3},{5,4},{6,5},{7,6},{0,7},{9,8},{10,9},{11,1... | collective-permute-start | bytes 460808 | tf_op jit(solution)/shard_map/ppermute | solution.py:23
  154.4 84.8 %copy-start.6 = (f32[1280]{0:T(1024)S(1)}, f32[1280]{0:T(1024)}, u32[]{:S(2)}) copy-start(f32[1280]{0:T(1024)} %param.18) | copy-start | bytes 15364
Sparse Core Ops, SparseCore 0:
  30.9 117.6 all-gather.4
  150.8 42.7 all-gather.8
  195.8 43.3 all-gather.6
where the time goes:
time: 251 us; the launch traced here: 250 us
  waiting for transfers between devices  84.7 us (34%)
  loops' own time  58.2 us (23%)
  local copies, waits for them, and re-layouts  35.2 us (14%)
  blocking collectives  33.6 us (13%)
  matrix products  16 us (6%)
  between operations  13.3 us (5%)
  starting transfers between devices  8.4 us (3%)
    another operation x1, loops' own time, contract_cycles(): return lax.map(cycle_output, jnp.arange(cycle_count, dtype=jnp.int32))  58.2 us
    all_gather x1, waiting for transfers between devices, shards(): lax.all_gather(partial_weights[1], 'lon', axis=1, tiled=True)  45.6 us
    all_gather x1, waiting for transfers between devices, shards(): lax.all_gather(partial_weights[2], 'lon', axis=1, tiled=True)  33.4 us
    all_gather x1, blocking collectives, shards(): lax.all_gather(mix_weight, 'lat', axis=1, tiled=True)  20.1 us
    another operation x198, local copies, waits for them, and re-layouts, cycle_output(): jnp.stack(pieces).reshape(R * BW, members * out_cells * channel_share)  16.2 us
    all_gather x1, blocking collectives, shards(): lax.all_gather(up_weight, 'lat', axis=0, tiled=True)  7.74 us
    dot_general x6, matrix products, cycle_output(): jnp.dot(cycle_filter, stacked, preferred_element_type=jnp.float32)  5.86 us
    all_gather x1, blocking collectives, shards(): lax.all_gather(down_weight, 'lat', axis=0, tiled=True)  5.8 us
  transfers between devices with their start and end apart: 7, of which 5 were waited for; matrix products, arithmetic and copies ran while one was open for 17% of the time, Pallas kernels for 0%

commit v1 on v0

--- a/solution.py
+++ b/solution.py
@@ -1,15 +1,460 @@
 import jax
 import jax.numpy as jnp
 from jax import lax
+from jax.experimental import pallas as pl
+from jax.experimental.pallas import tpu as pltpu
 from jax.sharding import PartitionSpec as P
 
+HREACH = 2
 KB = 9
 R = 4
 BW = 8
-HREACH = 2
-
-
 EPSILON = 1e-05
+BF = jnp.bfloat16
+F32 = jnp.float32
+AXES = ("lat", "lon")
+VMEM_BYTES = 56 * 1024 * 1024
+
+
+def shape_of(shape, dtype):
+    return jax.ShapeDtypeStruct(tuple(shape), dtype)
+
+
+def whole(count):
+    return [pl.BlockSpec(memory_space=pltpu.VMEM) for _ in range(count)]
+
+
+def scalars(count):
+    return [pl.BlockSpec(memory_space=pltpu.SMEM) for _ in range(count)]
+
+
+def params():
+    return pltpu.CompilerParams(vmem_limit_bytes=VMEM_BYTES)
+
+
+class Plan:
+    def __init__(self, lats, lons, latent, filters, mix_weight, up_weight, down_weight):
+        self.lats, self.lons = lats, lons
+        self.rows2 = lats // 2
+        self.zs = lons // 2
+        self.cycles, self.members, self.cells, self.width = latent.shape
+        self.basis, _, self.slots, self.band = filters.shape
+        self.depth, self.out = mix_weight.shape[1], mix_weight.shape[2]
+        self.lift = up_weight.shape[1]
+        self.down_rows = down_weight.shape[0]
+        self.lanes = self.members * self.depth
+        self.meta = self.basis * self.slots * self.band + 2 * self.slots
+        self.tail = 16
+        self.piece = self.cycles * self.cells + self.tail
+        self.kpad = -(-self.depth // 128) * 128
+        self.group = 3
+        self.parts = self.basis // 3
+        self.mix_rows = self.parts * self.depth
+        self.rest = self.down_rows - self.depth
+        self.rest_rows = -(-self.rest // (3 * 16)) * 16
+        self.mlp_rows = self.depth + self.rest_rows
+        self.pack_rows = self.mix_rows + self.mlp_rows
+        self.pack_lanes = self.group * self.out
+        self.total = self.cycles * lats
+        self.window = 4 * self.cells
+
+    def fits(self):
+        return (
+            self.lats % 2 == 0
+            and self.lons % 2 == 0
+            and self.cells == 8
+            and self.members == 2
+            and self.slots * self.window == 128
+            and self.band // 2 + 2 <= self.cells
+            and self.basis % 3 == 0
+            and self.lift == 2 * self.out
+            and self.depth % 16 == 0
+            and self.meta <= self.lanes
+            and self.cycles <= self.tail
+            and (self.cycles * self.cells) % 16 == 0
+            and self.rest > 0
+        )
+
+
+def prep_kernel(plan, spot, latent, gain, meta, mix, up, down, msgs, pack, stage):
+    p = plan
+    a = spot[0]
+    flat = latent[...].astype(F32).reshape(p.cycles * p.members * p.cells, p.width)
+    mean = jnp.mean(flat, axis=-1, keepdims=True)
+    centered = flat - mean
+    variance = jnp.mean(centered * centered, axis=-1, keepdims=True)
+    normal = centered * lax.rsqrt(variance + EPSILON) * gain[...]
+    normal = normal.reshape(p.cycles, p.members, p.cells, p.width)
+    body = p.cycles * p.cells
+    for e in range(p.members):
+        part = normal[:, e].reshape(body, p.width).astype(BF)
+        for q in range(p.lats):
+            slot = lax.rem(q - a + p.lats, p.lats)
+            stage[slot, 0:body, e * p.depth : (e + 1) * p.depth] = part[
+                :, q * p.depth : (q + 1) * p.depth
+            ]
+    for s in range(p.lats):
+        msgs[s][0:body, :] = stage[s, 0:body, :]
+        msgs[s][body:, :] = meta[...]
+    for k in range(p.basis):
+        u, v = k // p.group, k % p.group
+        pack[u * p.depth : (u + 1) * p.depth, v * p.out : (v + 1) * p.out] = mix[k]
+    base = p.mix_rows
+    pack[base : base + p.depth, 0 : p.lift] = up[...]
+    pack[base : base + p.depth, p.lift : p.lift + p.out] = down[0 : p.depth, :]
+    base += p.depth
+    for g in range(3):
+        lo = p.depth + g * p.rest_rows
+        hi = min(lo + p.rest_rows, p.down_rows)
+        if hi > lo:
+            pack[base : base + hi - lo, g * p.out : (g + 1) * p.out] = down[lo:hi, :]
+        if hi - lo < p.rest_rows:
+            gap = p.rest_rows - max(hi - lo, 0)
+            pack[base + p.rest_rows - gap : base + p.rest_rows, g * p.out : (g + 1) * p.out] = (
+                jnp.zeros((gap, p.out), BF)
+            )
+
+
+def prepare(plan, spot, latent, gain, meta, mix, up, down):
+    p = plan
+    outs = pl.pallas_call(
+        lambda *refs: prep_kernel(
+            p, *refs[:7], refs[7 : 7 + p.lats], refs[7 + p.lats], refs[8 + p.lats]
+        ),
+        out_shape=[shape_of((p.piece, p.lanes), BF)] * p.lats
+        + [shape_of((p.pack_rows, p.pack_lanes), BF)],
+        in_specs=scalars(1) + whole(6),
+        out_specs=whole(p.lats + 1),
+        scratch_shapes=[pltpu.VMEM((p.lats, p.cycles * p.cells, p.lanes), BF)],
+        compiler_params=params(),
+        name="normalize_pack",
+    )(spot, latent, gain, meta, mix, up, down)
+    return outs[: p.lats], outs[p.lats]
+
+
+def conv_kernel(plan, spot, rows, taps, own, pair, near, far, packs, keep, send, scratch):
+    p = plan
+    grid, contracted, slots, mixing = scratch
+    a, z, x = spot[0], spot[1], spot[2]
+    even = x == 0
+    body = p.cycles * p.cells
+    grid[...] = jnp.zeros_like(grid)
+    for s in range(p.lats):
+        band = lax.rem(a - s + p.lats, p.lats)
+        lo = s * p.piece
+
+        def read(ref):
+            return ref[lo : lo + body, :].astype(F32)
+
+        mine, other, first, second = read(own), read(pair), read(near), read(far)
+        blocks = (
+            jnp.where(even, first, second),
+            jnp.where(even, mine, other),
+            jnp.where(even, other, mine),
+            jnp.where(even, second, first),
+        )
+        joined = jnp.concatenate(
+            [block.reshape(p.cycles, p.cells, p.lanes) for block in blocks], axis=1
+        ).astype(BF)
+        where = HREACH + band * p.cycles
+        for e in range(p.members):
+            grid[pl.ds(where, p.cycles), :, e * p.kpad : e * p.kpad + p.depth] = joined[
+                :, :, e * p.depth : (e + 1) * p.depth
+            ]
+
+    mixing[...] = jnp.zeros_like(mixing)
+    for s in range(p.zs):
+        slots[lax.rem(z - s + p.zs, p.zs)] = packs[s][0 : p.mix_rows, :]
+    for b in range(p.zs):
+        for k in range(p.basis):
+            u, v = k // p.group, k % p.group
+            mixing[k * p.kpad : k * p.kpad + p.depth, b * p.out : (b + 1) * p.out] = slots[
+                b, u * p.depth : (u + 1) * p.depth, v * p.out : (v + 1) * p.out
+            ]
+
+    double = 2 * p.cells
+
+    def contract(i, carry):
+        source = jnp.concatenate(
+            [grid[i + HREACH + rows[i * p.slots + r]] for r in range(p.slots)], axis=0
+        )
+        tap = taps[i]
+        lhs = jnp.concatenate(
+            [
+                pltpu.roll(
+                    jnp.broadcast_to(tap[k : k + 1, :], (double, 128)),
+                    0,
+                    1,
+                    stride=1,
+                    stride_axis=0,
+                )
+                for k in range(p.basis)
+            ],
+            axis=0,
+        ).astype(BF)
+        result = jnp.dot(lhs, source, preferred_element_type=F32).astype(BF)
+        at = i * (p.members * double)
+        for e in range(p.members):
+            for k in range(p.basis):
+                contracted[
+                    pl.ds(pl.multiple_of(at + e * double, double), double),
+                    k * p.kpad : (k + 1) * p.kpad,
+                ] = result[k * double : (k + 1) * double, e * p.kpad : (e + 1) * p.kpad]
+        return carry
+
+    lax.fori_loop(0, p.total, contract, 0, unroll=4)
+
+    count = p.cycles * p.members * double
+    core = lax.rem(a, 2)
+    for t in range(p.rows2):
+        y = lax.rem(a // 2 + t, p.rows2)
+        for mate in range(2):
+            band = 2 * y + (core if mate == 0 else 1 - core)
+            at = pl.multiple_of(band * count, count)
+            total = jnp.dot(
+                contracted[pl.ds(at, count), :], mixing[...], preferred_element_type=F32
+            ).reshape(p.cycles * p.members, 2, p.cells, p.zs * p.out)
+            half = count // 2
+            left = total[:, 0].reshape(half, p.zs * p.out)
+            right = total[:, 1].reshape(half, p.zs * p.out)
+            for w in range(2):
+                value = jnp.where((x ^ w) == 0, left, right)
+                if mate == 0:
+                    keep[2 * t + w] = value
+                else:
+                    send[2 * t + w] = value.astype(BF)
+
+
+def convolve(plan, spot, rows, taps, own, pair, near, far, packs):
+    p = plan
+    half = p.cycles * p.members * p.cells
+    out = p.zs * p.out
+
+    def body(*refs):
+        fixed, rest = refs[:7], refs[7:]
+        conv_kernel(p, *fixed, rest[: p.zs], rest[p.zs], rest[p.zs + 1], rest[p.zs + 2 :])
+
+    return pl.pallas_call(
+        body,
+        out_shape=[
+            shape_of((2 * p.rows2, half, out), F32),
+            shape_of((2 * p.rows2, half, out), BF),
+        ],
+        in_specs=scalars(2) + whole(5 + p.zs),
+        out_specs=whole(2),
+        scratch_shapes=[
+            pltpu.VMEM((p.total + 2 * HREACH, p.window, p.members * p.kpad), BF),
+            pltpu.VMEM((p.total * p.members * 2 * p.cells, p.basis * p.kpad), BF),
+            pltpu.VMEM((p.zs, p.mix_rows, p.pack_lanes), BF),
+            pltpu.VMEM((p.basis * p.kpad, out), BF),
+        ],
+        compiler_params=params(),
+        name="contract_mix",
+    )(spot, rows, taps, own, pair, near, far, *packs)
+
+
+def add_kernel(keep, arrived, own, *msgs):
+    for i in range(keep.shape[0]):
+        value = keep[i] + arrived[i].astype(F32)
+        if i == 0:
+            own[...] = value
+        else:
+            msgs[i - 1][...] = value.astype(BF)
+
+
+def add_cores(keep, arrived):
+    count, half, out = keep.shape
+    outs = pl.pallas_call(
+        add_kernel,
+        out_shape=[shape_of((half, out), F32)] + [shape_of((half, out), BF)] * (count - 1),
+        in_specs=whole(2),
+        out_specs=whole(count),
+        compiler_params=params(),
+        name="add_cores",
+    )(keep, arrived)
+    return outs[0], outs[1:]
+
+
+def unpack_kernel(plan, spot, stacks, up, down, slots):
+    p = plan
+    a, z, x = spot[0], spot[1], spot[2]
+    core = lax.rem(a, 2)
+    for mate in range(2):
+        for t in range(p.rows2):
+            y = lax.rem(a // 2 - t + p.rows2, p.rows2)
+            lat = 2 * y + (core if mate == 0 else 1 - core)
+            for w in range(2):
+                for s in range(p.zs):
+                    lon = 2 * lax.rem(z - s + p.zs, p.zs) + (x ^ w)
+                    index = (t * 2 + w) * p.zs + s
+                    slots[lat * p.lons + lon] = stacks[mate][
+                        index * p.mlp_rows : (index + 1) * p.mlp_rows, :
+                    ]
+    for a in range(p.lats):
+        for b in range(p.lons):
+            i = a * p.lons + b
+            up[a * p.depth : (a + 1) * p.depth, b * p.lift : (b + 1) * p.lift] = slots[
+                i, 0 : p.depth, 0 : p.lift
+            ]
+            base = a * p.down_rows
+            cols = slice(b * p.out, (b + 1) * p.out)
+            down[base : base + p.depth, cols] = slots[
+                i, 0 : p.depth, p.lift : p.lift + p.out
+            ]
+            for g in range(3):
+                lo = p.depth + g * p.rest_rows
+                hi = min(lo + p.rest_rows, p.down_rows)
+                if hi > lo:
+                    down[base + lo : base + hi, cols] = slots[
+                        i, p.depth : p.depth + hi - lo, g * p.out : (g + 1) * p.out
+                    ]
+
+
+def unpack(plan, spot, mine, sibling):
+    p = plan
+    return pl.pallas_call(
+        lambda spot, one, two, up, down, slots: unpack_kernel(
+            p, spot, (one, two), up, down, slots
+        ),
+        out_shape=[
+            shape_of((p.lats * p.depth, p.lons * p.lift), BF),
+            shape_of((p.lats * p.down_rows, p.lons * p.out), BF),
+        ],
+        in_specs=scalars(1) + whole(2),
+        out_specs=whole(2),
+        scratch_shapes=[pltpu.VMEM((p.lats * p.lons, p.mlp_rows, p.pack_lanes), BF)],
+        compiler_params=params(),
+        name="mlp_weights",
+    )(spot, mine, sibling)
+
+
+def mlp_kernel(plan, spot, latent, bias, up, down, own, *rest):
+    p = plan
+    arrived, (out, conv) = rest[:-2], rest[-2:]
+    even = spot[2] == 0
+    mine = own[...]
+    other = None
+    for i, ref in enumerate(arrived):
+        value = ref[...].astype(F32)
+        if (i + 1) % 2 == 0:
+            mine = mine + value
+        else:
+            other = value if other is None else other + value
+    first = jnp.where(even, mine, other)
+    second = jnp.where(even, other, mine)
+    for b in range(p.zs):
+        cols = slice(b * p.out, (b + 1) * p.out)
+        conv[:, 2 * b * p.out : (2 * b + 1) * p.out] = first[:, cols]
+        conv[:, (2 * b + 1) * p.out : (2 * b + 2) * p.out] = second[:, cols]
+    half = p.cycles * p.members * p.cells
+    hidden = (latent[...].astype(F32).reshape(half, p.width) + conv[...]).astype(BF)
+    lifted = jnp.dot(hidden, up[...], preferred_element_type=F32) + bias[...]
+    activated = (lifted * (1.0 + lax.erf(lifted * (0.5**0.5))) * 0.5).astype(BF)
+    result = hidden.astype(F32) + jnp.dot(activated, down[...], preferred_element_type=F32)
+    out[...] = result.astype(BF).reshape(out.shape)
+
+
+def mlp(plan, spot, latent, bias, up, down, own, arrived):
+    p = plan
+    half = p.cycles * p.members * p.cells
+    return pl.pallas_call(
+        lambda *refs: mlp_kernel(p, *refs),
+        out_shape=shape_of(latent.shape, BF),
+        in_specs=scalars(1) + whole(5 + len(arrived)),
+        out_specs=pl.BlockSpec(memory_space=pltpu.VMEM),
+        scratch_shapes=[pltpu.VMEM((half, p.width), F32)],
+        compiler_params=params(),
+        name="sum_mlp",
+    )(spot, latent, bias, up, down, own, *arrived)
+
+
+def mover(plan):
+    p = plan
+
+    def move(value, target):
+        pairs = []
+        for a in range(p.lats):
+            for b in range(p.lons):
+                c, d = target(a, b)
+                pairs.append((a * p.lons + b, (c % p.lats) * p.lons + d % p.lons))
+        return lax.ppermute(value, AXES, pairs)
+
+    return move
+
+
+def shards_fast(
+    plan,
+    latent,
+    norm_gain,
+    filters,
+    row_offsets,
+    col_offsets,
+    mix_weight,
+    up_weight,
+    up_bias,
+    down_weight,
+):
+    p = plan
+    move = mover(p)
+    a, b = lax.axis_index("lat"), lax.axis_index("lon")
+    spot = jnp.stack([a, b // 2, b % 2]).astype(jnp.int32)
+    meta = jnp.concatenate(
+        [
+            filters.transpose(1, 0, 2, 3).reshape(p.cycles, -1),
+            row_offsets.astype(BF),
+            col_offsets.astype(BF),
+        ],
+        axis=1,
+    )
+    meta = jnp.pad(meta, ((0, p.tail - p.cycles), (0, p.lanes - p.meta)))
+    msgs, pack = prepare(
+        p, spot, latent, norm_gain.reshape(1, -1), meta, mix_weight, up_weight, down_weight
+    )
+    pieces = [msgs[0]]
+    for s in range(1, p.lats):
+        pieces.append(move(msgs[s], lambda i, j, s=s: (i + s, j)))
+    packs = [pack]
+    for s in range(1, p.zs):
+        packs.append(move(pack, lambda i, j, s=s: (i, j + 2 * s)))
+    own = jnp.concatenate(pieces, axis=0)
+    pair = move(own, lambda i, j: (i, j ^ 1))
+    near = move(own, lambda i, j: (i, j + 1 if j % 2 else j - 1))
+    far = move(own, lambda i, j: (i, j + 2 if j % 2 else j - 2))
+
+    infos = own.reshape(p.lats, p.piece, p.lanes)[:, p.piece - p.tail :][:, : p.cycles, : p.meta]
+    order = (a - jnp.arange(p.lats, dtype=jnp.int32)) % p.lats
+    infos = infos[order].reshape(p.total, p.meta)
+    split = p.basis * p.slots * p.band
+    offsets = infos[:, split:].astype(jnp.int32)
+    rows = offsets[:, : p.slots].reshape(-1)
+    starts = offsets[:, p.slots :] + p.cells
+    values = infos[:, :split].astype(F32).reshape(p.total, p.basis, p.slots, 1, p.band)
+    place = (
+        jnp.arange(p.window, dtype=jnp.int32)[:, None]
+        - jnp.arange(p.band, dtype=jnp.int32)[None, :]
+    )
+    hits = place[None, None] == starts[:, :, None, None]
+    taps = jnp.sum(jnp.where(hits[:, None], values, 0.0), axis=-1)
+    taps = taps.reshape(p.total, p.basis, p.slots * p.window)
+    taps = jnp.pad(taps, ((0, 0), (0, 16 - p.basis), (0, 0)))
+
+    share = jnp.concatenate([piece[p.mix_rows :] for piece in packs], axis=0)
+    share = jnp.concatenate([share, move(share, lambda i, j: (i, j ^ 1))], axis=0)
+    bands = [share]
+    for t in range(1, p.rows2):
+        bands.append(move(share, lambda i, j, t=t: (i + 2 * t, j)))
+    share = jnp.concatenate(bands, axis=0)
+    sibling = move(share, lambda i, j: (i ^ 1, j))
+    up, down = unpack(p, spot, share, sibling)
+
+    keep, send = convolve(p, spot, rows, taps, own, pair, near, far, packs)
+    arrived = move(send, lambda i, j: (i ^ 1, j))
+    mine, outgoing = add_cores(keep, arrived)
+    incoming = []
+    for index, value in enumerate(outgoing):
+        t, w = (index + 1) // 2, (index + 1) % 2
+        incoming.append(move(value, lambda i, j, t=t, w=w: (i + 2 * t, j ^ w)))
+    return mlp(p, spot, latent, up_bias.reshape(1, -1), up, down, mine, incoming)
 
 
 def padded(shard, sides, width, wrap):
@@ -60,7 +505,7 @@
     return lax.map(cycle_output, jnp.arange(cycle_count, dtype=jnp.int32))
 
 
-def shards(
+def shards_plain(
     latent,
     norm_gain,
     filters,
@@ -105,6 +550,15 @@
 
 
 def solution(mesh):
+    lats, lons = mesh.shape["lat"], mesh.shape["lon"]
+
+    def shards(*args):
+        latent, _, filters, _, _, mix_weight, up_weight, _, down_weight = args
+        plan = Plan(lats, lons, latent, filters, mix_weight, up_weight, down_weight)
+        if plan.fits():
+            return shards_fast(plan, *args)
+        return shards_plain(*args)
+
     in_specs = (
         P("lat", None, "lon", None),
         P(),

time: 251 us -> 129 us (0.51)
  loops' own time: 58.2 us -> 0 us
  blocking collectives: 33.6 us -> 0 us
  waiting for transfers between devices: 84.7 us -> 51.3 us
  Pallas kernels: 0 us -> 21.1 us
  starting transfers between devices: 8.4 us -> 25.2 us
  matrix products: 16 us -> 0 us
  between operations: 13.3 us -> 0.2 us
  local copies, waits for them, and re-layouts: 35.2 us -> 23.9 us
  other arithmetic: 0.69 us -> 6.36 us
    all_gather x3 -> x0, waiting for transfers between devices: 79 us -> none  [the longest x1 45.6 us: shards(): lax.all_gather(partial_weights[1], 'lon', axis=1, tiled=True)]
    another operation x1 -> x0, loops' own time: 58.2 us -> none  [contract_cycles(): return lax.map(cycle_output, jnp.arange(cycle_count, dtype=jnp.int32))]
    ppermute x4 -> x16, waiting for transfers between devices: 5.66 us -> 51.3 us  [move(): return lax.ppermute(value, AXES, pairs)]
    all_gather x3 -> x0, blocking collectives: 33.6 us -> none  [the longest x1 20.1 us: shards(): lax.all_gather(mix_weight, 'lat', axis=1, tiled=True)]
    pallas_call x0 -> x5, Pallas kernels: none -> 21.1 us  [the longest x1 7.67 us: convolve(): pl.pallas_call(body, out_shape=[shape_of((2 * p.rows2, half, out), F32),...]
    ppermute x4 -> x16, starting transfers between devices: 8.32 us -> 25.2 us  [move(): return lax.ppermute(value, AXES, pairs)]
    another operation x198 -> x0, local copies, waits for them, and re-layouts: 16.2 us -> none  [cycle_output(): jnp.stack(pieces).reshape(R * BW, members * out_cells * channel_share)]
    dot_general x8 -> x0, matrix products: 16 us -> none  [the longest x6 5.86 us: cycle_output(): jnp.dot(cycle_filter, stacked, preferred_element_type=jnp.float32)]
  transfers between devices with their start and end apart: 7 -> 16, of which waited for: 5 -> 7; matrix products, arithmetic and copies ran while one was open for 17% -> 15% of each run, Pallas kernels for 0% -> 12%
where the time goes in v1:
time: 129 us; the launch traced here: 128 us
  waiting for transfers between devices  51.3 us (40%)
  starting transfers between devices  25.2 us (20%)
  local copies, waits for them, and re-layouts  23.9 us (19%)
  Pallas kernels  21.1 us (16%)
  other arithmetic  6.36 us (5%)
    ppermute x16, waiting for transfers between devices, move(): return lax.ppermute(value, AXES, pairs)  51.3 us
    ppermute x16, starting transfers between devices, move(): return lax.ppermute(value, AXES, pairs)  25.2 us
    pallas_call x1, Pallas kernels, convolve(): pl.pallas_call(body, out_shape=[shape_of((2 * p.rows2, half, out), F32),...  7.67 us
    pallas_call x1, Pallas kernels, unpack(): pl.pallas_call(lambda spot, one, two, up, down, slots: unpack_kernel(p, s...  5.75 us
    unnamed x34, local copies, waits for them, and re-layouts  5.49 us
    ppermute x2, local copies, waits for them, and re-layouts, move(): return lax.ppermute(value, AXES, pairs)  3.71 us
    pallas_call x1, Pallas kernels, mlp(): pl.pallas_call(lambda *refs: mlp_kernel(p, *refs), out_shape=shape_of(lat...  3.54 us
    concatenate x2, local copies, waits for them, and re-layouts, shards_fast(): share = jnp.concatenate(bands, axis=0)  2.67 us
  transfers between devices with their start and end apart: 16, of which 7 were waited for; matrix products, arithmetic and copies ran while one was open for 15% of the time, Pallas kernels for 12%

profile of v1, /device:TPU:0, one launch (start us, length us, event | category | flops | bytes accessed | tf_op | source)
XLA Modules:
  0.0 128.0 jit_solution(4143454277915746176)
XLA Ops:
  0.0 1.6 %copy.47.refs_6_ = bf16[320,80]{1,0:T(8,128)(2,1)} copy(bf16[320,80]{0,1:T(8,128)(2,1)} %param.17) | data formatting | bytes 102400 | tf_op args[8]
  1.6 1.0 copy.44
  4.3 1.3 reshape.87.refs_2_
  6.9 2.3 %normalize_pack.1 = (bf16[64,320]{1,0:T(8,128)(2,1)}, bf16[64,320]{1,0:T(8,128)(2,1)}, bf16[64,320]{1,0:T(8,128)(2,1)}, bf16[64,320]{1,0:T(8,128)(2,1)}, bf16[704,240]{1,0:T(8,128)(2,1)}) custom-call(s32[3]{0:T(128)} %pad_add_fusion.refs_0_.spot, bf16[6,2,8,640]{3,2,1,0:T(8,128)(2,1)} %refs_1_.3, f32[1,640]{1,0:T(1,128)} %reshape.87.refs_2_, ...), custom_call_target="tpu_custom_call" | custom-call | tf_op jit(solution)/shard_map/normalize_pack/pallas_call | solution.py:120
  9.1 3.0 %collective-permute-start = (bf16[704,240]{1,0:T(8,128)(2,1)}, bf16[704,240]{1,0:T(8,128)(2,1)S(1)}, u32[]{:S(2)}, u32[]{:S(2)}) collective-permute-start(bf16[704,240]{1,0:T(8,128)(2,1)} %get-tuple-element.18.refs_7_), channel_id=1, source_target_pairs={{0,2},{1,3},{2,4},{3,5},{4,6},{5,7},{6,0},{7,1},{8,10},{9,11},{10,... | collective-permute-start | bytes 1013768 | tf_op jit(solution)/shard_map/ppermute | solution.py:380
  12.2 2.6 %collective-permute-start.1 = (bf16[704,240]{1,0:T(8,128)(2,1)}, bf16[704,240]{1,0:T(8,128)(2,1)S(1)}, u32[]{:S(2)}, u32[]{:S(2)}) collective-permute-start(bf16[704,240]{1,0:T(8,128)(2,1)} %get-tuple-element.18.refs_7_), channel_id=1, source_target_pairs={{0,4},{1,5},{2,6},{3,7},{4,0},{5,1},{6,2},{7,3},{8,12},{9,13},{10,... | collective-permute-start | bytes 1013768 | tf_op jit(solution)/shard_map/ppermute | solution.py:380
  14.8 1.3 %collective-permute-start.2 = (bf16[704,240]{1,0:T(8,128)(2,1)}, bf16[704,240]{1,0:T(8,128)(2,1)S(1)}, u32[]{:S(2)}, u32[]{:S(2)}) collective-permute-start(bf16[704,240]{1,0:T(8,128)(2,1)} %get-tuple-element.18.refs_7_), channel_id=1, source_target_pairs={{0,6},{1,7},{2,0},{3,1},{4,2},{5,3},{6,4},{7,5},{8,14},{9,15},{10,... | collective-permute-start | bytes 1013768 | tf_op jit(solution)/shard_map/ppermute | solution.py:380
  17.1 6.7 %collective-permute-done.refs_8_ = bf16[704,240]{1,0:T(8,128)(2,1)S(1)} collective-permute-done((bf16[704,240]{1,0:T(8,128)(2,1)}, bf16[704,240]{1,0:T(8,128)(2,1)S(1)}, u32[]{:S(2)}, u32[]{:S(2)}) %collective-permute-start) | collective-permute-done | bytes 337952 | tf_op jit(solution)/shard_map/ppermute | solution.py:380
  23.8 14.6 %collective-permute-done.1.refs_9_ = bf16[704,240]{1,0:T(8,128)(2,1)S(1)} collective-permute-done((bf16[704,240]{1,0:T(8,128)(2,1)}, bf16[704,240]{1,0:T(8,128)(2,1)S(1)}, u32[]{:S(2)}, u32[]{:S(2)}) %collective-permute-start.1) | collective-permute-done | bytes 337952 | tf_op jit(solution)/shard_map/ppermute | solution.py:380
  39.4 1.6 %collective-permute-start.3 = (bf16[896,240]{1,0:T(8,128)(2,1)S(1)}, bf16[896,240]{1,0:T(8,128)(2,1)S(1)}, u32[]{:S(2)}, u32[]{:S(2)}) collective-permute-start(bf16[896,240]{1,0:T(8,128)(2,1)S(1)} %pad_maximum_fusion), channel_id=1, source_target_pairs={{0,1},{1,0},{2,3},{3,2},{4,5},{5,4},{6,7},{7,6},{8,9},{9,8},{10,11... | collective-permute-start | bytes 1290248 | tf_op jit(solution)/shard_map/ppermute | solution.py:380
  40.9 10.9 %collective-permute-done.3 = bf16[896,240]{1,0:T(8,128)(2,1)S(1)} collective-permute-done((bf16[896,240]{1,0:T(8,128)(2,1)S(1)}, bf16[896,240]{1,0:T(8,128)(2,1)S(1)}, u32[]{:S(2)}, u32[]{:S(2)}) %collective-permute-start.3) | collective-permute-done | bytes 430112 | tf_op jit(solution)/shard_map/ppermute | solution.py:380
  51.9 1.3 copy.48
  53.1 1.5 %collective-permute-start.4 = (bf16[1792,240]{0,1:T(8,128)(2,1)}, bf16[1792,240]{0,1:T(8,128)(2,1)}, u32[]{:S(2)}, u32[]{:S(2)}) collective-permute-start(bf16[1792,240]{0,1:T(8,128)(2,1)} %copy.48), channel_id=1, source_target_pairs={{0,16},{1,17},{2,18},{3,19},{4,20},{5,21},{6,22},{7,23},{8,24},{9,... | collective-permute-start | bytes 2580488 | tf_op jit(solution)/shard_map/ppermute | solution.py:380
  55.2 1.4 %collective-permute-start.8 = (bf16[64,320]{1,0:T(8,128)(2,1)}, bf16[64,320]{1,0:T(8,128)(2,1)}, u32[]{:S(2)}, u32[]{:S(2)}) collective-permute-start(bf16[64,320]{1,0:T(8,128)(2,1)} %get-tuple-element.24), channel_id=1, source_target_pairs={{0,24},{1,25},{2,26},{3,27},{4,28},{5,29},{6,30},{7,31},{8,0},{9,1... | collective-permute-start | bytes 122888 | tf_op jit(solution)/shard_map/ppermute | solution.py:380
  57.8 14.7 %collective-permute-done.6 = bf16[64,320]{1,0:T(8,128)(2,1)S(1)} collective-permute-done((bf16[64,320]{1,0:T(8,128)(2,1)S(1)}, bf16[64,320]{1,0:T(8,128)(2,1)S(1)}, u32[]{:S(2)}, u32[]{:S(2)}) %collective-permute-start.6) | collective-permute-done | bytes 40992 | tf_op jit(solution)/shard_map/ppermute | solution.py:380
  72.5 2.5 %collective-permute-done.7 = bf16[64,320]{1,0:T(8,128)(2,1)S(1)} collective-permute-done((bf16[64,320]{1,0:T(8,128)(2,1)S(1)}, bf16[64,320]{1,0:T(8,128)(2,1)S(1)}, u32[]{:S(2)}, u32[]{:S(2)}) %collective-permute-start.7) | collective-permute-done | bytes 40992 | tf_op jit(solution)/shard_map/ppermute | solution.py:380
  75.7 1.4 %copy.49 = bf16[1792,240]{1,0:T(8,128)(2,1)S(1)} copy(bf16[1792,240]{0,1:T(8,128)(2,1)} %collective-permute-done.4) | data formatting | bytes 1720320 | tf_op jit(solution)/shard_map/ppermute | solution.py:380
  77.2 2.6 %copy.50 = bf16[3584,240]{0,1:T(8,128)(2,1)} copy(bf16[3584,240]{1,0:T(8,128)(2,1)S(1)} %constant_dynamic-update-slice_fusion.5.one) | data formatting | bytes 3440640 | tf_op jit(solution)/shard_map/concatenate | solution.py:446
  79.9 1.4 %constant_dynamic-update-slice_fusion.11.refs_3_ = bf16[256,320]{1,0:T(8,128)(2,1)} fusion(bf16[256,320]{1,0:T(8,128)(2,1)} %copy-done.4, bf16[64,320]{1,0:T(8,128)(2,1)} %collective-permute-done.8), kind=kLoop, calls=%fused_computation.15 | loop fusion | bytes 98304 | tf_op jit(solution)/shard_map/concatenate | solution.py:419
  81.3 8.2 %collective-permute-start.10 = (bf16[256,320]{1,0:T(8,128)(2,1)}, bf16[256,320]{1,0:T(8,128)(2,1)}, u32[]{:S(2)}, u32[]{:S(2)}) collective-permute-start(bf16[256,320]{1,0:T(8,128)(2,1)} %constant_dynamic-update-slice_fusion.11.refs_3_), channel_id=1, source_target_pairs={{0,7},{1,2},{2,1},{3,4},{4,3},{5,6},{6,5},{7,0},{8,15},{9,10},{10,... | collective-permute-start | bytes 491528 | tf_op jit(solution)/shard_map/ppermute | solution.py:380
  89.4 1.5 %collective-permute-start.11 = (bf16[256,320]{1,0:T(8,128)(2,1)}, bf16[256,320]{1,0:T(8,128)(2,1)}, u32[]{:S(2)}, u32[]{:S(2)}) collective-permute-start(bf16[256,320]{1,0:T(8,128)(2,1)} %constant_dynamic-update-slice_fusion.11.refs_3_), channel_id=1, source_target_pairs={{0,6},{1,3},{2,0},{3,5},{4,2},{5,7},{6,4},{7,1},{8,14},{9,11},{10,... | collective-permute-start | bytes 491528 | tf_op jit(solution)/shard_map/ppermute | solution.py:380
  91.0 1.4 %slice.43 = bf16[4,6,296]{2,1,0:T(8,128)(2,1)} slice(bf16[4,64,320]{2,1,0:T(8,128)(2,1)} %bitcast.9), slice={[0:4], [48:54], [0:296]} | slice | bytes 28416 | tf_op jit(solution)/shard_map/slice | solution.py:424
  92.4 2.0 %gather_fusion = bf16[4,6,296]{2,1,0:T(8,128)(2,1)} fusion(bf16[4,6,296]{2,1,0:T(8,128)(2,1)} %slice.43, s32[1024]{0:T(1024)} %pad_clamp_fusion), kind=kCustom, calls=%fused_computation | custom fusion | bytes 28432 | tf_op jit(solution)/shard_map/gather | solution.py:426
  96.5 1.4 %select_reduce_fusion = f32[24,9,4,32]{3,2,1,0:T(4,128)S(1)} fusion(f32[24,9,4,8]{3,2,1,0:T(4,128)S(1)} %copy.53, pred[24,4,32,8]{2,3,1,0:T(8,128)(4,1)S(1)} %broadcast_compare_fusion), kind=kLoop, calls=%fused_computation.1 | loop fusion | flops 414720 | bytes 162816 | tf_op jit(solution)/shard_map/reduce_sum | solution.py:437
  99.7 7.7 %contract_mix.1 = (f32[4,96,320]{2,1,0:T(8,128)}, bf16[4,96,320]{2,1,0:T(8,128)(2,1)}) custom-call(s32[3]{0:T(128)} %pad_add_fusion.refs_0_.spot, s32[96]{0:T(128)} %reshape.91.refs_1_, f32[24,16,128]{2,1,0:T(8,128)} %pad.9.refs_2_, bf16[256,320]{1,0:T(8,128)(2,1)} %constant_dynamic-update-slice_fusion.11.refs_3_, ...), custom_call_target="tpu_custom_call" | custom-call | tf_op jit(solution)/shard_map/contract_mix/pallas_call | solution.py:237
  107.3 1.8 %collective-permute-done.12.arrived = bf16[4,96,320]{2,1,0:T(8,128)(2,1)S(1)} collective-permute-done((bf16[4,96,320]{2,1,0:T(8,128)(2,1)}, bf16[4,96,320]{2,1,0:T(8,128)(2,1)S(1)}, u32[]{:S(2)}, u32[]{:S(2)}) %collective-permute-start.12) | collective-permute-done | bytes 245792 | tf_op jit(solution)/shard_map/ppermute | solution.py:380
  109.8 1.9 %add_cores.1 = (f32[96,320]{1,0:T(8,128)}, bf16[96,320]{1,0:T(8,128)(2,1)}, bf16[96,320]{1,0:T(8,128)(2,1)}, bf16[96,320]{1,0:T(8,128)(2,1)}) custom-call(f32[4,96,320]{2,1,0:T(8,128)} %get-tuple-element.25.keep, bf16[4,96,320]{2,1,0:T(8,128)(2,1)} %copy-done.5), custom_call_target="tpu_custom_call" | custom-call | tf_op jit(solution)/shard_map/add_cores/pallas_call | solution.py:267
  111.7 1.9 %collective-permute-start.13 = (bf16[96,320]{1,0:T(8,128)(2,1)}, bf16[96,320]{1,0:T(8,128)(2,1)S(1)}, u32[]{:S(2)}, u32[]{:S(2)}) collective-permute-start(bf16[96,320]{1,0:T(8,128)(2,1)} %get-tuple-element.28), channel_id=1, source_target_pairs={{0,1},{1,0},{2,3},{3,2},{4,5},{5,4},{6,7},{7,6},{8,9},{9,8},{10,11... | collective-permute-start | bytes 184328 | tf_op jit(solution)/shard_map/ppermute | solution.py:380
  113.6 1.5 %collective-permute-start.14 = (bf16[96,320]{1,0:T(8,128)(2,1)}, bf16[96,320]{1,0:T(8,128)(2,1)S(1)}, u32[]{:S(2)}, u32[]{:S(2)}) collective-permute-start(bf16[96,320]{1,0:T(8,128)(2,1)} %get-tuple-element.29), channel_id=1, source_target_pairs={{0,16},{1,17},{2,18},{3,19},{4,20},{5,21},{6,22},{7,23},{8,24},{9,... | collective-permute-start | bytes 184328 | tf_op jit(solution)/shard_map/ppermute | solution.py:380
  115.8 2.3 %copy.51.two = bf16[3584,240]{1,0:T(8,128)(2,1)} copy(bf16[3584,240]{0,1:T(8,128)(2,1)S(1)} %collective-permute-done.5) | data formatting | bytes 3440640 | tf_op jit(solution)/shard_map/ppermute | solution.py:380
  118.1 5.8 %mlp_weights.1 = (bf16[640,1280]{1,0:T(8,128)(2,1)}, bf16[1280,640]{1,0:T(8,128)(2,1)}) custom-call(s32[3]{0:T(128)} %pad_add_fusion.refs_0_.spot, bf16[3584,240]{1,0:T(8,128)(2,1)} %copy-done, bf16[3584,240]{1,0:T(8,128)(2,1)} %copy.51.two), custom_call_target="tpu_custom_call" | custom-call | tf_op jit(solution)/shard_map/mlp_weights/pallas_call | solution.py:315
  124.5 3.5 %sum_mlp.1 = bf16[6,2,8,640]{3,2,1,0:T(8,128)(2,1)} custom-call(s32[3]{0:T(128)} %pad_add_fusion.refs_0_.spot, bf16[6,2,8,640]{3,2,1,0:T(8,128)(2,1)} %refs_1_.3, f32[1,1280]{1,0:T(1,128)} %reshape.86.refs_2_, bf16[640,1280]{1,0:T(8,128)(2,1)} %get-tuple-element.19.refs_3_, bf16[1280,640]{1,0:T(8,128)(2,1)} %get-tuple-element.20.refs_4_, ...), custom_call_target="tpu_custom_call" | custom-call | tf_op jit(solution)/shard_map/sum_mlp/pallas_call | solution.py:360
  (73 shorter events, 13.4 us)
Async XLA Ops:
  9.1 14.6 %collective-permute-start = (bf16[704,240]{1,0:T(8,128)(2,1)}, bf16[704,240]{1,0:T(8,128)(2,1)S(1)}, u32[]{:S(2)}, u32[]{:S(2)}) collective-permute-start(bf16[704,240]{1,0:T(8,128)(2,1)} %get-tuple-element.18.refs_7_), channel_id=1, source_target_pairs={{0,2},{1,3},{2,4},{3,5},{4,6},{5,7},{6,0},{7,1},{8,10},{9,11},{10,... | collective-permute-start | bytes 1013768 | tf_op jit(solution)/shard_map/ppermute | solution.py:380
  12.2 26.2 %collective-permute-start.1 = (bf16[704,240]{1,0:T(8,128)(2,1)}, bf16[704,240]{1,0:T(8,128)(2,1)S(1)}, u32[]{:S(2)}, u32[]{:S(2)}) collective-permute-start(bf16[704,240]{1,0:T(8,128)(2,1)} %get-tuple-element.18.refs_7_), channel_id=1, source_target_pairs={{0,4},{1,5},{2,6},{3,7},{4,0},{5,1},{6,2},{7,3},{8,12},{9,13},{10,... | collective-permute-start | bytes 1013768 | tf_op jit(solution)/shard_map/ppermute | solution.py:380
  14.8 23.7 %collective-permute-start.2 = (bf16[704,240]{1,0:T(8,128)(2,1)}, bf16[704,240]{1,0:T(8,128)(2,1)S(1)}, u32[]{:S(2)}, u32[]{:S(2)}) collective-permute-start(bf16[704,240]{1,0:T(8,128)(2,1)} %get-tuple-element.18.refs_7_), channel_id=1, source_target_pairs={{0,6},{1,7},{2,0},{3,1},{4,2},{5,3},{6,4},{7,5},{8,14},{9,15},{10,... | collective-permute-start | bytes 1013768 | tf_op jit(solution)/shard_map/ppermute | solution.py:380
  23.8 14.7 %copy-start.1 = (bf16[704,240]{1,0:T(8,128)(2,1)}, bf16[704,240]{1,0:T(8,128)(2,1)S(1)}, u32[]{:S(2)}) copy-start(bf16[704,240]{1,0:T(8,128)(2,1)S(1)} %collective-permute-done.refs_8_) | copy-start | bytes 1013764
  38.4 0.8 copy-start.2
  38.4 0.9 copy-start.3
  39.3 15.4 %copy-start.12 = (bf16[64,320]{1,0:T(8,128)(2,1)S(1)}, bf16[64,320]{1,0:T(8,128)(2,1)}, u32[]{:S(2)}) copy-start(bf16[64,320]{1,0:T(8,128)(2,1)} %get-tuple-element.22) | copy-start | bytes 122884
  39.3 15.4 %copy-start.11 = (bf16[64,320]{1,0:T(8,128)(2,1)S(1)}, bf16[64,320]{1,0:T(8,128)(2,1)}, u32[]{:S(2)}) copy-start(bf16[64,320]{1,0:T(8,128)(2,1)} %get-tuple-element.23) | copy-start | bytes 122884
  39.3 17.9 %copy-start.9 = (bf16[64,320]{1,0:T(8,128)(2,1)S(1)}, bf16[64,320]{1,0:T(8,128)(2,1)}, u32[]{:S(2)}) copy-start(bf16[64,320]{1,0:T(8,128)(2,1)} %get-tuple-element.21) | copy-start | bytes 122884
  39.4 12.4 %collective-permute-start.3 = (bf16[896,240]{1,0:T(8,128)(2,1)S(1)}, bf16[896,240]{1,0:T(8,128)(2,1)S(1)}, u32[]{:S(2)}, u32[]{:S(2)}) collective-permute-start(bf16[896,240]{1,0:T(8,128)(2,1)S(1)} %pad_maximum_fusion), channel_id=1, source_target_pairs={{0,1},{1,0},{2,3},{3,2},{4,5},{5,4},{6,7},{7,6},{8,9},{9,8},{10,11... | collective-permute-start | bytes 1290248 | tf_op jit(solution)/shard_map/ppermute | solution.py:380
  53.1 22.6 %collective-permute-start.4 = (bf16[1792,240]{0,1:T(8,128)(2,1)}, bf16[1792,240]{0,1:T(8,128)(2,1)}, u32[]{:S(2)}, u32[]{:S(2)}) collective-permute-start(bf16[1792,240]{0,1:T(8,128)(2,1)} %copy.48), channel_id=1, source_target_pairs={{0,16},{1,17},{2,18},{3,19},{4,20},{5,21},{6,22},{7,23},{8,24},{9,... | collective-permute-start | bytes 2580488 | tf_op jit(solution)/shard_map/ppermute | solution.py:380
  54.7 17.9 %collective-permute-start.6 = (bf16[64,320]{1,0:T(8,128)(2,1)S(1)}, bf16[64,320]{1,0:T(8,128)(2,1)S(1)}, u32[]{:S(2)}, u32[]{:S(2)}) collective-permute-start(bf16[64,320]{1,0:T(8,128)(2,1)S(1)} %copy-done.12), channel_id=1, source_target_pairs={{0,8},{1,9},{2,10},{3,11},{4,12},{5,13},{6,14},{7,15},{8,16},{9,17... | collective-permute-start | bytes 122888 | tf_op jit(solution)/shard_map/ppermute | solution.py:380
  54.7 20.3 %collective-permute-start.7 = (bf16[64,320]{1,0:T(8,128)(2,1)S(1)}, bf16[64,320]{1,0:T(8,128)(2,1)S(1)}, u32[]{:S(2)}, u32[]{:S(2)}) collective-permute-start(bf16[64,320]{1,0:T(8,128)(2,1)S(1)} %copy-done.11), channel_id=1, source_target_pairs={{0,16},{1,17},{2,18},{3,19},{4,20},{5,21},{6,22},{7,23},{8,24},{9,... | collective-permute-start | bytes 122888 | tf_op jit(solution)/shard_map/ppermute | solution.py:380
  55.2 24.6 %collective-permute-start.8 = (bf16[64,320]{1,0:T(8,128)(2,1)}, bf16[64,320]{1,0:T(8,128)(2,1)}, u32[]{:S(2)}, u32[]{:S(2)}) collective-permute-start(bf16[64,320]{1,0:T(8,128)(2,1)} %get-tuple-element.24), channel_id=1, source_target_pairs={{0,24},{1,25},{2,26},{3,27},{4,28},{5,29},{6,30},{7,31},{8,0},{9,1... | collective-permute-start | bytes 122888 | tf_op jit(solution)/shard_map/ppermute | solution.py:380
  75.0 0.7 copy-start.4
  77.2 15.2 %copy-start = (bf16[3584,240]{1,0:T(8,128)(2,1)}, bf16[3584,240]{1,0:T(8,128)(2,1)S(1)}, u32[]{:S(2)}) copy-start(bf16[3584,240]{1,0:T(8,128)(2,1)S(1)} %constant_dynamic-update-slice_fusion.5.one) | copy-start | bytes 5160964
  79.8 36.0 %collective-permute-start.5 = (bf16[3584,240]{0,1:T(8,128)(2,1)}, bf16[3584,240]{0,1:T(8,128)(2,1)S(1)}, u32[]{:S(2)}, u32[]{:S(2)}) collective-permute-start(bf16[3584,240]{0,1:T(8,128)(2,1)} %copy.50), channel_id=1, source_target_pairs={{0,8},{1,9},{2,10},{3,11},{4,12},{5,13},{6,14},{7,15},{8,0},{9,1},... | collective-permute-start | bytes 5160968 | tf_op jit(solution)/shard_map/ppermute | solution.py:380
  81.3 18.3 %collective-permute-start.10 = (bf16[256,320]{1,0:T(8,128)(2,1)}, bf16[256,320]{1,0:T(8,128)(2,1)}, u32[]{:S(2)}, u32[]{:S(2)}) collective-permute-start(bf16[256,320]{1,0:T(8,128)(2,1)} %constant_dynamic-update-slice_fusion.11.refs_3_), channel_id=1, source_target_pairs={{0,7},{1,2},{2,1},{3,4},{4,3},{5,6},{6,5},{7,0},{8,15},{9,10},{10,... | collective-permute-start | bytes 491528 | tf_op jit(solution)/shard_map/ppermute | solution.py:380
  89.4 10.2 %collective-permute-start.11 = (bf16[256,320]{1,0:T(8,128)(2,1)}, bf16[256,320]{1,0:T(8,128)(2,1)}, u32[]{:S(2)}, u32[]{:S(2)}) collective-permute-start(bf16[256,320]{1,0:T(8,128)(2,1)} %constant_dynamic-update-slice_fusion.11.refs_3_), channel_id=1, source_target_pairs={{0,6},{1,3},{2,0},{3,5},{4,2},{5,7},{6,4},{7,1},{8,14},{9,11},{10,... | collective-permute-start | bytes 491528 | tf_op jit(solution)/shard_map/ppermute | solution.py:380
  91.0 8.7 %collective-permute-start.9 = (bf16[256,320]{1,0:T(8,128)(2,1)}, bf16[256,320]{1,0:T(8,128)(2,1)}, u32[]{:S(2)}, u32[]{:S(2)}) collective-permute-start(bf16[256,320]{1,0:T(8,128)(2,1)} %constant_dynamic-update-slice_fusion.11.refs_3_), channel_id=1, source_target_pairs={{0,1},{1,0},{2,3},{3,2},{4,5},{5,4},{6,7},{7,6},{8,9},{9,8},{10,11... | collective-permute-start | bytes 491528 | tf_op jit(solution)/shard_map/ppermute | solution.py:380
  98.8 16.4 %copy-start.10 = (f32[1280]{0:T(1024)S(1)}, f32[1280]{0:T(1024)}, u32[]{:S(2)}) copy-start(f32[1280]{0:T(1024)} %param.16) | copy-start | bytes 15364
  107.3 1.8 %collective-permute-start.12 = (bf16[4,96,320]{2,1,0:T(8,128)(2,1)}, bf16[4,96,320]{2,1,0:T(8,128)(2,1)S(1)}, u32[]{:S(2)}, u32[]{:S(2)}) collective-permute-start(bf16[4,96,320]{2,1,0:T(8,128)(2,1)} %get-tuple-element.26), channel_id=1, source_target_pairs={{0,8},{1,9},{2,10},{3,11},{4,12},{5,13},{6,14},{7,15},{8,0},{9,1},... | collective-permute-start | bytes 737288 | tf_op jit(solution)/shard_map/ppermute | solution.py:380
  109.1 0.7 copy-start.5
  111.7 12.1 %collective-permute-start.13 = (bf16[96,320]{1,0:T(8,128)(2,1)}, bf16[96,320]{1,0:T(8,128)(2,1)S(1)}, u32[]{:S(2)}, u32[]{:S(2)}) collective-permute-start(bf16[96,320]{1,0:T(8,128)(2,1)} %get-tuple-element.28), channel_id=1, source_target_pairs={{0,1},{1,0},{2,3},{3,2},{4,5},{5,4},{6,7},{7,6},{8,9},{9,8},{10,11... | collective-permute-start | bytes 184328 | tf_op jit(solution)/shard_map/ppermute | solution.py:380
  113.6 10.3 %collective-permute-start.14 = (bf16[96,320]{1,0:T(8,128)(2,1)}, bf16[96,320]{1,0:T(8,128)(2,1)S(1)}, u32[]{:S(2)}, u32[]{:S(2)}) collective-permute-start(bf16[96,320]{1,0:T(8,128)(2,1)} %get-tuple-element.29), channel_id=1, source_target_pairs={{0,16},{1,17},{2,18},{3,19},{4,20},{5,21},{6,22},{7,23},{8,24},{9,... | collective-permute-start | bytes 184328 | tf_op jit(solution)/shard_map/ppermute | solution.py:380
  115.1 8.7 %collective-permute-start.15 = (bf16[96,320]{1,0:T(8,128)(2,1)}, bf16[96,320]{1,0:T(8,128)(2,1)S(1)}, u32[]{:S(2)}, u32[]{:S(2)}) collective-permute-start(bf16[96,320]{1,0:T(8,128)(2,1)} %get-tuple-element.30), channel_id=1, source_target_pairs={{0,17},{1,16},{2,19},{3,18},{4,21},{5,20},{6,23},{7,22},{8,25},{9,... | collective-permute-start | bytes 184328 | tf_op jit(solution)/shard_map/ppermute | solution.py:380
  123.8 0.6 copy-start.6
  123.8 0.6 copy-start.7
  123.8 0.7 copy-start.8

commit v2 on v1

v2 whole, which is shorter than its diff:
```python
import jax
import jax.numpy as jnp
from jax import lax
from jax.experimental import pallas as pl
from jax.experimental.pallas import tpu as pltpu
from jax.sharding import PartitionSpec as P

HREACH = 2
KB = 9
R = 4
BW = 8
EPSILON = 1e-05
BF = jnp.bfloat16
F32 = jnp.float32
AXES = ("lat", "lon")


def shape_of(shape, dtype):
    return jax.ShapeDtypeStruct(tuple(shape), dtype)


def whole(count):
    return [pl.BlockSpec(memory_space=pltpu.VMEM) for _ in range(count)]


def scalars(count):
    return [pl.BlockSpec(memory_space=pltpu.SMEM) for _ in range(count)]


def params(mebibytes=24):
    return pltpu.CompilerParams(vmem_limit_bytes=mebibytes * 1024 * 1024)


class Plan:
    def __init__(self, lats, lons, latent, filters, mix_weight, up_weight, down_weight):
        self.lats, self.lons = lats, lons
        self.ys = lats // 2
        self.zs = lons // 2
        self.cycles, self.members, self.cells, self.width = latent.shape
        self.basis, _, self.slots, self.band = filters.shape
        self.depth, self.out = mix_weight.shape[1], mix_weight.shape[2]
        self.lift = up_weight.shape[1]
        self.down_rows = down_weight.shape[0]
        self.half = self.cycles * self.members * self.cells
        self.body = self.cycles * self.cells
        self.lanes = self.members * self.depth
        self.wide = -(-self.lanes // 128) * 128
        self.taps_row = self.wide // 128
        self.groups = -(-self.cycles // self.taps_row)
        self.piece = self.body + 16 * self.groups
        self.kpad = -(-self.depth // 128) * 128
        self.group = 3
        self.mix_rows = (self.basis // 3) * self.depth
        self.mix_lanes = -(-self.group * self.out // 128) * 128
        self.mlp_lanes = 8 * self.out
        self.total = self.cycles * lats
        self.window = 4 * self.cells
        self.double = 2 * self.cells

    def fits(self):
        return (
            self.lats == 4
            and self.lons % 2 == 0
            and self.cells == 8
            and self.members == 2
            and self.slots * self.window == 128
            and self.band == 8
            and self.basis % 3 == 0
            and self.basis < 16
            and self.lift == 2 * self.out
            and self.depth == self.lift
            and self.down_rows == 4 * self.out
            and self.out % 16 == 0
            and self.mlp_lanes % 128 == 0
            and self.body % 16 == 0
        )


def place():
    a, b = lax.axis_index("lat"), lax.axis_index("lon")
    return a, b // 2, b % 2


def normal_kernel(plan, rows, cols, latent, gain, filters, *rest):
    p = plan
    msgs, stage = rest[: p.lats], rest[p.lats]
    a, _, _ = place()
    flat = latent[...].astype(F32).reshape(p.half, p.width)
    mean = jnp.mean(flat, axis=-1, keepdims=True)
    centered = flat - mean
    variance = jnp.mean(centered * centered, axis=-1, keepdims=True)
    normal = centered * lax.rsqrt(variance + EPSILON) * gain[...]
    normal = normal.reshape(p.cycles, p.members, p.cells, p.width)
    for e in range(p.members):
        part = normal[:, e].reshape(p.body, p.width).astype(BF)
        for q in range(p.lats):
            slot = lax.rem(q - a + p.lats, p.lats)
            stage[slot, :, e * p.depth : (e + 1) * p.depth] = part[
                :, q * p.depth : (q + 1) * p.depth
            ]
    row = lax.broadcasted_iota(jnp.int32, (p.slots * p.band, 128), 0)
    lane = lax.broadcasted_iota(jnp.int32, (p.slots * p.band, 128), 1)
    first = lax.broadcasted_iota(jnp.int32, (16, 128), 0)
    second = lax.broadcasted_iota(jnp.int32, (16, 128), 1)
    tails = []
    for g in range(p.groups):
        blocks = []
        for i in range(g * p.taps_row, (g + 1) * p.taps_row):
            if i >= p.cycles:
                blocks.append(jnp.zeros((16, 128), F32))
                continue
            target = jnp.zeros((p.slots * p.band, 128), jnp.int32)
            offset = jnp.zeros((16, 128), jnp.int32)
            for r in range(p.slots):
                start = r * p.window + p.cells + cols[r, i] - r * p.band
                target = jnp.where(row // p.band == r, start + row, target)
                offset = jnp.where(second == r, rows[r, i], offset)
            hit = jnp.where(lane == target, 1.0, 0.0).astype(BF)
            taps = lax.dot_general(
                filters[i], hit, (((0,), (0,)), ((), ())), preferred_element_type=F32
            )
            taps = jnp.concatenate([taps, jnp.zeros((16 - p.basis, 128), F32)], axis=0)
            blocks.append(jnp.where(first == p.basis, offset.astype(F32), taps))
        tails.append(jnp.concatenate(blocks, axis=1).astype(BF))
    for s in range(p.lats):
        msgs[s][0 : p.body, 0 : p.lanes] = stage[s]
        if p.wide > p.lanes:
            msgs[s][0 : p.body, p.lanes :] = jnp.zeros((p.body, p.wide - p.lanes), BF)
        for g in range(p.groups):
            msgs[s][p.body + 16 * g : p.body + 16 * (g + 1), :] = tails[g]


def normal_pieces(plan, rows, cols, latent, gain, filters):
    p = plan
    return pl.pallas_call(
        lambda *refs: normal_kernel(p, *refs),
        out_shape=[shape_of((p.piece, p.wide), BF)] * p.lats,
        in_specs=scalars(2) + whole(3),
        out_specs=whole(p.lats),
        scratch_shapes=[pltpu.VMEM((p.lats, p.body, p.lanes), BF)],
        compiler_params=params(60),
        name="normalize",
    )(rows, cols, latent, gain, filters)


def pack_kernel(plan, mix, up, down, mlp_pack, mix_pack):
    p = plan
    for q in range(p.lift // p.out):
        mlp_pack[:, q * p.depth : (q + 1) * p.depth] = up[q * p.out : (q + 1) * p.out, :]
    mlp_pack[:, 2 * p.depth :] = down[...]
    for k in range(p.basis):
        u, v = k // p.group, k % p.group
        mix_pack[u * p.depth : (u + 1) * p.depth, v * p.out : (v + 1) * p.out] = mix[k]
    used = p.group * p.out
    if p.mix_lanes > used:
        mix_pack[:, used:] = jnp.zeros((p.mix_rows, p.mix_lanes - used), BF)


def pack_weights(plan, mix, up, down):
    p = plan
    return pl.pallas_call(
        lambda *refs: pack_kernel(p, *refs),
        out_shape=[
            shape_of((p.out, p.mlp_lanes), BF),
            shape_of((p.mix_rows, p.mix_lanes), BF),
        ],
        in_specs=whole(3),
        out_specs=whole(2),
        compiler_params=params(60),
        name="pack_weights",
    )(mix, up, down)


def contract_kernel(plan, own, pair, near, far, *rest):
    p = plan
    pieces = rest[: p.lats]
    contracted, grid, taps, numbers, table, done = rest[p.lats :]
    a, z, x = place()
    even = x == 0
    for s in range(p.lats):
        for g in range(p.groups):
            lo = p.body + 16 * g
            block = pieces[s][lo : lo + 16, :].astype(F32)
            for i in range(p.taps_row):
                if g * p.taps_row + i < p.cycles:
                    taps[s * p.cycles + g * p.taps_row + i] = block[:, i * 128 : (i + 1) * 128]
            numbers[8 * (s * p.groups + g) : 8 * (s * p.groups + g) + 8, :] = block[
                8:16, :
            ].astype(jnp.int32)
    load = pltpu.make_async_copy(numbers, table, done)
    load.start()
    edge = jnp.zeros((HREACH,) + grid.shape[1:], BF)
    grid[0:HREACH] = edge
    grid[HREACH + p.total : 2 * HREACH + p.total] = edge
    gap = p.kpad - p.depth
    for s in range(p.lats):
        band = lax.rem(a - s + p.lats, p.lats)
        lo = s * p.body

        def read(ref):
            return ref[lo : lo + p.body, 0 : p.lanes].astype(F32)

        mine, other, first, second = read(own), read(pair), read(near), read(far)
        blocks = (
            jnp.where(even, first, second),
            jnp.where(even, mine, other),
            jnp.where(even, other, mine),
            jnp.where(even, second, first),
        )
        joined = jnp.concatenate(
            [block.reshape(p.cycles, p.cells, p.lanes) for block in blocks], axis=1
        ).astype(BF)
        where = HREACH + band * p.cycles
        for e in range(p.members):
            grid[pl.ds(where, p.cycles), :, e * p.kpad : e * p.kpad + p.depth] = joined[
                :, :, e * p.depth : (e + 1) * p.depth
            ]
            if gap:
                grid[pl.ds(where, p.cycles), :, e * p.kpad + p.depth : (e + 1) * p.kpad] = (
                    jnp.zeros((p.cycles, p.window, gap), BF)
                )
    load.wait()

    for s in range(p.lats):
        band = lax.rem(a - s + p.lats, p.lats)
        for c in range(p.cycles):
            i = band * p.cycles + c
            line = 8 * (s * p.groups + c // p.taps_row) + p.basis - 8
            lane = (c % p.taps_row) * 128
            source = jnp.concatenate(
                [grid[i + HREACH + table[line, lane + r]] for r in range(p.slots)], axis=0
            )
            lhs = jnp.concatenate(
                [
                    pltpu.roll(
                        jnp.broadcast_to(
                            taps[s * p.cycles + c, k : k + 1, :], (p.double, 128)
                        ),
                        0,
                        1,
                        stride=1,
                        stride_axis=0,
                    )
                    for k in range(p.basis)
                ],
                axis=0,
            ).astype(BF)
            result = jnp.dot(lhs, source, preferred_element_type=F32).astype(BF)
            at = i * (p.members * p.double)
            for e in range(p.members):
                for k in range(p.basis):
                    contracted[
                        pl.ds(pl.multiple_of(at + e * p.double, p.double), p.double),
                        k * p.kpad : (k + 1) * p.kpad,
                    ] = result[
                        k * p.double : (k + 1) * p.double, e * p.kpad : (e + 1) * p.kpad
                    ]


def contract(plan, own, pair, near, far, pieces):
    p = plan
    lines = 8 * p.lats * p.groups
    return pl.pallas_call(
        lambda *refs: contract_kernel(p, *refs),
        out_shape=shape_of((p.total * p.members * p.double, p.basis * p.kpad), BF),
        in_specs=whole(4 + p.lats),
        out_specs=pl.BlockSpec(memory_space=pltpu.VMEM),
        scratch_shapes=[
            pltpu.VMEM((p.total + 2 * HREACH, p.window, p.members * p.kpad), BF),
            pltpu.VMEM((p.total, 16, 128), F32),
            pltpu.VMEM((lines, p.wide), jnp.int32),
            pltpu.SMEM((lines, p.wide), jnp.int32),
            pltpu.SemaphoreType.DMA,
        ],
        compiler_params=params(),
        name="contract",
    )(own, pair, near, far, *pieces)


def mix_kernel(plan, contracted, *rest):
    p = plan
    packs = rest[: p.zs]
    keep, send, slots, mixing = rest[p.zs :]
    a, z, x = place()
    if p.kpad > p.depth:
        for k in range(p.basis):
            mixing[k * p.kpad + p.depth : (k + 1) * p.kpad, :] = jnp.zeros(
                (p.kpad - p.depth, p.zs * p.out), BF
            )
    for s in range(p.zs):
        slots[lax.rem(z - s + p.zs, p.zs)] = packs[s][...]
    for b in range(p.zs):
        for k in range(p.basis):
            u, v = k // p.group, k % p.group
            mixing[k * p.kpad : k * p.kpad + p.depth, b * p.out : (b + 1) * p.out] = slots[
                b, u * p.depth : (u + 1) * p.depth, v * p.out : (v + 1) * p.out
            ]
    count = 2 * p.half
    core = lax.rem(a, 2)
    for t in range(p.ys):
        y = lax.rem(a // 2 + t, p.ys)
        for mate in range(2):
            band = 2 * y + (core if mate == 0 else 1 - core)
            at = pl.multiple_of(band * count, count)
            total = jnp.dot(
                contracted[pl.ds(at, count), :], mixing[...], preferred_element_type=F32
            ).reshape(p.cycles * p.members, 2, p.cells, p.zs * p.out)
            left = total[:, 0].reshape(p.half, p.zs * p.out)
            right = total[:, 1].reshape(p.half, p.zs * p.out)
            for w in range(2):
                value = jnp.where((x ^ w) == 0, left, right)
                if mate == 0:
                    keep[2 * t + w] = value
                else:
                    send[2 * t + w] = value.astype(BF)


def mix_basis(plan, contracted, packs):
    p = plan
    out = p.zs * p.out
    return pl.pallas_call(
        lambda *refs: mix_kernel(p, *refs),
        out_shape=[
            shape_of((2 * p.ys, p.half, out), F32),
            shape_of((2 * p.ys, p.half, out), BF),
        ],
        in_specs=whole(1 + p.zs),
        out_specs=whole(2),
        scratch_shapes=[
            pltpu.VMEM((p.zs, p.mix_rows, p.mix_lanes), BF),
            pltpu.VMEM((p.basis * p.kpad, out), BF),
        ],
        compiler_params=params(),
        name="mix_basis",
    )(contracted, *packs)


def add_kernel(keep, arrived, own, *msgs):
    for i in range(keep.shape[0]):
        value = keep[i] + arrived[i].astype(F32)
        if i == 0:
            own[...] = value
        else:
            msgs[i - 1][...] = value.astype(BF)


def add_cores(keep, arrived):
    count, half, out = keep.shape
    outs = pl.pallas_call(
        add_kernel,
        out_shape=[shape_of((half, out), F32)] + [shape_of((half, out), BF)] * (count - 1),
        in_specs=whole(2),
        out_specs=whole(count),
        compiler_params=params(),
        name="add_cores",
    )(keep, arrived)
    return outs[0], outs[1:]


def unpack_kernel(plan, mine, sibling, up, down, slots):
    p = plan
    a, z, x = place()
    core = lax.rem(a, 2)
    for mate, stack in enumerate((mine, sibling)):
        c = core if mate == 0 else 1 - core
        for step in range(4):
            low, high = step % 2, step // 2
            dx = jnp.where(c == 0, low, high)
            dy = jnp.where(c == 0, high, low)
            lat = 2 * ((a // 2) ^ dy) + c
            for s in range(p.zs):
                lon = 2 * lax.rem(z - s + p.zs, p.zs) + (x ^ dx)
                index = step * p.zs + s
                slots[lat * p.lons + lon] = stack[index * p.out : (index + 1) * p.out, :]
    for a in range(p.lats):
        for b in range(p.lons):
            i = a * p.lons + b
            for q in range(p.lift // p.out):
                up[
                    a * p.depth + q * p.out : a * p.depth + (q + 1) * p.out,
                    b * p.lift : (b + 1) * p.lift,
                ] = slots[i, :, q * p.depth : (q + 1) * p.depth]
            down[
                b * p.out : (b + 1) * p.out, a * p.down_rows : (a + 1) * p.down_rows
            ] = slots[i, :, 2 * p.depth :]


def unpack(plan, mine, sibling):
    p = plan
    return pl.pallas_call(
        lambda *refs: unpack_kernel(p, *refs),
        out_shape=[
            shape_of((p.lats * p.depth, p.lons * p.lift), BF),
            shape_of((p.lons * p.out, p.lats * p.down_rows), BF),
        ],
        in_specs=whole(2),
        out_specs=whole(2),
        scratch_shapes=[pltpu.VMEM((p.lats * p.lons, p.out, p.mlp_lanes), BF)],
        compiler_params=params(),
        name="mlp_weights",
    )(mine, sibling)


def mlp_kernel(plan, latent, bias, up, down, own, *rest):
    p = plan
    arrived, (out, conv) = rest[:-2], rest[-2:]
    _, _, x = place()
    even = x == 0
    mine = own[...]
    other = None
    for i, ref in enumerate(arrived):
        value = ref[...].astype(F32)
        if (i + 1) % 2 == 0:
            mine = mine + value
        else:
            other = value if other is None else other + value
    first = jnp.where(even, mine, other)
    second = jnp.where(even, other, mine)
    for b in range(p.zs):
        cols = slice(b * p.out, (b + 1) * p.out)
        conv[:, 2 * b * p.out : (2 * b + 1) * p.out] = first[:, cols]
        conv[:, (2 * b + 1) * p.out : (2 * b + 2) * p.out] = second[:, cols]
    hidden = (latent[...].astype(F32).reshape(p.half, p.width) + conv[...]).astype(BF)
    lifted = jnp.dot(hidden, up[...], preferred_element_type=F32) + bias[...]
    activated = (lifted * (1.0 + lax.erf(lifted * (0.5**0.5))) * 0.5).astype(BF)
    lowered = lax.dot_general(
        activated, down[...], (((1,), (1,)), ((), ())), preferred_element_type=F32
    )
    out[...] = (hidden.astype(F32) + lowered).astype(BF).reshape(out.shape)


def mlp(plan, latent, bias, up, down, own, arrived):
    p = plan
    return pl.pallas_call(
        lambda *refs: mlp_kernel(p, *refs),
        out_shape=shape_of(latent.shape, BF),
        in_specs=whole(5 + len(arrived)),
        out_specs=pl.BlockSpec(memory_space=pltpu.VMEM),
        scratch_shapes=[pltpu.VMEM((p.half, p.width), F32)],
        compiler_params=params(),
        name="sum_mlp",
    )(latent, bias, up, down, own, *arrived)


def mover(plan):
    p = plan

    def move(value, target):
        pairs = []
        for a in range(p.lats):
            for b in range(p.lons):
                c, d = target(a, b)
                pairs.append((a * p.lons + b, (c % p.lats) * p.lons + d % p.lons))
        return lax.ppermute(value, AXES, pairs)

    return move


def after(value, *others):
    return lax.optimization_barrier((value,) + others)[0]


def shards_fast(
    plan,
    latent,
    norm_gain,
    filters,
    row_offsets,
    col_offsets,
    mix_weight,
    up_weight,
    up_bias,
    down_weight,
):
    p = plan
    move = mover(p)
    taps = filters.transpose(1, 2, 3, 0).reshape(p.cycles, p.slots * p.band, p.basis)
    msgs = normal_pieces(
        p, row_offsets.T, col_offsets.T, latent, norm_gain, taps
    )
    pieces = [msgs[0]]
    for s in range(1, p.lats):
        pieces.append(move(msgs[s], lambda i, j, s=s: (i + s, j)))
    mlp_pack, mix_pack = pack_weights(
        p, mix_weight, after(up_weight, msgs[0]), down_weight.T
    )
    shares = [mlp_pack]
    for s in range(1, p.zs):
        shares.append(move(mlp_pack, lambda i, j, s=s: (i, j + 2 * s)))
    own = jnp.concatenate([piece[: p.body] for piece in pieces], axis=0)
    pair = move(own, lambda i, j: (i, j ^ 1))
    near = move(own, lambda i, j: (i, j + 1 if j % 2 else j - 1))
    far = move(own, lambda i, j: (i, j + 2 if j % 2 else j - 2))

    mix_pack = after(mix_pack, own)
    packs = [mix_pack]
    for s in range(1, p.zs):
        packs.append(move(mix_pack, lambda i, j, s=s: (i, j + 2 * s)))

    contracted = contract(p, own, pair, near, far, pieces)
    share = after(jnp.concatenate(shares, axis=0), near, far)
    crossed = move(share, lambda i, j: (i + 2, j) if i % 2 else (i, j ^ 1))
    share = after(jnp.concatenate([share, crossed], axis=0), contracted, packs[1])
    crossed = move(share, lambda i, j: (i, j ^ 1) if i % 2 else (i + 2, j))
    keep, send = mix_basis(p, contracted, packs)
    arrived = move(send, lambda i, j: (i ^ 1, j))
    mine, outgoing = add_cores(keep, arrived)
    share = after(jnp.concatenate([share, crossed], axis=0), mine)
    up, down = unpack(p, share, move(share, lambda i, j: (i ^ 1, j)))
    incoming = []
    for index, value in enumerate(outgoing):
        t, w = (index + 1) // 2, (index + 1) % 2
        incoming.append(move(value, lambda i, j, t=t, w=w: (i + 2 * t, j ^ w)))

    return mlp(p, latent, up_bias, up, down, mine, incoming)


def padded(shard, sides, width, wrap):
    for axis, dim in sides:
        size, length = (lax.axis_size(axis), shard.shape[dim])
        up = [(i, (i + 1) % size) for i in range(size if wrap else size - 1)]
        down = [(j, i) for i, j in up]
        last = lax.slice_in_dim(shard, length - width, length, axis=dim)
        leading = lax.slice_in_dim(shard, 0, width, axis=dim)
        before = lax.ppermute(last, axis, up)
        after = lax.ppermute(leading, axis, down)
        shard = jnp.concatenate([before, shard, after], axis=dim)
    return shard


def normalize(latent, norm_gain):
    widened = latent.astype(jnp.float32)
    channel_mean = jnp.mean(widened, axis=-1, keepdims=True)
    centered = widened - channel_mean
    variance = jnp.mean(centered * centered, axis=-1, keepdims=True)
    return (centered * lax.rsqrt(variance + EPSILON) * norm_gain).astype(jnp.bfloat16)


def contract_cycles(
    band_slab, filters, row_offsets, col_offsets, cycle_count, out_cells, shift_cells
):
    members = band_slab.shape[1]
    channel_share = band_slab.shape[3]

    def cycle_output(cycle_index):
        pieces = []
        for row_slot in range(R):
            where = cycle_index + HREACH + row_offsets[cycle_index, row_slot]
            source = lax.dynamic_index_in_dim(band_slab, where, 0, keepdims=False)
            start = col_offsets[cycle_index, row_slot] + shift_cells
            segment = lax.dynamic_slice_in_dim(source, start, out_cells + BW - 1, 1)
            for band_step in range(BW):
                pieces.append(segment[:, band_step : band_step + out_cells])
        stacked = jnp.stack(pieces).reshape(R * BW, members * out_cells * channel_share)
        cycle_filter = lax.dynamic_index_in_dim(filters, cycle_index, 1, keepdims=False).reshape(
            KB, R * BW
        )
        contracted = jnp.dot(cycle_filter, stacked, preferred_element_type=jnp.float32).astype(
            jnp.bfloat16
        )
        return contracted.reshape(KB, members, out_cells, channel_share)

    return lax.map(cycle_output, jnp.arange(cycle_count, dtype=jnp.int32))


def shards_plain(
    latent,
    norm_gain,
    filters,
    row_offsets,
    col_offsets,
    mix_weight,
    up_weight,
    up_bias,
    down_weight,
):
    cycle_count = latent.shape[0]
    local_cells = latent.shape[2]
    width = latent.shape[3]
    partial_weights = (
        lax.all_gather(mix_weight, "lat", axis=1, tiled=True),
        lax.all_gather(up_weight, "lat", axis=0, tiled=True),
        lax.all_gather(down_weight, "lat", axis=0, tiled=True),
    )
    mix_full, up_full, down_full = (
        lax.all_gather(partial_weights[0], "lon", axis=2, tiled=True),
        lax.all_gather(partial_weights[1], "lon", axis=1, tiled=True),
        lax.all_gather(partial_weights[2], "lon", axis=1, tiled=True),
    )
    normalized = normalize(latent, norm_gain)
    side_reach = BW // 2 + 2
    cycle_rims = padded(normalized, (("lat", 0),), HREACH, False)
    band_slab = padded(cycle_rims, (("lon", 2),), side_reach, True)
    contracted = contract_cycles(
        band_slab, filters, row_offsets, col_offsets, cycle_count, local_cells, side_reach
    )
    convolved = jnp.einsum(
        "ikejc,kcd->iejd", contracted, mix_full, preferred_element_type=jnp.float32
    )
    hidden = (latent.astype(jnp.float32) + convolved).astype(jnp.bfloat16)
    flattened = hidden.reshape(-1, width)
    lifted = jnp.dot(flattened, up_full, preferred_element_type=jnp.float32) + up_bias
    activated = jax.nn.gelu(lifted, approximate=False).astype(jnp.bfloat16)
    result = flattened.astype(jnp.float32) + jnp.dot(
        activated, down_full, preferred_element_type=jnp.float32
    )
    return result.astype(jnp.bfloat16).reshape(latent.shape)


def solution(mesh):
    lats, lons = mesh.shape["lat"], mesh.shape["lon"]

    def shards(*args):
        latent, _, filters, _, _, mix_weight, up_weight, _, down_weight = args
        plan = Plan(lats, lons, latent, filters, mix_weight, up_weight, down_weight)
        if plan.fits():
            return shards_fast(plan, *args)
        return shards_plain(*args)

    in_specs = (
        P("lat", None, "lon", None),
        P(),
        P(None, "lat", None, None),
        P("lat", None),
        P("lat", None),
        P(None, "lat", "lon"),
        P("lat", "lon"),
        P(),
        P("lat", "lon"),
    )
    out_specs = P("lat", None, "lon", None)
    return jax.shard_map(shards, mesh=mesh, in_specs=in_specs, out_specs=out_specs, check_vma=False)
```

time: 129 us -> 70.1 us (0.54)
  local copies, waits for them, and re-layouts: 23.9 us -> 0.8 us
  waiting for transfers between devices: 51.3 us -> 30 us
  Pallas kernels: 21.1 us -> 12.8 us
  other arithmetic: 6.36 us -> 1.16 us
    ppermute x16 -> x19, waiting for transfers between devices: 51.3 us -> 30 us  [move(): return lax.ppermute(value, AXES, pairs)]
    unnamed x34 -> x8, local copies, waits for them, and re-layouts: 5.49 us -> 0.02 us
    concatenate x5 -> x0, local copies, waits for them, and re-layouts: 5.42 us -> none  [the longest x2 2.67 us: shards_fast(): share = jnp.concatenate(bands, axis=0)]
    pallas_call x3 -> x5, Pallas kernels: 15.7 us -> 11.1 us  [the longest x1 3.47 us: contract(): pl.pallas_call(lambda *refs: contract_kernel(p, *refs), out_shape=shape_o...]
    ppermute x2 -> x0, local copies, waits for them, and re-layouts: 3.71 us -> none  [move(): return lax.ppermute(value, AXES, pairs)]
    reshape x6 -> x0, local copies, waits for them, and re-layouts: 3.61 us -> none  [the longest x1 1.28 us: shards_fast(): norm_gain.reshape(1, -1)]
    gather x1 -> x0, local copies, waits for them, and re-layouts: 2.01 us -> none  [shards_fast(): infos = infos[order].reshape(p.total, p.meta)]
    pallas_call x1, Pallas kernels: 3.54 us -> 1.67 us  [mlp(): pl.pallas_call(lambda *refs: mlp_kernel(p, *refs), out_shape=shape_of(lat...]
  transfers between devices with their start and end apart: 16 -> 19, of which waited for: 7 -> 8; matrix products, arithmetic and copies ran while one was open for 15% -> 3% of each run, Pallas kernels for 12% -> 13%
where the time goes in v2:
time: 70.1 us; the launch traced here: 69.9 us
  waiting for transfers between devices  30 us (43%)
  starting transfers between devices  25 us (36%)
  Pallas kernels  12.8 us (18%)
  other arithmetic  1.16 us (2%)
  local copies, waits for them, and re-layouts  0.8 us (1%)
    ppermute x19, waiting for transfers between devices, move(): return lax.ppermute(value, AXES, pairs)  30 us
    ppermute x19, starting transfers between devices, move(): return lax.ppermute(value, AXES, pairs)  25 us
    pallas_call x1, Pallas kernels, contract(): pl.pallas_call(lambda *refs: contract_kernel(p, *refs), out_shape=shape_o...  3.47 us
    pallas_call x1, Pallas kernels, mix_basis(): pl.pallas_call(lambda *refs: mix_kernel(p, *refs), out_shape=[shape_of((2...  2.55 us
    pallas_call x1, Pallas kernels, pack_weights(): pl.pallas_call(lambda *refs: pack_kernel(p, *refs), out_shape=[shape_of((...  1.96 us
    pallas_call x1, Pallas kernels, normal_pieces(): pl.pallas_call(lambda *refs: normal_kernel(p, *refs), out_shape=[shape_of...  1.93 us
    pallas_call x1, Pallas kernels, mlp(): pl.pallas_call(lambda *refs: mlp_kernel(p, *refs), out_shape=shape_of(lat...  1.67 us
  transfers between devices with their start and end apart: 19, of which 8 were waited for; matrix products, arithmetic and copies ran while one was open for 3% of the time, Pallas kernels for 13%

profile of v2, /device:TPU:0, one launch (start us, length us, event | category | flops | bytes accessed | tf_op | source)
XLA Modules:
  0.0 69.9 jit_solution(11549221527564788339)
XLA Ops:
  0.0 1.9 %normalize.1 = (bf16[80,384]{1,0:T(8,128)(2,1)}, bf16[80,384]{1,0:T(8,128)(2,1)}, bf16[80,384]{1,0:T(8,128)(2,1)}, bf16[80,384]{1,0:T(8,128)(2,1)}) custom-call(s32[4,6]{1,0:T(4,128)} %bitcast.8, s32[4,6]{1,0:T(4,128)} %bitcast.9, bf16[6,2,8,640]{3,2,1,0:T(8,128)(2,1)} %refs_0_.3, f32[640]{0:T(1024)} %refs_3_.1, bf16[6,32,9]{2,1,0:T(8,128)(2,1)} %bitcast.7), custom_call_target="tpu_custom_call" | custom-call | tf_op jit(solution)/shard_map/normalize/pallas_call | solution.py:135
  1.9 0.5 collective-permute-start.3
  2.4 2.6 %collective-permute-start.4 = (bf16[80,384]{1,0:T(8,128)(2,1)}, bf16[80,384]{1,0:T(8,128)(2,1)S(1)}, u32[]{:S(2)}, u32[]{:S(2)}) collective-permute-start(bf16[80,384]{1,0:T(8,128)(2,1)} %get-tuple-element.28), channel_id=1, source_target_pairs={{0,16},{1,17},{2,18},{3,19},{4,20},{5,21},{6,22},{7,23},{8,24},{9,... | collective-permute-start | bytes 184328 | tf_op jit(solution)/shard_map/ppermute | solution.py:454
  5.0 1.4 %collective-permute-start.5 = (bf16[80,384]{1,0:T(8,128)(2,1)}, bf16[80,384]{1,0:T(8,128)(2,1)S(1)}, u32[]{:S(2)}, u32[]{:S(2)}) collective-permute-start(bf16[80,384]{1,0:T(8,128)(2,1)} %get-tuple-element.29), channel_id=1, source_target_pairs={{0,24},{1,25},{2,26},{3,27},{4,28},{5,29},{6,30},{7,31},{8,0},{9,1... | collective-permute-start | bytes 184328 | tf_op jit(solution)/shard_map/ppermute | solution.py:454
  6.4 2.0 %pack_weights.1 = (bf16[80,640]{1,0:T(8,128)(2,1)}, bf16[480,256]{1,0:T(8,128)(2,1)}) custom-call(bf16[9,160,80]{2,1,0:T(8,128)(2,1)} %refs_0_.2, bf16[160,160]{1,0:T(8,128)(2,1)} %refs_1_.1, bf16[80,320]{1,0:T(8,128)(2,1)} %bitcast.6), custom_call_target="tpu_custom_call" | custom-call | tf_op jit(solution)/shard_map/pack_weights/pallas_call | solution.py:161
  8.3 3.6 %collective-permute-start.2 = (bf16[80,640]{1,0:T(8,128)(2,1)}, bf16[80,640]{1,0:T(8,128)(2,1)S(1)}, u32[]{:S(2)}, u32[]{:S(2)}) collective-permute-start(bf16[80,640]{1,0:T(8,128)(2,1)} %get-tuple-element.26), channel_id=1, source_target_pairs={{0,6},{1,7},{2,0},{3,1},{4,2},{5,3},{6,4},{7,5},{8,14},{9,15},{10,... | collective-permute-start | bytes 307208 | tf_op jit(solution)/shard_map/ppermute | solution.py:454
  11.9 0.8 %slice.12 = bf16[48,384]{1,0:T(8,128)(2,1)S(1)} slice(bf16[80,384]{1,0:T(8,128)(2,1)} %get-tuple-element.24.refs_4_), slice={[0:48], [0:384]} | slice | bytes 73728 | tf_op jit(solution)/shard_map/slice | solution.py:490
  12.7 1.0 %collective-permute-start = (bf16[80,640]{1,0:T(8,128)(2,1)}, bf16[80,640]{1,0:T(8,128)(2,1)S(1)}, u32[]{:S(2)}, u32[]{:S(2)}) collective-permute-start(bf16[80,640]{1,0:T(8,128)(2,1)} %get-tuple-element.26), channel_id=1, source_target_pairs={{0,2},{1,3},{2,4},{3,5},{4,6},{5,7},{6,0},{7,1},{8,10},{9,11},{10,... | collective-permute-start | bytes 307208 | tf_op jit(solution)/shard_map/ppermute | solution.py:454
  13.8 2.9 %collective-permute-start.7 = (bf16[192,384]{1,0:T(8,128)(2,1)S(1)}, bf16[192,384]{1,0:T(8,128)(2,1)S(1)}, u32[]{:S(2)}, u32[]{:S(2)}) collective-permute-start(bf16[192,384]{1,0:T(8,128)(2,1)S(1)} %pad_maximum_fusion.3.refs_0_), channel_id=1, source_target_pairs={{0,6},{1,3},{2,0},{3,5},{4,2},{5,7},{6,4},{7,1},{8,14},{9,11},{10,... | collective-permute-start | bytes 442376 | tf_op jit(solution)/shard_map/ppermute | solution.py:454
  16.7 1.9 %collective-permute-start.6 = (bf16[192,384]{1,0:T(8,128)(2,1)S(1)}, bf16[192,384]{1,0:T(8,128)(2,1)S(1)}, u32[]{:S(2)}, u32[]{:S(2)}) collective-permute-start(bf16[192,384]{1,0:T(8,128)(2,1)S(1)} %pad_maximum_fusion.3.refs_0_), channel_id=1, source_target_pairs={{0,7},{1,2},{2,1},{3,4},{4,3},{5,6},{6,5},{7,0},{8,15},{9,10},{10,... | collective-permute-start | bytes 442376 | tf_op jit(solution)/shard_map/ppermute | solution.py:454
  18.6 2.8 %collective-permute-done.1 = bf16[80,640]{1,0:T(8,128)(2,1)S(1)} collective-permute-done((bf16[80,640]{1,0:T(8,128)(2,1)}, bf16[80,640]{1,0:T(8,128)(2,1)S(1)}, u32[]{:S(2)}, u32[]{:S(2)}) %collective-permute-start.1) | collective-permute-done | bytes 102432 | tf_op jit(solution)/shard_map/ppermute | solution.py:454
  21.5 0.9 %pad_maximum_fusion.2 = bf16[320,640]{1,0:T(8,128)(2,1)S(1)} fusion(bf16[80,640]{1,0:T(8,128)(2,1)S(1)} %collective-permute-done.2, bf16[80,640]{1,0:T(8,128)(2,1)S(1)} %collective-permute-done.1, bf16[80,640]{1,0:T(8,128)(2,1)S(1)} %collective-permute-done, bf16[80,640]{1,0:T(8,128)(2,1)} %get-tuple-element.26), kind=kLoop, calls=%fused_computation.2 | loop fusion | flops 1638400 | bytes 819200 | tf_op jit(solution)/shard_map/concatenate | solution.py:501
  22.4 1.6 %collective-permute-done.7.refs_3_ = bf16[192,384]{1,0:T(8,128)(2,1)S(1)} collective-permute-done((bf16[192,384]{1,0:T(8,128)(2,1)S(1)}, bf16[192,384]{1,0:T(8,128)(2,1)S(1)}, u32[]{:S(2)}, u32[]{:S(2)}) %collective-permute-start.7) | collective-permute-done | bytes 147488 | tf_op jit(solution)/shard_map/ppermute | solution.py:454
  24.0 2.2 %collective-permute-done.6.refs_2_ = bf16[192,384]{1,0:T(8,128)(2,1)S(1)} collective-permute-done((bf16[192,384]{1,0:T(8,128)(2,1)S(1)}, bf16[192,384]{1,0:T(8,128)(2,1)S(1)}, u32[]{:S(2)}, u32[]{:S(2)}) %collective-permute-start.6) | collective-permute-done | bytes 147488 | tf_op jit(solution)/shard_map/ppermute | solution.py:454
  26.2 3.4 %collective-permute-start.8 = (bf16[320,640]{1,0:T(8,128)(2,1)S(1)}, bf16[320,640]{1,0:T(8,128)(2,1)S(1)}, u32[]{:S(2)}, u32[]{:S(2)}) collective-permute-start(bf16[320,640]{1,0:T(8,128)(2,1)S(1)} %pad_maximum_fusion.2), channel_id=1, source_target_pairs={{0,1},{1,0},{2,3},{3,2},{4,5},{5,4},{6,7},{7,6},{8,24},{9,25},{10,... | collective-permute-start | bytes 1228808 | tf_op jit(solution)/shard_map/ppermute | solution.py:454
  29.7 0.6 collective-permute-start.10
  30.4 7.8 %collective-permute-done.9.refs_1_ = bf16[192,384]{1,0:T(8,128)(2,1)S(1)} collective-permute-done((bf16[192,384]{1,0:T(8,128)(2,1)S(1)}, bf16[192,384]{1,0:T(8,128)(2,1)S(1)}, u32[]{:S(2)}, u32[]{:S(2)}) %collective-permute-start.9) | collective-permute-done | bytes 147488 | tf_op jit(solution)/shard_map/ppermute | solution.py:454
  38.2 3.5 %contract.1.refs_0_ = bf16[768,2304]{1,0:T(8,128)(2,1)S(1)} custom-call(bf16[192,384]{1,0:T(8,128)(2,1)S(1)} %pad_maximum_fusion.3.refs_0_, bf16[192,384]{1,0:T(8,128)(2,1)S(1)} %collective-permute-done.9.refs_1_, bf16[192,384]{1,0:T(8,128)(2,1)S(1)} %collective-permute-done.6.refs_2_, bf16[192,384]{1,0:T(8,128)(2,1)S(1)} %collective-permute-done.7.refs_3_, ...), custom_call_target="tpu_custom_call" | custom-call | tf_op jit(solution)/shard_map/contract/pallas_call | solution.py:263
  41.8 1.1 %collective-permute-start.11 = (bf16[640,640]{1,0:T(8,128)(2,1)S(1)}, bf16[640,640]{1,0:T(8,128)(2,1)S(1)}, u32[]{:S(2)}, u32[]{:S(2)}) collective-permute-start(bf16[640,640]{1,0:T(8,128)(2,1)S(1)} %pad_maximum_fusion.1), channel_id=1, source_target_pairs={{0,16},{1,17},{2,18},{3,19},{4,20},{5,21},{6,22},{7,23},{8,9},{9,8... | collective-permute-start | bytes 2457608 | tf_op jit(solution)/shard_map/ppermute | solution.py:454
  42.9 1.3 %collective-permute-start.13 = (bf16[480,256]{1,0:T(8,128)(2,1)S(1)}, bf16[480,256]{1,0:T(8,128)(2,1)S(1)}, u32[]{:S(2)}, u32[]{:S(2)}) collective-permute-start(bf16[480,256]{1,0:T(8,128)(2,1)S(1)} %copy-done.1), channel_id=1, source_target_pairs={{0,6},{1,7},{2,0},{3,1},{4,2},{5,3},{6,4},{7,5},{8,14},{9,15},{10,... | collective-permute-start | bytes 737288 | tf_op jit(solution)/shard_map/ppermute | solution.py:454
  44.2 0.7 %collective-permute-start.12 = (bf16[480,256]{1,0:T(8,128)(2,1)S(1)}, bf16[480,256]{1,0:T(8,128)(2,1)S(1)}, u32[]{:S(2)}, u32[]{:S(2)}) collective-permute-start(bf16[480,256]{1,0:T(8,128)(2,1)S(1)} %copy-done.1), channel_id=1, source_target_pairs={{0,4},{1,5},{2,6},{3,7},{4,0},{5,1},{6,2},{7,3},{8,12},{9,13},{10,... | collective-permute-start | bytes 737288 | tf_op jit(solution)/shard_map/ppermute | solution.py:454
  44.9 5.5 %collective-permute-done.13.refs_4_ = bf16[480,256]{1,0:T(8,128)(2,1)S(1)} collective-permute-done((bf16[480,256]{1,0:T(8,128)(2,1)S(1)}, bf16[480,256]{1,0:T(8,128)(2,1)S(1)}, u32[]{:S(2)}, u32[]{:S(2)}) %collective-permute-start.13) | collective-permute-done | bytes 245792 | tf_op jit(solution)/shard_map/ppermute | solution.py:454
  50.4 6.2 %collective-permute-done.12.refs_3_ = bf16[480,256]{1,0:T(8,128)(2,1)S(1)} collective-permute-done((bf16[480,256]{1,0:T(8,128)(2,1)S(1)}, bf16[480,256]{1,0:T(8,128)(2,1)S(1)}, u32[]{:S(2)}, u32[]{:S(2)}) %collective-permute-start.12) | collective-permute-done | bytes 245792 | tf_op jit(solution)/shard_map/ppermute | solution.py:454
  56.6 2.5 %mix_basis.1 = (f32[4,96,320]{2,1,0:T(8,128)S(1)}, bf16[4,96,320]{2,1,0:T(8,128)(2,1)S(1)}) custom-call(bf16[768,2304]{1,0:T(8,128)(2,1)S(1)} %contract.1.refs_0_, bf16[480,256]{1,0:T(8,128)(2,1)S(1)} %copy-done.1, bf16[480,256]{1,0:T(8,128)(2,1)S(1)} %collective-permute-done.10.refs_2_, bf16[480,256]{1,0:T(8,128)(2,1)S(1)} %collective-permute-done.12.refs_3_, ...), custom_call_target="tpu_custom_call" | custom-call | tf_op jit(solution)/shard_map/mix_basis/pallas_call | solution.py:321
  59.3 1.6 %collective-permute-done.14.arrived = bf16[4,96,320]{2,1,0:T(8,128)(2,1)S(1)} collective-permute-done((bf16[4,96,320]{2,1,0:T(8,128)(2,1)S(1)}, bf16[4,96,320]{2,1,0:T(8,128)(2,1)S(1)}, u32[]{:S(2)}, u32[]{:S(2)}) %collective-permute-start.14) | collective-permute-done | bytes 245792 | tf_op jit(solution)/shard_map/ppermute | solution.py:454
  61.0 0.2 collective-permute-start.15
  61.2 1.0 %collective-permute-start.16 = (bf16[96,320]{1,0:T(8,128)(2,1)S(1)}, bf16[96,320]{1,0:T(8,128)(2,1)S(1)}, u32[]{:S(2)}, u32[]{:S(2)}) collective-permute-start(bf16[96,320]{1,0:T(8,128)(2,1)S(1)} %get-tuple-element.40), channel_id=1, source_target_pairs={{0,1},{1,0},{2,3},{3,2},{4,5},{5,4},{6,7},{7,6},{8,9},{9,8},{10,11... | collective-permute-start | bytes 184328 | tf_op jit(solution)/shard_map/ppermute | solution.py:454
  62.3 0.2 collective-permute-start.17
  62.5 2.3 %collective-permute-start.18 = (bf16[96,320]{1,0:T(8,128)(2,1)S(1)}, bf16[96,320]{1,0:T(8,128)(2,1)S(1)}, u32[]{:S(2)}, u32[]{:S(2)}) collective-permute-start(bf16[96,320]{1,0:T(8,128)(2,1)S(1)} %get-tuple-element.42), channel_id=1, source_target_pairs={{0,17},{1,16},{2,19},{3,18},{4,21},{5,20},{6,23},{7,22},{8,25},{9,... | collective-permute-start | bytes 184328 | tf_op jit(solution)/shard_map/ppermute | solution.py:454
  64.8 1.2 %mlp_weights.1 = (bf16[640,1280]{1,0:T(8,128)(2,1)S(1)}, bf16[640,1280]{1,0:T(8,128)(2,1)S(1)}) custom-call(bf16[1280,640]{1,0:T(8,128)(2,1)S(1)} %pad_maximum_fusion.refs_0_, bf16[1280,640]{1,0:T(8,128)(2,1)S(1)} %collective-permute-done.15.refs_1_), custom_call_target="tpu_custom_call" | custom-call | tf_op jit(solution)/shard_map/mlp_weights/pallas_call | solution.py:390
  66.0 2.2 %collective-permute-done.17.refs_6_ = bf16[96,320]{1,0:T(8,128)(2,1)S(1)} collective-permute-done((bf16[96,320]{1,0:T(8,128)(2,1)S(1)}, bf16[96,320]{1,0:T(8,128)(2,1)S(1)}, u32[]{:S(2)}, u32[]{:S(2)}) %collective-permute-start.17) | collective-permute-done | bytes 61472 | tf_op jit(solution)/shard_map/ppermute | solution.py:454
  68.2 1.7 %sum_mlp.1 = bf16[6,2,8,640]{3,2,1,0:T(8,128)(2,1)} custom-call(bf16[6,2,8,640]{3,2,1,0:T(8,128)(2,1)S(1)} %copy-done, f32[1280]{0:T(1024)S(1)} %copy-done.3, bf16[640,1280]{1,0:T(8,128)(2,1)S(1)} %get-tuple-element.38.refs_2_, bf16[640,1280]{1,0:T(8,128)(2,1)S(1)} %get-tuple-element.39.refs_3_, f32[96,320]{1,0:T(8,128)S(1)} %get-tuple-element.36.refs_4_, ...), custom_call_target="tpu_custom_call" | custom-call | tf_op jit(solution)/shard_map/sum_mlp/pallas_call | solution.py:434
  (29 shorter events, 0.5 us)
Async XLA Ops:
  1.9 36.2 %copy-start.2 = (bf16[80,384]{1,0:T(8,128)(2,1)S(1)}, bf16[80,384]{1,0:T(8,128)(2,1)}, u32[]{:S(2)}) copy-start(bf16[80,384]{1,0:T(8,128)(2,1)} %get-tuple-element.24.refs_4_) | copy-start | bytes 184324
  1.9 10.8 %collective-permute-start.3 = (bf16[80,384]{1,0:T(8,128)(2,1)}, bf16[80,384]{1,0:T(8,128)(2,1)S(1)}, u32[]{:S(2)}, u32[]{:S(2)}) collective-permute-start(bf16[80,384]{1,0:T(8,128)(2,1)} %get-tuple-element.27), channel_id=1, source_target_pairs={{0,8},{1,9},{2,10},{3,11},{4,12},{5,13},{6,14},{7,15},{8,16},{9,17... | collective-permute-start | bytes 184328 | tf_op jit(solution)/shard_map/ppermute | solution.py:454
  2.4 11.3 %collective-permute-start.4 = (bf16[80,384]{1,0:T(8,128)(2,1)}, bf16[80,384]{1,0:T(8,128)(2,1)S(1)}, u32[]{:S(2)}, u32[]{:S(2)}) collective-permute-start(bf16[80,384]{1,0:T(8,128)(2,1)} %get-tuple-element.28), channel_id=1, source_target_pairs={{0,16},{1,17},{2,18},{3,19},{4,20},{5,21},{6,22},{7,23},{8,24},{9,... | collective-permute-start | bytes 184328 | tf_op jit(solution)/shard_map/ppermute | solution.py:454
  5.0 8.8 %collective-permute-start.5 = (bf16[80,384]{1,0:T(8,128)(2,1)}, bf16[80,384]{1,0:T(8,128)(2,1)S(1)}, u32[]{:S(2)}, u32[]{:S(2)}) collective-permute-start(bf16[80,384]{1,0:T(8,128)(2,1)} %get-tuple-element.29), channel_id=1, source_target_pairs={{0,24},{1,25},{2,26},{3,27},{4,28},{5,29},{6,30},{7,31},{8,0},{9,1... | collective-permute-start | bytes 184328 | tf_op jit(solution)/shard_map/ppermute | solution.py:454
  8.3 10.3 %collective-permute-start.2 = (bf16[80,640]{1,0:T(8,128)(2,1)}, bf16[80,640]{1,0:T(8,128)(2,1)S(1)}, u32[]{:S(2)}, u32[]{:S(2)}) collective-permute-start(bf16[80,640]{1,0:T(8,128)(2,1)} %get-tuple-element.26), channel_id=1, source_target_pairs={{0,6},{1,7},{2,0},{3,1},{4,2},{5,3},{6,4},{7,5},{8,14},{9,15},{10,... | collective-permute-start | bytes 307208 | tf_op jit(solution)/shard_map/ppermute | solution.py:454
  11.9 9.5 %collective-permute-start.1 = (bf16[80,640]{1,0:T(8,128)(2,1)}, bf16[80,640]{1,0:T(8,128)(2,1)S(1)}, u32[]{:S(2)}, u32[]{:S(2)}) collective-permute-start(bf16[80,640]{1,0:T(8,128)(2,1)} %get-tuple-element.26), channel_id=1, source_target_pairs={{0,4},{1,5},{2,6},{3,7},{4,0},{5,1},{6,2},{7,3},{8,12},{9,13},{10,... | collective-permute-start | bytes 307208 | tf_op jit(solution)/shard_map/ppermute | solution.py:454
  12.7 8.7 %collective-permute-start = (bf16[80,640]{1,0:T(8,128)(2,1)}, bf16[80,640]{1,0:T(8,128)(2,1)S(1)}, u32[]{:S(2)}, u32[]{:S(2)}) collective-permute-start(bf16[80,640]{1,0:T(8,128)(2,1)} %get-tuple-element.26), channel_id=1, source_target_pairs={{0,2},{1,3},{2,4},{3,5},{4,6},{5,7},{6,0},{7,1},{8,10},{9,11},{10,... | collective-permute-start | bytes 307208 | tf_op jit(solution)/shard_map/ppermute | solution.py:454
  13.8 10.2 %collective-permute-start.7 = (bf16[192,384]{1,0:T(8,128)(2,1)S(1)}, bf16[192,384]{1,0:T(8,128)(2,1)S(1)}, u32[]{:S(2)}, u32[]{:S(2)}) collective-permute-start(bf16[192,384]{1,0:T(8,128)(2,1)S(1)} %pad_maximum_fusion.3.refs_0_), channel_id=1, source_target_pairs={{0,6},{1,3},{2,0},{3,5},{4,2},{5,7},{6,4},{7,1},{8,14},{9,11},{10,... | collective-permute-start | bytes 442376 | tf_op jit(solution)/shard_map/ppermute | solution.py:454
  16.7 9.5 %collective-permute-start.6 = (bf16[192,384]{1,0:T(8,128)(2,1)S(1)}, bf16[192,384]{1,0:T(8,128)(2,1)S(1)}, u32[]{:S(2)}, u32[]{:S(2)}) collective-permute-start(bf16[192,384]{1,0:T(8,128)(2,1)S(1)} %pad_maximum_fusion.3.refs_0_), channel_id=1, source_target_pairs={{0,7},{1,2},{2,1},{3,4},{4,3},{5,6},{6,5},{7,0},{8,15},{9,10},{10,... | collective-permute-start | bytes 442376 | tf_op jit(solution)/shard_map/ppermute | solution.py:454
  26.2 15.5 %collective-permute-start.8 = (bf16[320,640]{1,0:T(8,128)(2,1)S(1)}, bf16[320,640]{1,0:T(8,128)(2,1)S(1)}, u32[]{:S(2)}, u32[]{:S(2)}) collective-permute-start(bf16[320,640]{1,0:T(8,128)(2,1)S(1)} %pad_maximum_fusion.2), channel_id=1, source_target_pairs={{0,1},{1,0},{2,3},{3,2},{4,5},{5,4},{6,7},{7,6},{8,24},{9,25},{10,... | collective-permute-start | bytes 1228808 | tf_op jit(solution)/shard_map/ppermute | solution.py:454
  29.6 8.5 %collective-permute-start.9 = (bf16[192,384]{1,0:T(8,128)(2,1)S(1)}, bf16[192,384]{1,0:T(8,128)(2,1)S(1)}, u32[]{:S(2)}, u32[]{:S(2)}) collective-permute-start(bf16[192,384]{1,0:T(8,128)(2,1)S(1)} %pad_maximum_fusion.3.refs_0_), channel_id=1, source_target_pairs={{0,1},{1,0},{2,3},{3,2},{4,5},{5,4},{6,7},{7,6},{8,9},{9,8},{10,11... | collective-permute-start | bytes 442376 | tf_op jit(solution)/shard_map/ppermute | solution.py:454
  29.7 12.0 %collective-permute-start.10 = (bf16[480,256]{1,0:T(8,128)(2,1)}, bf16[480,256]{1,0:T(8,128)(2,1)S(1)}, u32[]{:S(2)}, u32[]{:S(2)}) collective-permute-start(bf16[480,256]{1,0:T(8,128)(2,1)} %get-tuple-element.32.refs_1_), channel_id=1, source_target_pairs={{0,2},{1,3},{2,4},{3,5},{4,6},{5,7},{6,0},{7,1},{8,10},{9,11},{10,... | collective-permute-start | bytes 737288 | tf_op jit(solution)/shard_map/ppermute | solution.py:454
  41.6 1.2 %copy-start.1 = (bf16[480,256]{1,0:T(8,128)(2,1)S(1)}, bf16[480,256]{1,0:T(8,128)(2,1)}, u32[]{:S(2)}) copy-start(bf16[480,256]{1,0:T(8,128)(2,1)} %get-tuple-element.32.refs_1_) | copy-start | bytes 737284
  41.8 19.1 %collective-permute-start.11 = (bf16[640,640]{1,0:T(8,128)(2,1)S(1)}, bf16[640,640]{1,0:T(8,128)(2,1)S(1)}, u32[]{:S(2)}, u32[]{:S(2)}) collective-permute-start(bf16[640,640]{1,0:T(8,128)(2,1)S(1)} %pad_maximum_fusion.1), channel_id=1, source_target_pairs={{0,16},{1,17},{2,18},{3,19},{4,20},{5,21},{6,22},{7,23},{8,9},{9,8... | collective-permute-start | bytes 2457608 | tf_op jit(solution)/shard_map/ppermute | solution.py:454
  42.9 7.6 %collective-permute-start.13 = (bf16[480,256]{1,0:T(8,128)(2,1)S(1)}, bf16[480,256]{1,0:T(8,128)(2,1)S(1)}, u32[]{:S(2)}, u32[]{:S(2)}) collective-permute-start(bf16[480,256]{1,0:T(8,128)(2,1)S(1)} %copy-done.1), channel_id=1, source_target_pairs={{0,6},{1,7},{2,0},{3,1},{4,2},{5,3},{6,4},{7,5},{8,14},{9,15},{10,... | collective-permute-start | bytes 737288 | tf_op jit(solution)/shard_map/ppermute | solution.py:454
  44.2 12.4 %collective-permute-start.12 = (bf16[480,256]{1,0:T(8,128)(2,1)S(1)}, bf16[480,256]{1,0:T(8,128)(2,1)S(1)}, u32[]{:S(2)}, u32[]{:S(2)}) collective-permute-start(bf16[480,256]{1,0:T(8,128)(2,1)S(1)} %copy-done.1), channel_id=1, source_target_pairs={{0,4},{1,5},{2,6},{3,7},{4,0},{5,1},{6,2},{7,3},{8,12},{9,13},{10,... | collective-permute-start | bytes 737288 | tf_op jit(solution)/shard_map/ppermute | solution.py:454
  59.2 1.6 %collective-permute-start.14 = (bf16[4,96,320]{2,1,0:T(8,128)(2,1)S(1)}, bf16[4,96,320]{2,1,0:T(8,128)(2,1)S(1)}, u32[]{:S(2)}, u32[]{:S(2)}) collective-permute-start(bf16[4,96,320]{2,1,0:T(8,128)(2,1)S(1)} %get-tuple-element.35), channel_id=1, source_target_pairs={{0,8},{1,9},{2,10},{3,11},{4,12},{5,13},{6,14},{7,15},{8,0},{9,1},... | collective-permute-start | bytes 737288 | tf_op jit(solution)/shard_map/ppermute | solution.py:454
  61.0 3.7 %collective-permute-start.15 = (bf16[1280,640]{1,0:T(8,128)(2,1)S(1)}, bf16[1280,640]{1,0:T(8,128)(2,1)S(1)}, u32[]{:S(2)}, u32[]{:S(2)}) collective-permute-start(bf16[1280,640]{1,0:T(8,128)(2,1)S(1)} %pad_maximum_fusion.refs_0_), channel_id=1, source_target_pairs={{0,8},{1,9},{2,10},{3,11},{4,12},{5,13},{6,14},{7,15},{8,0},{9,1},... | collective-permute-start | bytes 4915208 | tf_op jit(solution)/shard_map/ppermute | solution.py:454
  61.2 4.7 %collective-permute-start.16 = (bf16[96,320]{1,0:T(8,128)(2,1)S(1)}, bf16[96,320]{1,0:T(8,128)(2,1)S(1)}, u32[]{:S(2)}, u32[]{:S(2)}) collective-permute-start(bf16[96,320]{1,0:T(8,128)(2,1)S(1)} %get-tuple-element.40), channel_id=1, source_target_pairs={{0,1},{1,0},{2,3},{3,2},{4,5},{5,4},{6,7},{7,6},{8,9},{9,8},{10,11... | collective-permute-start | bytes 184328 | tf_op jit(solution)/shard_map/ppermute | solution.py:454
  62.3 5.9 %collective-permute-start.17 = (bf16[96,320]{1,0:T(8,128)(2,1)S(1)}, bf16[96,320]{1,0:T(8,128)(2,1)S(1)}, u32[]{:S(2)}, u32[]{:S(2)}) collective-permute-start(bf16[96,320]{1,0:T(8,128)(2,1)S(1)} %get-tuple-element.41), channel_id=1, source_target_pairs={{0,16},{1,17},{2,18},{3,19},{4,20},{5,21},{6,22},{7,23},{8,24},{9,... | collective-permute-start | bytes 184328 | tf_op jit(solution)/shard_map/ppermute | solution.py:454
  62.5 5.7 %copy-start = (bf16[6,2,8,640]{3,2,1,0:T(8,128)(2,1)S(1)}, bf16[6,2,8,640]{3,2,1,0:T(8,128)(2,1)}, u32[]{:S(2)}) copy-start(bf16[6,2,8,640]{3,2,1,0:T(8,128)(2,1)} %refs_0_.3) | copy-start | bytes 368644
  62.5 5.7 %copy-start.3 = (f32[1280]{0:T(1024)S(1)}, f32[1280]{0:T(1024)}, u32[]{:S(2)}) copy-start(f32[1280]{0:T(1024)} %refs_1_.2) | copy-start | bytes 15364
  62.5 5.7 %collective-permute-start.18 = (bf16[96,320]{1,0:T(8,128)(2,1)S(1)}, bf16[96,320]{1,0:T(8,128)(2,1)S(1)}, u32[]{:S(2)}, u32[]{:S(2)}) collective-permute-start(bf16[96,320]{1,0:T(8,128)(2,1)S(1)} %get-tuple-element.42), channel_id=1, source_target_pairs={{0,17},{1,16},{2,19},{3,18},{4,21},{5,20},{6,23},{7,22},{8,25},{9,... | collective-permute-start | bytes 184328 | tf_op jit(solution)/shard_map/ppermute | solution.py:454

commit v3 on v2

--- a/solution.py
+++ b/solution.py
@@ -51,7 +51,8 @@
         self.kpad = -(-self.depth // 128) * 128
         self.group = 3
         self.mix_rows = (self.basis // 3) * self.depth
-        self.mix_lanes = -(-self.group * self.out // 128) * 128
+        self.mix_lanes = 256
+        self.fold = 2 * self.mix_rows // 5
         self.mlp_lanes = 8 * self.out
         self.total = self.cycles * lats
         self.window = 4 * self.cells
@@ -60,7 +61,7 @@
     def fits(self):
         return (
             self.lats == 4
-            and self.lons % 2 == 0
+            and self.zs == 4
             and self.cells == 8
             and self.members == 2
             and self.slots * self.window == 128
@@ -71,9 +72,22 @@
             and self.depth == self.lift
             and self.down_rows == 4 * self.out
             and self.out % 16 == 0
-            and self.mlp_lanes % 128 == 0
+            and self.mlp_lanes == 5 * 128
+            and 3 * self.out <= self.mix_lanes
+            and self.fold % 32 == 0
+            and 5 * self.fold == 2 * self.mix_rows
             and self.body % 16 == 0
         )
+
+
+def folds(plan):
+    p = plan
+    places = []
+    for c in range(2):
+        for h in range(2):
+            places.append((0, (2 * c + h) * 128, h * p.fold, c * 128, p.fold))
+        places.append((c * (p.fold // 2), 512, 2 * p.fold, c * 128, p.fold // 2))
+    return places
 
 
 def place():
@@ -143,17 +157,21 @@
     )(rows, cols, latent, gain, filters)
 
 
-def pack_kernel(plan, mix, up, down, mlp_pack, mix_pack):
+def pack_kernel(plan, mix, up, down, mlp_pack, mix_pack, block):
     p = plan
     for q in range(p.lift // p.out):
         mlp_pack[:, q * p.depth : (q + 1) * p.depth] = up[q * p.out : (q + 1) * p.out, :]
     mlp_pack[:, 2 * p.depth :] = down[...]
     for k in range(p.basis):
         u, v = k // p.group, k % p.group
-        mix_pack[u * p.depth : (u + 1) * p.depth, v * p.out : (v + 1) * p.out] = mix[k]
+        block[u * p.depth : (u + 1) * p.depth, v * p.out : (v + 1) * p.out] = mix[k]
     used = p.group * p.out
     if p.mix_lanes > used:
-        mix_pack[:, used:] = jnp.zeros((p.mix_rows, p.mix_lanes - used), BF)
+        block[:, used:] = jnp.zeros((p.mix_rows, p.mix_lanes - used), BF)
+    for row, lane, at, column, count in folds(p):
+        mix_pack[row : row + count, lane : lane + 128] = block[
+            at : at + count, column : column + 128
+        ]
 
 
 def pack_weights(plan, mix, up, down):
@@ -162,16 +180,21 @@
         lambda *refs: pack_kernel(p, *refs),
         out_shape=[
             shape_of((p.out, p.mlp_lanes), BF),
-            shape_of((p.mix_rows, p.mix_lanes), BF),
+            shape_of((p.fold, p.mlp_lanes), BF),
         ],
         in_specs=whole(3),
         out_specs=whole(2),
+        scratch_shapes=[pltpu.VMEM((p.mix_rows, p.mix_lanes), BF)],
         compiler_params=params(60),
         name="pack_weights",
     )(mix, up, down)
 
 
-def contract_kernel(plan, own, pair, near, far, *rest):
+def sources(z):
+    return z, z ^ 3, z ^ 1, z ^ 2
+
+
+def contract_kernel(plan, own, far, both, *rest):
     p = plan
     pieces = rest[: p.lats]
     contracted, grid, taps, numbers, table, done = rest[p.lats :]
@@ -197,10 +220,12 @@
         band = lax.rem(a - s + p.lats, p.lats)
         lo = s * p.body
 
-        def read(ref):
-            return ref[lo : lo + p.body, 0 : p.lanes].astype(F32)
-
-        mine, other, first, second = read(own), read(pair), read(near), read(far)
+        def read(ref, start=0):
+            at = start + lo
+            return ref[at : at + p.body, 0 : p.lanes].astype(F32)
+
+        mine, other = read(own), read(both)
+        first, second = read(both, p.lats * p.body), read(far)
         blocks = (
             jnp.where(even, first, second),
             jnp.where(even, mine, other),
@@ -257,13 +282,13 @@
                     ]
 
 
-def contract(plan, own, pair, near, far, pieces):
+def contract(plan, own, far, both, pieces):
     p = plan
     lines = 8 * p.lats * p.groups
     return pl.pallas_call(
         lambda *refs: contract_kernel(p, *refs),
         out_shape=shape_of((p.total * p.members * p.double, p.basis * p.kpad), BF),
-        in_specs=whole(4 + p.lats),
+        in_specs=whole(3 + p.lats),
         out_specs=pl.BlockSpec(memory_space=pltpu.VMEM),
         scratch_shapes=[
             pltpu.VMEM((p.total + 2 * HREACH, p.window, p.members * p.kpad), BF),
@@ -274,21 +299,25 @@
         ],
         compiler_params=params(),
         name="contract",
-    )(own, pair, near, far, *pieces)
+    )(own, far, both, *pieces)
 
 
 def mix_kernel(plan, contracted, *rest):
     p = plan
-    packs = rest[: p.zs]
-    keep, send, slots, mixing = rest[p.zs :]
+    packs = rest[:4]
+    keep, send, slots, mixing = rest[4:]
     a, z, x = place()
     if p.kpad > p.depth:
         for k in range(p.basis):
             mixing[k * p.kpad + p.depth : (k + 1) * p.kpad, :] = jnp.zeros(
                 (p.kpad - p.depth, p.zs * p.out), BF
             )
-    for s in range(p.zs):
-        slots[lax.rem(z - s + p.zs, p.zs)] = packs[s][...]
+    for ref, source in zip(packs, sources(z)):
+        top = ref.shape[0] - p.fold
+        for row, lane, at, column, count in folds(p):
+            slots[source, at : at + count, column : column + 128] = ref[
+                top + row : top + row + count, lane : lane + 128
+            ]
     for b in range(p.zs):
         for k in range(p.basis):
             u, v = k // p.group, k % p.group
@@ -324,7 +353,7 @@
             shape_of((2 * p.ys, p.half, out), F32),
             shape_of((2 * p.ys, p.half, out), BF),
         ],
-        in_specs=whole(1 + p.zs),
+        in_specs=whole(5),
         out_specs=whole(2),
         scratch_shapes=[
             pltpu.VMEM((p.zs, p.mix_rows, p.mix_lanes), BF),
@@ -368,8 +397,8 @@
             dx = jnp.where(c == 0, low, high)
             dy = jnp.where(c == 0, high, low)
             lat = 2 * ((a // 2) ^ dy) + c
-            for s in range(p.zs):
-                lon = 2 * lax.rem(z - s + p.zs, p.zs) + (x ^ dx)
+            for s, source in enumerate(sources(z)):
+                lon = 2 * source + (x ^ dx)
                 index = step * p.zs + s
                 slots[lat * p.lons + lon] = stack[index * p.out : (index + 1) * p.out, :]
     for a in range(p.lats):
@@ -484,34 +513,39 @@
     mlp_pack, mix_pack = pack_weights(
         p, mix_weight, after(up_weight, msgs[0]), down_weight.T
     )
-    shares = [mlp_pack]
-    for s in range(1, p.zs):
-        shares.append(move(mlp_pack, lambda i, j, s=s: (i, j + 2 * s)))
+
+    def mirror(i, j):
+        return i, 2 * (p.zs - 1) - 2 * (j // 2) + j % 2
+
+    def beside(i, j):
+        return i, j ^ 2
+
+    turned = move(mix_pack, mirror)
+    last = move(turned, beside)
+
     own = jnp.concatenate([piece[: p.body] for piece in pieces], axis=0)
-    pair = move(own, lambda i, j: (i, j ^ 1))
-    near = move(own, lambda i, j: (i, j + 1 if j % 2 else j - 1))
     far = move(own, lambda i, j: (i, j + 2 if j % 2 else j - 2))
-
-    mix_pack = after(mix_pack, own)
-    packs = [mix_pack]
-    for s in range(1, p.zs):
-        packs.append(move(mix_pack, lambda i, j, s=s: (i, j + 2 * s)))
-
-    contracted = contract(p, own, pair, near, far, pieces)
-    share = after(jnp.concatenate(shares, axis=0), near, far)
+    both = move(jnp.concatenate([own, far], axis=0), lambda i, j: (i, j ^ 1))
+    contracted = contract(p, own, far, both, pieces)
+
+    near = jnp.concatenate([mlp_pack, move(mlp_pack, mirror), mix_pack], axis=0)
+    next_to = move(after(near, far), beside)
+    packs = [mix_pack, turned, next_to, last]
+    share = jnp.concatenate([near[: 2 * p.out], next_to[: 2 * p.out]], axis=0)
+    share = after(share, both, turned)
     crossed = move(share, lambda i, j: (i + 2, j) if i % 2 else (i, j ^ 1))
-    share = after(jnp.concatenate([share, crossed], axis=0), contracted, packs[1])
+    share = after(jnp.concatenate([share, crossed], axis=0), last, contracted)
     crossed = move(share, lambda i, j: (i, j ^ 1) if i % 2 else (i + 2, j))
     keep, send = mix_basis(p, contracted, packs)
     arrived = move(send, lambda i, j: (i ^ 1, j))
     mine, outgoing = add_cores(keep, arrived)
-    share = after(jnp.concatenate([share, crossed], axis=0), mine)
-    up, down = unpack(p, share, move(share, lambda i, j: (i ^ 1, j)))
     incoming = []
     for index, value in enumerate(outgoing):
         t, w = (index + 1) // 2, (index + 1) % 2
         incoming.append(move(value, lambda i, j, t=t, w=w: (i + 2 * t, j ^ w)))
 
+    share = after(jnp.concatenate([share, crossed], axis=0), incoming[0])
+    up, down = unpack(p, share, move(share, lambda i, j: (i ^ 1, j)))
     return mlp(p, latent, up_bias, up, down, mine, incoming)
 
 

time: 70.1 us -> 65.9 us (0.940)
  waiting for transfers between devices: 30 us -> 26.9 us
  starting transfers between devices: 25 us -> 23.5 us
    ppermute x19 -> x16, waiting for transfers between devices: 30 us -> 26.9 us  [move(): return lax.ppermute(value, AXES, pairs)]
    ppermute x19 -> x16, starting transfers between devices: 25 us -> 23.5 us  [move(): return lax.ppermute(value, AXES, pairs)]
    unnamed x8 -> x14, local copies, waits for them, and re-layouts: 0.02 us -> 0.84 us
    slice x4 -> x1, local copies, waits for them, and re-layouts: 0.79 us -> 0.02 us  [shards_fast(): share = jnp.concatenate([near[:2 * p.out], next_to[:2 * p.out]], axis=0)]
  transfers between devices with their start and end apart: 19 -> 16, of which waited for: 8 -> 10; matrix products, arithmetic and copies ran while one was open for 3% -> 3% of each run, Pallas kernels for 13% -> 14%
where the time goes in v3:
time: 65.9 us; the launch traced here: 65.7 us
  waiting for transfers between devices  26.9 us (41%)
  starting transfers between devices  23.5 us (36%)
  Pallas kernels  12.9 us (20%)
  other arithmetic  1.33 us (2%)
  local copies, waits for them, and re-layouts  0.88 us (1%)
    ppermute x16, waiting for transfers between devices, move(): return lax.ppermute(value, AXES, pairs)  26.9 us
    ppermute x16, starting transfers between devices, move(): return lax.ppermute(value, AXES, pairs)  23.5 us
    pallas_call x1, Pallas kernels, contract(): pl.pallas_call(lambda *refs: contract_kernel(p, *refs), out_shape=shape_o...  3.47 us
    pallas_call x1, Pallas kernels, mix_basis(): pl.pallas_call(lambda *refs: mix_kernel(p, *refs), out_shape=[shape_of((2...  2.59 us
    pallas_call x1, Pallas kernels, pack_weights(): pl.pallas_call(lambda *refs: pack_kernel(p, *refs), out_shape=[shape_of((...  2.01 us
    pallas_call x1, Pallas kernels, normal_pieces(): pl.pallas_call(lambda *refs: normal_kernel(p, *refs), out_shape=[shape_of...  1.93 us
    pallas_call x1, Pallas kernels, mlp(): pl.pallas_call(lambda *refs: mlp_kernel(p, *refs), out_shape=shape_of(lat...  1.67 us
  transfers between devices with their start and end apart: 16, of which 10 were waited for; matrix products, arithmetic and copies ran while one was open for 3% of the time, Pallas kernels for 14%

profile of v3, /device:TPU:0, one launch (start us, length us, event | category | flops | bytes accessed | tf_op | source)
XLA Modules:
  0.0 65.7 jit_solution(3982937731383472118)
XLA Ops:
  0.0 1.9 %normalize.1 = (bf16[80,384]{1,0:T(8,128)(2,1)}, bf16[80,384]{1,0:T(8,128)(2,1)}, bf16[80,384]{1,0:T(8,128)(2,1)}, bf16[80,384]{1,0:T(8,128)(2,1)}) custom-call(s32[4,6]{1,0:T(4,128)} %bitcast.8, s32[4,6]{1,0:T(4,128)} %bitcast.9, bf16[6,2,8,640]{3,2,1,0:T(8,128)(2,1)} %refs_0_.3, f32[640]{0:T(1024)} %refs_3_.1, bf16[6,32,9]{2,1,0:T(8,128)(2,1)} %bitcast.7), custom_call_target="tpu_custom_call" | custom-call | tf_op jit(solution)/shard_map/normalize/pallas_call | solution.py:149
  1.9 0.5 collective-permute-start.1
  2.4 2.6 %collective-permute-start.2 = (bf16[80,384]{1,0:T(8,128)(2,1)}, bf16[80,384]{1,0:T(8,128)(2,1)S(1)}, u32[]{:S(2)}, u32[]{:S(2)}) collective-permute-start(bf16[80,384]{1,0:T(8,128)(2,1)} %get-tuple-element.29), channel_id=1, source_target_pairs={{0,16},{1,17},{2,18},{3,19},{4,20},{5,21},{6,22},{7,23},{8,24},{9,... | collective-permute-start | bytes 184328 | tf_op jit(solution)/shard_map/ppermute | solution.py:483
  5.0 1.4 %collective-permute-start.3 = (bf16[80,384]{1,0:T(8,128)(2,1)}, bf16[80,384]{1,0:T(8,128)(2,1)S(1)}, u32[]{:S(2)}, u32[]{:S(2)}) collective-permute-start(bf16[80,384]{1,0:T(8,128)(2,1)} %get-tuple-element.30), channel_id=1, source_target_pairs={{0,24},{1,25},{2,26},{3,27},{4,28},{5,29},{6,30},{7,31},{8,0},{9,1... | collective-permute-start | bytes 184328 | tf_op jit(solution)/shard_map/ppermute | solution.py:483
  6.4 2.0 %pack_weights.1 = (bf16[80,640]{1,0:T(8,128)(2,1)}, bf16[192,640]{1,0:T(8,128)(2,1)}) custom-call(bf16[9,160,80]{2,1,0:T(8,128)(2,1)} %refs_0_.2, bf16[160,160]{1,0:T(8,128)(2,1)} %refs_1_.1, bf16[80,320]{1,0:T(8,128)(2,1)} %bitcast.6), custom_call_target="tpu_custom_call" | custom-call | tf_op jit(solution)/shard_map/pack_weights/pallas_call | solution.py:179
  8.4 3.7 %collective-permute-start = (bf16[80,640]{1,0:T(8,128)(2,1)}, bf16[80,640]{1,0:T(8,128)(2,1)S(1)}, u32[]{:S(2)}, u32[]{:S(2)}) collective-permute-start(bf16[80,640]{1,0:T(8,128)(2,1)} %get-tuple-element.26), channel_id=1, source_target_pairs={{0,6},{1,7},{2,4},{3,5},{4,2},{5,3},{6,0},{7,1},{8,14},{9,15},{10,... | collective-permute-start | bytes 307208 | tf_op jit(solution)/shard_map/ppermute | solution.py:483
  12.0 0.8 %constant_dynamic-update-slice_fusion.4 = (bf16[384,384]{1,0:T(8,128)(2,1)S(1)}, bf16[48,384]{1,0:T(8,128)(2,1)S(1)}) fusion(bf16[80,384]{1,0:T(8,128)(2,1)} %get-tuple-element.24.refs_3_), kind=kLoop, calls=%fused_computation.9 | loop fusion | bytes 110592
  12.9 0.3 collective-permute-start.4
  13.2 3.0 %collective-permute-done = bf16[80,640]{1,0:T(8,128)(2,1)S(1)} collective-permute-done((bf16[80,640]{1,0:T(8,128)(2,1)}, bf16[80,640]{1,0:T(8,128)(2,1)S(1)}, u32[]{:S(2)}, u32[]{:S(2)}) %collective-permute-start) | collective-permute-done | bytes 102432 | tf_op jit(solution)/shard_map/ppermute | solution.py:483
  16.2 1.1 %pad_maximum_fusion.2 = bf16[352,640]{1,0:T(8,128)(2,1)S(1)} fusion(bf16[192,640]{1,0:T(8,128)(2,1)} %get-tuple-element.27.refs_1_, bf16[80,640]{1,0:T(8,128)(2,1)S(1)} %collective-permute-done, bf16[80,640]{1,0:T(8,128)(2,1)} %get-tuple-element.26), kind=kLoop, calls=%fused_computation.2 | loop fusion | flops 1351680 | bytes 901120 | tf_op jit(solution)/shard_map/concatenate | solution.py:531
  17.3 1.2 %collective-permute-done.4.refs_1_ = bf16[192,384]{1,0:T(8,128)(2,1)S(1)} collective-permute-done((bf16[192,384]{1,0:T(8,128)(2,1)S(1)}, bf16[192,384]{1,0:T(8,128)(2,1)S(1)}, u32[]{:S(2)}, u32[]{:S(2)}) %collective-permute-start.4) | collective-permute-done | bytes 147488 | tf_op jit(solution)/shard_map/ppermute | solution.py:483
  18.5 2.1 %collective-permute-start.5 = (bf16[352,640]{1,0:T(8,128)(2,1)S(1)}, bf16[352,640]{1,0:T(8,128)(2,1)S(1)}, u32[]{:S(2)}, u32[]{:S(2)}) collective-permute-start(bf16[352,640]{1,0:T(8,128)(2,1)S(1)} %pad_maximum_fusion.2), channel_id=1, source_target_pairs={{0,2},{1,3},{2,0},{3,1},{4,6},{5,7},{6,4},{7,5},{8,10},{9,11},{10,... | collective-permute-start | bytes 1351688 | tf_op jit(solution)/shard_map/ppermute | solution.py:483
  20.6 0.9 %collective-permute-start.6 = (bf16[384,384]{1,0:T(8,128)(2,1)S(1)}, bf16[384,384]{1,0:T(8,128)(2,1)S(1)}, u32[]{:S(2)}, u32[]{:S(2)}) collective-permute-start(bf16[384,384]{1,0:T(8,128)(2,1)S(1)} %constant_dynamic-update-slice_fusion), channel_id=1, source_target_pairs={{0,1},{1,0},{2,3},{3,2},{4,5},{5,4},{6,7},{7,6},{8,9},{9,8},{10,11... | collective-permute-start | bytes 884744 | tf_op jit(solution)/shard_map/ppermute | solution.py:483
  21.5 2.5 %collective-permute-start.7 = (bf16[192,640]{1,0:T(8,128)(2,1)S(1)}, bf16[192,640]{1,0:T(8,128)(2,1)S(1)}, u32[]{:S(2)}, u32[]{:S(2)}) collective-permute-start(bf16[192,640]{1,0:T(8,128)(2,1)S(1)} %copy-done), channel_id=1, source_target_pairs={{0,6},{1,7},{2,4},{3,5},{4,2},{5,3},{6,0},{7,1},{8,14},{9,15},{10,... | collective-permute-start | bytes 737288 | tf_op jit(solution)/shard_map/ppermute | solution.py:483
  24.0 8.1 %collective-permute-done.5.refs_3_ = bf16[352,640]{1,0:T(8,128)(2,1)S(1)} collective-permute-done((bf16[352,640]{1,0:T(8,128)(2,1)S(1)}, bf16[352,640]{1,0:T(8,128)(2,1)S(1)}, u32[]{:S(2)}, u32[]{:S(2)}) %collective-permute-start.5) | collective-permute-done | bytes 450592 | tf_op jit(solution)/shard_map/ppermute | solution.py:483
  32.2 3.7 %collective-permute-done.7.refs_2_ = bf16[192,640]{1,0:T(8,128)(2,1)S(1)} collective-permute-done((bf16[192,640]{1,0:T(8,128)(2,1)S(1)}, bf16[192,640]{1,0:T(8,128)(2,1)S(1)}, u32[]{:S(2)}, u32[]{:S(2)}) %collective-permute-start.7) | collective-permute-done | bytes 245792 | tf_op jit(solution)/shard_map/ppermute | solution.py:483
  35.9 2.0 %collective-permute-start.8 = (bf16[320,640]{1,0:T(8,128)(2,1)S(1)}, bf16[320,640]{1,0:T(8,128)(2,1)S(1)}, u32[]{:S(2)}, u32[]{:S(2)}) collective-permute-start(bf16[320,640]{1,0:T(8,128)(2,1)S(1)} %pad_maximum_fusion.3), channel_id=1, source_target_pairs={{0,1},{1,0},{2,3},{3,2},{4,5},{5,4},{6,7},{7,6},{8,24},{9,25},{10,... | collective-permute-start | bytes 1228808 | tf_op jit(solution)/shard_map/ppermute | solution.py:483
  38.0 3.5 %contract.1.refs_0_ = bf16[768,2304]{1,0:T(8,128)(2,1)S(1)} custom-call(bf16[192,384]{1,0:T(8,128)(2,1)S(1)} %pad_maximum_fusion.4.refs_0_, bf16[192,384]{1,0:T(8,128)(2,1)S(1)} %collective-permute-done.4.refs_1_, bf16[384,384]{1,0:T(8,128)(2,1)S(1)} %collective-permute-done.6.refs_2_, bf16[80,384]{1,0:T(8,128)(2,1)S(1)} %copy-done.2, ...), custom_call_target="tpu_custom_call" | custom-call | tf_op jit(solution)/shard_map/contract/pallas_call | solution.py:288
  41.4 2.4 %collective-permute-done.8 = bf16[320,640]{1,0:T(8,128)(2,1)S(1)} collective-permute-done((bf16[320,640]{1,0:T(8,128)(2,1)S(1)}, bf16[320,640]{1,0:T(8,128)(2,1)S(1)}, u32[]{:S(2)}, u32[]{:S(2)}) %collective-permute-start.8) | collective-permute-done | bytes 409632 | tf_op jit(solution)/shard_map/ppermute | solution.py:483
  44.0 0.2 collective-permute-done.9.refs_4_
  44.1 2.0 %collective-permute-start.10 = (bf16[640,640]{1,0:T(8,128)(2,1)S(1)}, bf16[640,640]{1,0:T(8,128)(2,1)S(1)}, u32[]{:S(2)}, u32[]{:S(2)}) collective-permute-start(bf16[640,640]{1,0:T(8,128)(2,1)S(1)} %pad_maximum_fusion.1), channel_id=1, source_target_pairs={{0,16},{1,17},{2,18},{3,19},{4,20},{5,21},{6,22},{7,23},{8,9},{9,8... | collective-permute-start | bytes 2457608 | tf_op jit(solution)/shard_map/ppermute | solution.py:483
  46.1 2.6 %mix_basis.1 = (f32[4,96,320]{2,1,0:T(8,128)S(1)}, bf16[4,96,320]{2,1,0:T(8,128)(2,1)S(1)}) custom-call(bf16[768,2304]{1,0:T(8,128)(2,1)S(1)} %contract.1.refs_0_, bf16[192,640]{1,0:T(8,128)(2,1)S(1)} %copy-done, bf16[192,640]{1,0:T(8,128)(2,1)S(1)} %collective-permute-done.7.refs_2_, bf16[352,640]{1,0:T(8,128)(2,1)S(1)} %collective-permute-done.5.refs_3_, ...), custom_call_target="tpu_custom_call" | custom-call | tf_op jit(solution)/shard_map/mix_basis/pallas_call | solution.py:350
  48.8 1.6 %collective-permute-done.11.arrived = bf16[4,96,320]{2,1,0:T(8,128)(2,1)S(1)} collective-permute-done((bf16[4,96,320]{2,1,0:T(8,128)(2,1)S(1)}, bf16[4,96,320]{2,1,0:T(8,128)(2,1)S(1)}, u32[]{:S(2)}, u32[]{:S(2)}) %collective-permute-start.11) | collective-permute-done | bytes 245792 | tf_op jit(solution)/shard_map/ppermute | solution.py:483
  50.4 2.0 %collective-permute-start.12 = (bf16[96,320]{1,0:T(8,128)(2,1)S(1)}, bf16[96,320]{1,0:T(8,128)(2,1)S(1)}, u32[]{:S(2)}, u32[]{:S(2)}) collective-permute-start(bf16[96,320]{1,0:T(8,128)(2,1)S(1)} %get-tuple-element.36), channel_id=1, source_target_pairs={{0,1},{1,0},{2,3},{3,2},{4,5},{5,4},{6,7},{7,6},{8,9},{9,8},{10,11... | collective-permute-start | bytes 184328 | tf_op jit(solution)/shard_map/ppermute | solution.py:483
  52.4 4.1 %collective-permute-done.10 = bf16[640,640]{1,0:T(8,128)(2,1)S(1)} collective-permute-done((bf16[640,640]{1,0:T(8,128)(2,1)S(1)}, bf16[640,640]{1,0:T(8,128)(2,1)S(1)}, u32[]{:S(2)}, u32[]{:S(2)}) %collective-permute-start.10) | collective-permute-done | bytes 819232 | tf_op jit(solution)/shard_map/ppermute | solution.py:483
  56.5 0.1 pad_maximum_fusion.refs_0_
  56.7 2.0 %collective-permute-start.14 = (bf16[96,320]{1,0:T(8,128)(2,1)S(1)}, bf16[96,320]{1,0:T(8,128)(2,1)S(1)}, u32[]{:S(2)}, u32[]{:S(2)}) collective-permute-start(bf16[96,320]{1,0:T(8,128)(2,1)S(1)} %get-tuple-element.41), channel_id=1, source_target_pairs={{0,16},{1,17},{2,18},{3,19},{4,20},{5,21},{6,22},{7,23},{8,24},{9,... | collective-permute-start | bytes 184328 | tf_op jit(solution)/shard_map/ppermute | solution.py:483
  58.8 1.4 %collective-permute-start.15 = (bf16[96,320]{1,0:T(8,128)(2,1)S(1)}, bf16[96,320]{1,0:T(8,128)(2,1)S(1)}, u32[]{:S(2)}, u32[]{:S(2)}) collective-permute-start(bf16[96,320]{1,0:T(8,128)(2,1)S(1)} %get-tuple-element.42), channel_id=1, source_target_pairs={{0,17},{1,16},{2,19},{3,18},{4,21},{5,20},{6,23},{7,22},{8,25},{9,... | collective-permute-start | bytes 184328 | tf_op jit(solution)/shard_map/ppermute | solution.py:483
  60.2 1.2 %mlp_weights.1 = (bf16[640,1280]{1,0:T(8,128)(2,1)S(1)}, bf16[640,1280]{1,0:T(8,128)(2,1)S(1)}) custom-call(bf16[1280,640]{1,0:T(8,128)(2,1)S(1)} %pad_maximum_fusion.refs_0_, bf16[1280,640]{1,0:T(8,128)(2,1)S(1)} %collective-permute-done.13.refs_1_), custom_call_target="tpu_custom_call" | custom-call | tf_op jit(solution)/shard_map/mlp_weights/pallas_call | solution.py:419
  61.4 0.2 collective-permute-done.14.refs_6_
  61.6 2.4 %collective-permute-done.15.refs_7_ = bf16[96,320]{1,0:T(8,128)(2,1)S(1)} collective-permute-done((bf16[96,320]{1,0:T(8,128)(2,1)S(1)}, bf16[96,320]{1,0:T(8,128)(2,1)S(1)}, u32[]{:S(2)}, u32[]{:S(2)}) %collective-permute-start.15) | collective-permute-done | bytes 61472 | tf_op jit(solution)/shard_map/ppermute | solution.py:483
  64.0 1.7 %sum_mlp.1 = bf16[6,2,8,640]{3,2,1,0:T(8,128)(2,1)} custom-call(bf16[6,2,8,640]{3,2,1,0:T(8,128)(2,1)S(1)} %copy-done.1, f32[1280]{0:T(1024)S(1)} %copy-done.3, bf16[640,1280]{1,0:T(8,128)(2,1)S(1)} %get-tuple-element.38.refs_2_, bf16[640,1280]{1,0:T(8,128)(2,1)S(1)} %get-tuple-element.39.refs_3_, f32[96,320]{1,0:T(8,128)S(1)} %get-tuple-element.40.refs_4_, ...), custom_call_target="tpu_custom_call" | custom-call | tf_op jit(solution)/shard_map/sum_mlp/pallas_call | solution.py:463
  (28 shorter events, 0.5 us)
Async XLA Ops:
  1.9 10.9 %collective-permute-start.1 = (bf16[80,384]{1,0:T(8,128)(2,1)}, bf16[80,384]{1,0:T(8,128)(2,1)S(1)}, u32[]{:S(2)}, u32[]{:S(2)}) collective-permute-start(bf16[80,384]{1,0:T(8,128)(2,1)} %get-tuple-element.28), channel_id=1, source_target_pairs={{0,8},{1,9},{2,10},{3,11},{4,12},{5,13},{6,14},{7,15},{8,16},{9,17... | collective-permute-start | bytes 184328 | tf_op jit(solution)/shard_map/ppermute | solution.py:483
  2.4 10.5 %collective-permute-start.2 = (bf16[80,384]{1,0:T(8,128)(2,1)}, bf16[80,384]{1,0:T(8,128)(2,1)S(1)}, u32[]{:S(2)}, u32[]{:S(2)}) collective-permute-start(bf16[80,384]{1,0:T(8,128)(2,1)} %get-tuple-element.29), channel_id=1, source_target_pairs={{0,16},{1,17},{2,18},{3,19},{4,20},{5,21},{6,22},{7,23},{8,24},{9,... | collective-permute-start | bytes 184328 | tf_op jit(solution)/shard_map/ppermute | solution.py:483
  5.0 7.9 %collective-permute-start.3 = (bf16[80,384]{1,0:T(8,128)(2,1)}, bf16[80,384]{1,0:T(8,128)(2,1)S(1)}, u32[]{:S(2)}, u32[]{:S(2)}) collective-permute-start(bf16[80,384]{1,0:T(8,128)(2,1)} %get-tuple-element.30), channel_id=1, source_target_pairs={{0,24},{1,25},{2,26},{3,27},{4,28},{5,29},{6,30},{7,31},{8,0},{9,1... | collective-permute-start | bytes 184328 | tf_op jit(solution)/shard_map/ppermute | solution.py:483
  8.4 13.1 %copy-start = (bf16[192,640]{1,0:T(8,128)(2,1)S(1)}, bf16[192,640]{1,0:T(8,128)(2,1)}, u32[]{:S(2)}) copy-start(bf16[192,640]{1,0:T(8,128)(2,1)} %get-tuple-element.27.refs_1_) | copy-start | bytes 737284
  8.4 23.8 %copy-start.4 = (bf16[80,640]{1,0:T(8,128)(2,1)S(1)}, bf16[80,640]{1,0:T(8,128)(2,1)}, u32[]{:S(2)}) copy-start(bf16[80,640]{1,0:T(8,128)(2,1)} %get-tuple-element.26) | copy-start | bytes 307204
  8.4 29.6 %copy-start.2 = (bf16[80,384]{1,0:T(8,128)(2,1)S(1)}, bf16[80,384]{1,0:T(8,128)(2,1)}, u32[]{:S(2)}) copy-start(bf16[80,384]{1,0:T(8,128)(2,1)} %get-tuple-element.24.refs_3_) | copy-start | bytes 184324
  8.4 7.8 %collective-permute-start = (bf16[80,640]{1,0:T(8,128)(2,1)}, bf16[80,640]{1,0:T(8,128)(2,1)S(1)}, u32[]{:S(2)}, u32[]{:S(2)}) collective-permute-start(bf16[80,640]{1,0:T(8,128)(2,1)} %get-tuple-element.26), channel_id=1, source_target_pairs={{0,6},{1,7},{2,4},{3,5},{4,2},{5,3},{6,0},{7,1},{8,14},{9,15},{10,... | collective-permute-start | bytes 307208 | tf_op jit(solution)/shard_map/ppermute | solution.py:483
  12.9 5.5 %collective-permute-start.4 = (bf16[192,384]{1,0:T(8,128)(2,1)S(1)}, bf16[192,384]{1,0:T(8,128)(2,1)S(1)}, u32[]{:S(2)}, u32[]{:S(2)}) collective-permute-start(bf16[192,384]{1,0:T(8,128)(2,1)S(1)} %pad_maximum_fusion.4.refs_0_), channel_id=1, source_target_pairs={{0,6},{1,3},{2,0},{3,5},{4,2},{5,7},{6,4},{7,1},{8,14},{9,11},{10,... | collective-permute-start | bytes 442376 | tf_op jit(solution)/shard_map/ppermute | solution.py:483
  18.5 13.7 %collective-permute-start.5 = (bf16[352,640]{1,0:T(8,128)(2,1)S(1)}, bf16[352,640]{1,0:T(8,128)(2,1)S(1)}, u32[]{:S(2)}, u32[]{:S(2)}) collective-permute-start(bf16[352,640]{1,0:T(8,128)(2,1)S(1)} %pad_maximum_fusion.2), channel_id=1, source_target_pairs={{0,2},{1,3},{2,0},{3,1},{4,6},{5,7},{6,4},{7,5},{8,10},{9,11},{10,... | collective-permute-start | bytes 1351688 | tf_op jit(solution)/shard_map/ppermute | solution.py:483
  20.6 15.3 %collective-permute-start.6 = (bf16[384,384]{1,0:T(8,128)(2,1)S(1)}, bf16[384,384]{1,0:T(8,128)(2,1)S(1)}, u32[]{:S(2)}, u32[]{:S(2)}) collective-permute-start(bf16[384,384]{1,0:T(8,128)(2,1)S(1)} %constant_dynamic-update-slice_fusion), channel_id=1, source_target_pairs={{0,1},{1,0},{2,3},{3,2},{4,5},{5,4},{6,7},{7,6},{8,9},{9,8},{10,11... | collective-permute-start | bytes 884744 | tf_op jit(solution)/shard_map/ppermute | solution.py:483
  21.5 14.4 %collective-permute-start.7 = (bf16[192,640]{1,0:T(8,128)(2,1)S(1)}, bf16[192,640]{1,0:T(8,128)(2,1)S(1)}, u32[]{:S(2)}, u32[]{:S(2)}) collective-permute-start(bf16[192,640]{1,0:T(8,128)(2,1)S(1)} %copy-done), channel_id=1, source_target_pairs={{0,6},{1,7},{2,4},{3,5},{4,2},{5,3},{6,0},{7,1},{8,14},{9,15},{10,... | collective-permute-start | bytes 737288 | tf_op jit(solution)/shard_map/ppermute | solution.py:483
  35.9 8.0 %collective-permute-start.8 = (bf16[320,640]{1,0:T(8,128)(2,1)S(1)}, bf16[320,640]{1,0:T(8,128)(2,1)S(1)}, u32[]{:S(2)}, u32[]{:S(2)}) collective-permute-start(bf16[320,640]{1,0:T(8,128)(2,1)S(1)} %pad_maximum_fusion.3), channel_id=1, source_target_pairs={{0,1},{1,0},{2,3},{3,2},{4,5},{5,4},{6,7},{7,6},{8,24},{9,25},{10,... | collective-permute-start | bytes 1228808 | tf_op jit(solution)/shard_map/ppermute | solution.py:483
  37.9 6.2 %collective-permute-start.9 = (bf16[192,640]{1,0:T(8,128)(2,1)S(1)}, bf16[192,640]{1,0:T(8,128)(2,1)S(1)}, u32[]{:S(2)}, u32[]{:S(2)}) collective-permute-start(bf16[192,640]{1,0:T(8,128)(2,1)S(1)} %collective-permute-done.7.refs_2_), channel_id=1, source_target_pairs={{0,2},{1,3},{2,0},{3,1},{4,6},{5,7},{6,4},{7,5},{8,10},{9,11},{10,... | collective-permute-start | bytes 737288 | tf_op jit(solution)/shard_map/ppermute | solution.py:483
  44.1 12.3 %collective-permute-start.10 = (bf16[640,640]{1,0:T(8,128)(2,1)S(1)}, bf16[640,640]{1,0:T(8,128)(2,1)S(1)}, u32[]{:S(2)}, u32[]{:S(2)}) collective-permute-start(bf16[640,640]{1,0:T(8,128)(2,1)S(1)} %pad_maximum_fusion.1), channel_id=1, source_target_pairs={{0,16},{1,17},{2,18},{3,19},{4,20},{5,21},{6,22},{7,23},{8,9},{9,8... | collective-permute-start | bytes 2457608 | tf_op jit(solution)/shard_map/ppermute | solution.py:483
  48.7 1.6 %collective-permute-start.11 = (bf16[4,96,320]{2,1,0:T(8,128)(2,1)S(1)}, bf16[4,96,320]{2,1,0:T(8,128)(2,1)S(1)}, u32[]{:S(2)}, u32[]{:S(2)}) collective-permute-start(bf16[4,96,320]{2,1,0:T(8,128)(2,1)S(1)} %get-tuple-element.35), channel_id=1, source_target_pairs={{0,8},{1,9},{2,10},{3,11},{4,12},{5,13},{6,14},{7,15},{8,0},{9,1},... | collective-permute-start | bytes 737288 | tf_op jit(solution)/shard_map/ppermute | solution.py:483
  50.4 6.2 %collective-permute-start.12 = (bf16[96,320]{1,0:T(8,128)(2,1)S(1)}, bf16[96,320]{1,0:T(8,128)(2,1)S(1)}, u32[]{:S(2)}, u32[]{:S(2)}) collective-permute-start(bf16[96,320]{1,0:T(8,128)(2,1)S(1)} %get-tuple-element.36), channel_id=1, source_target_pairs={{0,1},{1,0},{2,3},{3,2},{4,5},{5,4},{6,7},{7,6},{8,9},{9,8},{10,11... | collective-permute-start | bytes 184328 | tf_op jit(solution)/shard_map/ppermute | solution.py:483
  56.6 3.6 %collective-permute-start.13 = (bf16[1280,640]{1,0:T(8,128)(2,1)S(1)}, bf16[1280,640]{1,0:T(8,128)(2,1)S(1)}, u32[]{:S(2)}, u32[]{:S(2)}) collective-permute-start(bf16[1280,640]{1,0:T(8,128)(2,1)S(1)} %pad_maximum_fusion.refs_0_), channel_id=1, source_target_pairs={{0,8},{1,9},{2,10},{3,11},{4,12},{5,13},{6,14},{7,15},{8,0},{9,1},... | collective-permute-start | bytes 4915208 | tf_op jit(solution)/shard_map/ppermute | solution.py:483
  56.7 4.9 %collective-permute-start.14 = (bf16[96,320]{1,0:T(8,128)(2,1)S(1)}, bf16[96,320]{1,0:T(8,128)(2,1)S(1)}, u32[]{:S(2)}, u32[]{:S(2)}) collective-permute-start(bf16[96,320]{1,0:T(8,128)(2,1)S(1)} %get-tuple-element.41), channel_id=1, source_target_pairs={{0,16},{1,17},{2,18},{3,19},{4,20},{5,21},{6,22},{7,23},{8,24},{9,... | collective-permute-start | bytes 184328 | tf_op jit(solution)/shard_map/ppermute | solution.py:483
  58.8 5.3 %copy-start.1 = (bf16[6,2,8,640]{3,2,1,0:T(8,128)(2,1)S(1)}, bf16[6,2,8,640]{3,2,1,0:T(8,128)(2,1)}, u32[]{:S(2)}) copy-start(bf16[6,2,8,640]{3,2,1,0:T(8,128)(2,1)} %refs_0_.3) | copy-start | bytes 368644
  58.8 5.3 %copy-start.3 = (f32[1280]{0:T(1024)S(1)}, f32[1280]{0:T(1024)}, u32[]{:S(2)}) copy-start(f32[1280]{0:T(1024)} %refs_1_.2) | copy-start | bytes 15364
  58.8 5.3 %collective-permute-start.15 = (bf16[96,320]{1,0:T(8,128)(2,1)S(1)}, bf16[96,320]{1,0:T(8,128)(2,1)S(1)}, u32[]{:S(2)}, u32[]{:S(2)}) collective-permute-start(bf16[96,320]{1,0:T(8,128)(2,1)S(1)} %get-tuple-element.42), channel_id=1, source_target_pairs={{0,17},{1,16},{2,19},{3,18},{4,21},{5,20},{6,23},{7,22},{8,25},{9,... | collective-permute-start | bytes 184328 | tf_op jit(solution)/shard_map/ppermute | solution.py:483

commit v4 on v3

--- a/solution.py
+++ b/solution.py
@@ -532,9 +532,9 @@
     next_to = move(after(near, far), beside)
     packs = [mix_pack, turned, next_to, last]
     share = jnp.concatenate([near[: 2 * p.out], next_to[: 2 * p.out]], axis=0)
-    share = after(share, both, turned)
+    share = after(share, both)
     crossed = move(share, lambda i, j: (i + 2, j) if i % 2 else (i, j ^ 1))
-    share = after(jnp.concatenate([share, crossed], axis=0), last, contracted)
+    share = after(jnp.concatenate([share, crossed], axis=0), turned, contracted)
     crossed = move(share, lambda i, j: (i, j ^ 1) if i % 2 else (i + 2, j))
     keep, send = mix_basis(p, contracted, packs)
     arrived = move(send, lambda i, j: (i ^ 1, j))
@@ -544,7 +544,7 @@
         t, w = (index + 1) // 2, (index + 1) % 2
         incoming.append(move(value, lambda i, j, t=t, w=w: (i + 2 * t, j ^ w)))
 
-    share = after(jnp.concatenate([share, crossed], axis=0), incoming[0])
+    share = after(jnp.concatenate([share, crossed], axis=0), mine)
     up, down = unpack(p, share, move(share, lambda i, j: (i ^ 1, j)))
     return mlp(p, latent, up_bias, up, down, mine, incoming)
 

time: 65.9 us -> 63.5 us (0.964)
  waiting for transfers between devices: 26.9 us -> 24.4 us
    ppermute x16, waiting for transfers between devices: 26.9 us -> 24.4 us  [move(): return lax.ppermute(value, AXES, pairs)]
  transfers between devices with their start and end apart: 16 -> 16, of which waited for: 10 -> 8; matrix products, arithmetic and copies ran while one was open for 3% -> 3% of each run, Pallas kernels for 14% -> 15%
where the time goes in v4:
time: 63.5 us; the launch traced here: 63.3 us
  waiting for transfers between devices  24.4 us (38%)
  starting transfers between devices  23.6 us (37%)
  Pallas kernels  12.9 us (20%)
  other arithmetic  1.33 us (2%)
  local copies, waits for them, and re-layouts  0.88 us (1%)
    ppermute x16, waiting for transfers between devices, move(): return lax.ppermute(value, AXES, pairs)  24.4 us
    ppermute x16, starting transfers between devices, move(): return lax.ppermute(value, AXES, pairs)  23.6 us
    pallas_call x1, Pallas kernels, contract(): pl.pallas_call(lambda *refs: contract_kernel(p, *refs), out_shape=shape_o...  3.47 us
    pallas_call x1, Pallas kernels, mix_basis(): pl.pallas_call(lambda *refs: mix_kernel(p, *refs), out_shape=[shape_of((2...  2.59 us
    pallas_call x1, Pallas kernels, pack_weights(): pl.pallas_call(lambda *refs: pack_kernel(p, *refs), out_shape=[shape_of((...  2.01 us
    pallas_call x1, Pallas kernels, normal_pieces(): pl.pallas_call(lambda *refs: normal_kernel(p, *refs), out_shape=[shape_of...  1.93 us
    pallas_call x1, Pallas kernels, mlp(): pl.pallas_call(lambda *refs: mlp_kernel(p, *refs), out_shape=shape_of(lat...  1.67 us
  transfers between devices with their start and end apart: 16, of which 8 were waited for; matrix products, arithmetic and copies ran while one was open for 3% of the time, Pallas kernels for 15%

profile of v4, /device:TPU:0, one launch (start us, length us, event | category | flops | bytes accessed | tf_op | source)
XLA Modules:
  0.0 63.3 jit_solution(15187867831655686378)
XLA Ops:
  0.0 1.9 %normalize.1 = (bf16[80,384]{1,0:T(8,128)(2,1)}, bf16[80,384]{1,0:T(8,128)(2,1)}, bf16[80,384]{1,0:T(8,128)(2,1)}, bf16[80,384]{1,0:T(8,128)(2,1)}) custom-call(s32[4,6]{1,0:T(4,128)} %bitcast.8, s32[4,6]{1,0:T(4,128)} %bitcast.9, bf16[6,2,8,640]{3,2,1,0:T(8,128)(2,1)} %refs_0_.3, f32[640]{0:T(1024)} %refs_3_.1, bf16[6,32,9]{2,1,0:T(8,128)(2,1)} %bitcast.7), custom_call_target="tpu_custom_call" | custom-call | tf_op jit(solution)/shard_map/normalize/pallas_call | solution.py:149
  1.9 0.5 collective-permute-start.1
  2.4 2.6 %collective-permute-start.2 = (bf16[80,384]{1,0:T(8,128)(2,1)}, bf16[80,384]{1,0:T(8,128)(2,1)S(1)}, u32[]{:S(2)}, u32[]{:S(2)}) collective-permute-start(bf16[80,384]{1,0:T(8,128)(2,1)} %get-tuple-element.29), channel_id=1, source_target_pairs={{0,16},{1,17},{2,18},{3,19},{4,20},{5,21},{6,22},{7,23},{8,24},{9,... | collective-permute-start | bytes 184328 | tf_op jit(solution)/shard_map/ppermute | solution.py:483
  5.0 1.4 %collective-permute-start.3 = (bf16[80,384]{1,0:T(8,128)(2,1)}, bf16[80,384]{1,0:T(8,128)(2,1)S(1)}, u32[]{:S(2)}, u32[]{:S(2)}) collective-permute-start(bf16[80,384]{1,0:T(8,128)(2,1)} %get-tuple-element.30), channel_id=1, source_target_pairs={{0,24},{1,25},{2,26},{3,27},{4,28},{5,29},{6,30},{7,31},{8,0},{9,1... | collective-permute-start | bytes 184328 | tf_op jit(solution)/shard_map/ppermute | solution.py:483
  6.4 2.0 %pack_weights.1 = (bf16[80,640]{1,0:T(8,128)(2,1)}, bf16[192,640]{1,0:T(8,128)(2,1)}) custom-call(bf16[9,160,80]{2,1,0:T(8,128)(2,1)} %refs_0_.2, bf16[160,160]{1,0:T(8,128)(2,1)} %refs_1_.1, bf16[80,320]{1,0:T(8,128)(2,1)} %bitcast.6), custom_call_target="tpu_custom_call" | custom-call | tf_op jit(solution)/shard_map/pack_weights/pallas_call | solution.py:179
  8.4 3.7 %collective-permute-start = (bf16[80,640]{1,0:T(8,128)(2,1)}, bf16[80,640]{1,0:T(8,128)(2,1)S(1)}, u32[]{:S(2)}, u32[]{:S(2)}) collective-permute-start(bf16[80,640]{1,0:T(8,128)(2,1)} %get-tuple-element.26), channel_id=1, source_target_pairs={{0,6},{1,7},{2,4},{3,5},{4,2},{5,3},{6,0},{7,1},{8,14},{9,15},{10,... | collective-permute-start | bytes 307208 | tf_op jit(solution)/shard_map/ppermute | solution.py:483
  12.0 0.8 %constant_dynamic-update-slice_fusion.4 = (bf16[384,384]{1,0:T(8,128)(2,1)S(1)}, bf16[48,384]{1,0:T(8,128)(2,1)S(1)}) fusion(bf16[80,384]{1,0:T(8,128)(2,1)} %get-tuple-element.24.refs_3_), kind=kLoop, calls=%fused_computation.9 | loop fusion | bytes 110592
  12.9 0.3 collective-permute-start.4
  13.2 3.0 %collective-permute-done = bf16[80,640]{1,0:T(8,128)(2,1)S(1)} collective-permute-done((bf16[80,640]{1,0:T(8,128)(2,1)}, bf16[80,640]{1,0:T(8,128)(2,1)S(1)}, u32[]{:S(2)}, u32[]{:S(2)}) %collective-permute-start) | collective-permute-done | bytes 102432 | tf_op jit(solution)/shard_map/ppermute | solution.py:483
  16.2 1.1 %pad_maximum_fusion.2 = bf16[352,640]{1,0:T(8,128)(2,1)S(1)} fusion(bf16[192,640]{1,0:T(8,128)(2,1)} %get-tuple-element.27.refs_1_, bf16[80,640]{1,0:T(8,128)(2,1)S(1)} %collective-permute-done, bf16[80,640]{1,0:T(8,128)(2,1)} %get-tuple-element.26), kind=kLoop, calls=%fused_computation.2 | loop fusion | flops 1351680 | bytes 901120 | tf_op jit(solution)/shard_map/concatenate | solution.py:531
  17.3 1.2 %collective-permute-done.4.refs_1_ = bf16[192,384]{1,0:T(8,128)(2,1)S(1)} collective-permute-done((bf16[192,384]{1,0:T(8,128)(2,1)S(1)}, bf16[192,384]{1,0:T(8,128)(2,1)S(1)}, u32[]{:S(2)}, u32[]{:S(2)}) %collective-permute-start.4) | collective-permute-done | bytes 147488 | tf_op jit(solution)/shard_map/ppermute | solution.py:483
  18.5 2.1 %collective-permute-start.5 = (bf16[352,640]{1,0:T(8,128)(2,1)S(1)}, bf16[352,640]{1,0:T(8,128)(2,1)S(1)}, u32[]{:S(2)}, u32[]{:S(2)}) collective-permute-start(bf16[352,640]{1,0:T(8,128)(2,1)S(1)} %pad_maximum_fusion.2), channel_id=1, source_target_pairs={{0,2},{1,3},{2,0},{3,1},{4,6},{5,7},{6,4},{7,5},{8,10},{9,11},{10,... | collective-permute-start | bytes 1351688 | tf_op jit(solution)/shard_map/ppermute | solution.py:483
  20.6 0.9 %collective-permute-start.6 = (bf16[384,384]{1,0:T(8,128)(2,1)S(1)}, bf16[384,384]{1,0:T(8,128)(2,1)S(1)}, u32[]{:S(2)}, u32[]{:S(2)}) collective-permute-start(bf16[384,384]{1,0:T(8,128)(2,1)S(1)} %constant_dynamic-update-slice_fusion), channel_id=1, source_target_pairs={{0,1},{1,0},{2,3},{3,2},{4,5},{5,4},{6,7},{7,6},{8,9},{9,8},{10,11... | collective-permute-start | bytes 884744 | tf_op jit(solution)/shard_map/ppermute | solution.py:483
  21.5 8.0 %collective-permute-done.5.refs_3_ = bf16[352,640]{1,0:T(8,128)(2,1)S(1)} collective-permute-done((bf16[352,640]{1,0:T(8,128)(2,1)S(1)}, bf16[352,640]{1,0:T(8,128)(2,1)S(1)}, u32[]{:S(2)}, u32[]{:S(2)}) %collective-permute-start.5) | collective-permute-done | bytes 450592 | tf_op jit(solution)/shard_map/ppermute | solution.py:483
  29.6 1.9 %collective-permute-start.7 = (bf16[320,640]{1,0:T(8,128)(2,1)S(1)}, bf16[320,640]{1,0:T(8,128)(2,1)S(1)}, u32[]{:S(2)}, u32[]{:S(2)}) collective-permute-start(bf16[320,640]{1,0:T(8,128)(2,1)S(1)} %pad_maximum_fusion.3), channel_id=1, source_target_pairs={{0,1},{1,0},{2,3},{3,2},{4,5},{5,4},{6,7},{7,6},{8,24},{9,25},{10,... | collective-permute-start | bytes 1228808 | tf_op jit(solution)/shard_map/ppermute | solution.py:483
  31.5 2.7 %collective-permute-start.8 = (bf16[192,640]{1,0:T(8,128)(2,1)S(1)}, bf16[192,640]{1,0:T(8,128)(2,1)S(1)}, u32[]{:S(2)}, u32[]{:S(2)}) collective-permute-start(bf16[192,640]{1,0:T(8,128)(2,1)S(1)} %copy-done), channel_id=1, source_target_pairs={{0,6},{1,7},{2,4},{3,5},{4,2},{5,3},{6,0},{7,1},{8,14},{9,15},{10,... | collective-permute-start | bytes 737288 | tf_op jit(solution)/shard_map/ppermute | solution.py:483
  34.2 3.5 %contract.1.refs_0_ = bf16[768,2304]{1,0:T(8,128)(2,1)S(1)} custom-call(bf16[192,384]{1,0:T(8,128)(2,1)S(1)} %pad_maximum_fusion.4.refs_0_, bf16[192,384]{1,0:T(8,128)(2,1)S(1)} %collective-permute-done.4.refs_1_, bf16[384,384]{1,0:T(8,128)(2,1)S(1)} %collective-permute-done.6.refs_2_, bf16[80,384]{1,0:T(8,128)(2,1)S(1)} %copy-done.2, ...), custom_call_target="tpu_custom_call" | custom-call | tf_op jit(solution)/shard_map/contract/pallas_call | solution.py:288
  37.8 1.8 %collective-permute-done.8.refs_2_ = bf16[192,640]{1,0:T(8,128)(2,1)S(1)} collective-permute-done((bf16[192,640]{1,0:T(8,128)(2,1)S(1)}, bf16[192,640]{1,0:T(8,128)(2,1)S(1)}, u32[]{:S(2)}, u32[]{:S(2)}) %collective-permute-start.8) | collective-permute-done | bytes 245792 | tf_op jit(solution)/shard_map/ppermute | solution.py:483
  39.6 1.8 %collective-permute-start.9 = (bf16[640,640]{1,0:T(8,128)(2,1)S(1)}, bf16[640,640]{1,0:T(8,128)(2,1)S(1)}, u32[]{:S(2)}, u32[]{:S(2)}) collective-permute-start(bf16[640,640]{1,0:T(8,128)(2,1)S(1)} %pad_maximum_fusion.1), channel_id=1, source_target_pairs={{0,16},{1,17},{2,18},{3,19},{4,20},{5,21},{6,22},{7,23},{8,9},{9,8... | collective-permute-start | bytes 2457608 | tf_op jit(solution)/shard_map/ppermute | solution.py:483
  41.4 2.0 %collective-permute-start.10 = (bf16[192,640]{1,0:T(8,128)(2,1)S(1)}, bf16[192,640]{1,0:T(8,128)(2,1)S(1)}, u32[]{:S(2)}, u32[]{:S(2)}) collective-permute-start(bf16[192,640]{1,0:T(8,128)(2,1)S(1)} %collective-permute-done.8.refs_2_), channel_id=1, source_target_pairs={{0,2},{1,3},{2,0},{3,1},{4,6},{5,7},{6,4},{7,5},{8,10},{9,11},{10,... | collective-permute-start | bytes 737288 | tf_op jit(solution)/shard_map/ppermute | solution.py:483
  43.4 6.7 %collective-permute-done.10.refs_4_ = bf16[192,640]{1,0:T(8,128)(2,1)S(1)} collective-permute-done((bf16[192,640]{1,0:T(8,128)(2,1)S(1)}, bf16[192,640]{1,0:T(8,128)(2,1)S(1)}, u32[]{:S(2)}, u32[]{:S(2)}) %collective-permute-start.10) | collective-permute-done | bytes 245792 | tf_op jit(solution)/shard_map/ppermute | solution.py:483
  50.1 2.6 %mix_basis.1 = (f32[4,96,320]{2,1,0:T(8,128)S(1)}, bf16[4,96,320]{2,1,0:T(8,128)(2,1)S(1)}) custom-call(bf16[768,2304]{1,0:T(8,128)(2,1)S(1)} %contract.1.refs_0_, bf16[192,640]{1,0:T(8,128)(2,1)S(1)} %copy-done, bf16[192,640]{1,0:T(8,128)(2,1)S(1)} %collective-permute-done.8.refs_2_, bf16[352,640]{1,0:T(8,128)(2,1)S(1)} %collective-permute-done.5.refs_3_, ...), custom_call_target="tpu_custom_call" | custom-call | tf_op jit(solution)/shard_map/mix_basis/pallas_call | solution.py:350
  52.7 1.6 %collective-permute-done.11.arrived = bf16[4,96,320]{2,1,0:T(8,128)(2,1)S(1)} collective-permute-done((bf16[4,96,320]{2,1,0:T(8,128)(2,1)S(1)}, bf16[4,96,320]{2,1,0:T(8,128)(2,1)S(1)}, u32[]{:S(2)}, u32[]{:S(2)}) %collective-permute-start.11) | collective-permute-done | bytes 245792 | tf_op jit(solution)/shard_map/ppermute | solution.py:483
  54.4 0.1 pad_maximum_fusion.refs_0_
  54.5 0.2 collective-permute-start.12
  54.7 0.3 collective-permute-start.13
  55.0 1.3 %collective-permute-start.14 = (bf16[96,320]{1,0:T(8,128)(2,1)S(1)}, bf16[96,320]{1,0:T(8,128)(2,1)S(1)}, u32[]{:S(2)}, u32[]{:S(2)}) collective-permute-start(bf16[96,320]{1,0:T(8,128)(2,1)S(1)} %get-tuple-element.41), channel_id=1, source_target_pairs={{0,16},{1,17},{2,18},{3,19},{4,20},{5,21},{6,22},{7,23},{8,24},{9,... | collective-permute-start | bytes 184328 | tf_op jit(solution)/shard_map/ppermute | solution.py:483
  56.4 1.9 %collective-permute-start.15 = (bf16[96,320]{1,0:T(8,128)(2,1)S(1)}, bf16[96,320]{1,0:T(8,128)(2,1)S(1)}, u32[]{:S(2)}, u32[]{:S(2)}) collective-permute-start(bf16[96,320]{1,0:T(8,128)(2,1)S(1)} %get-tuple-element.42), channel_id=1, source_target_pairs={{0,17},{1,16},{2,19},{3,18},{4,21},{5,20},{6,23},{7,22},{8,25},{9,... | collective-permute-start | bytes 184328 | tf_op jit(solution)/shard_map/ppermute | solution.py:483
  58.2 1.2 %mlp_weights.1 = (bf16[640,1280]{1,0:T(8,128)(2,1)S(1)}, bf16[640,1280]{1,0:T(8,128)(2,1)S(1)}) custom-call(bf16[1280,640]{1,0:T(8,128)(2,1)S(1)} %pad_maximum_fusion.refs_0_, bf16[1280,640]{1,0:T(8,128)(2,1)S(1)} %collective-permute-done.12.refs_1_), custom_call_target="tpu_custom_call" | custom-call | tf_op jit(solution)/shard_map/mlp_weights/pallas_call | solution.py:419
  59.5 0.3 collective-permute-done.13.refs_5_
  59.7 1.9 %collective-permute-done.15.refs_7_ = bf16[96,320]{1,0:T(8,128)(2,1)S(1)} collective-permute-done((bf16[96,320]{1,0:T(8,128)(2,1)S(1)}, bf16[96,320]{1,0:T(8,128)(2,1)S(1)}, u32[]{:S(2)}, u32[]{:S(2)}) %collective-permute-start.15) | collective-permute-done | bytes 61472 | tf_op jit(solution)/shard_map/ppermute | solution.py:483
  61.6 1.7 %sum_mlp.1 = bf16[6,2,8,640]{3,2,1,0:T(8,128)(2,1)} custom-call(bf16[6,2,8,640]{3,2,1,0:T(8,128)(2,1)S(1)} %copy-done.1, f32[1280]{0:T(1024)S(1)} %copy-done.3, bf16[640,1280]{1,0:T(8,128)(2,1)S(1)} %get-tuple-element.38.refs_2_, bf16[640,1280]{1,0:T(8,128)(2,1)S(1)} %get-tuple-element.39.refs_3_, f32[96,320]{1,0:T(8,128)S(1)} %get-tuple-element.36.refs_4_, ...), custom_call_target="tpu_custom_call" | custom-call | tf_op jit(solution)/shard_map/sum_mlp/pallas_call | solution.py:463
  (28 shorter events, 0.4 us)
Async XLA Ops:
  1.9 10.9 %collective-permute-start.1 = (bf16[80,384]{1,0:T(8,128)(2,1)}, bf16[80,384]{1,0:T(8,128)(2,1)S(1)}, u32[]{:S(2)}, u32[]{:S(2)}) collective-permute-start(bf16[80,384]{1,0:T(8,128)(2,1)} %get-tuple-element.28), channel_id=1, source_target_pairs={{0,8},{1,9},{2,10},{3,11},{4,12},{5,13},{6,14},{7,15},{8,16},{9,17... | collective-permute-start | bytes 184328 | tf_op jit(solution)/shard_map/ppermute | solution.py:483
  2.4 10.5 %collective-permute-start.2 = (bf16[80,384]{1,0:T(8,128)(2,1)}, bf16[80,384]{1,0:T(8,128)(2,1)S(1)}, u32[]{:S(2)}, u32[]{:S(2)}) collective-permute-start(bf16[80,384]{1,0:T(8,128)(2,1)} %get-tuple-element.29), channel_id=1, source_target_pairs={{0,16},{1,17},{2,18},{3,19},{4,20},{5,21},{6,22},{7,23},{8,24},{9,... | collective-permute-start | bytes 184328 | tf_op jit(solution)/shard_map/ppermute | solution.py:483
  5.0 7.9 %collective-permute-start.3 = (bf16[80,384]{1,0:T(8,128)(2,1)}, bf16[80,384]{1,0:T(8,128)(2,1)S(1)}, u32[]{:S(2)}, u32[]{:S(2)}) collective-permute-start(bf16[80,384]{1,0:T(8,128)(2,1)} %get-tuple-element.30), channel_id=1, source_target_pairs={{0,24},{1,25},{2,26},{3,27},{4,28},{5,29},{6,30},{7,31},{8,0},{9,1... | collective-permute-start | bytes 184328 | tf_op jit(solution)/shard_map/ppermute | solution.py:483
  8.4 21.2 %copy-start.4 = (bf16[80,640]{1,0:T(8,128)(2,1)S(1)}, bf16[80,640]{1,0:T(8,128)(2,1)}, u32[]{:S(2)}) copy-start(bf16[80,640]{1,0:T(8,128)(2,1)} %get-tuple-element.26) | copy-start | bytes 307204
  8.4 23.1 %copy-start = (bf16[192,640]{1,0:T(8,128)(2,1)S(1)}, bf16[192,640]{1,0:T(8,128)(2,1)}, u32[]{:S(2)}) copy-start(bf16[192,640]{1,0:T(8,128)(2,1)} %get-tuple-element.27.refs_1_) | copy-start | bytes 737284
  8.4 25.8 %copy-start.2 = (bf16[80,384]{1,0:T(8,128)(2,1)S(1)}, bf16[80,384]{1,0:T(8,128)(2,1)}, u32[]{:S(2)}) copy-start(bf16[80,384]{1,0:T(8,128)(2,1)} %get-tuple-element.24.refs_3_) | copy-start | bytes 184324
  8.4 7.8 %collective-permute-start = (bf16[80,640]{1,0:T(8,128)(2,1)}, bf16[80,640]{1,0:T(8,128)(2,1)S(1)}, u32[]{:S(2)}, u32[]{:S(2)}) collective-permute-start(bf16[80,640]{1,0:T(8,128)(2,1)} %get-tuple-element.26), channel_id=1, source_target_pairs={{0,6},{1,7},{2,4},{3,5},{4,2},{5,3},{6,0},{7,1},{8,14},{9,15},{10,... | collective-permute-start | bytes 307208 | tf_op jit(solution)/shard_map/ppermute | solution.py:483
  12.9 5.5 %collective-permute-start.4 = (bf16[192,384]{1,0:T(8,128)(2,1)S(1)}, bf16[192,384]{1,0:T(8,128)(2,1)S(1)}, u32[]{:S(2)}, u32[]{:S(2)}) collective-permute-start(bf16[192,384]{1,0:T(8,128)(2,1)S(1)} %pad_maximum_fusion.4.refs_0_), channel_id=1, source_target_pairs={{0,6},{1,3},{2,0},{3,5},{4,2},{5,7},{6,4},{7,1},{8,14},{9,11},{10,... | collective-permute-start | bytes 442376 | tf_op jit(solution)/shard_map/ppermute | solution.py:483
  18.5 11.0 %collective-permute-start.5 = (bf16[352,640]{1,0:T(8,128)(2,1)S(1)}, bf16[352,640]{1,0:T(8,128)(2,1)S(1)}, u32[]{:S(2)}, u32[]{:S(2)}) collective-permute-start(bf16[352,640]{1,0:T(8,128)(2,1)S(1)} %pad_maximum_fusion.2), channel_id=1, source_target_pairs={{0,2},{1,3},{2,0},{3,1},{4,6},{5,7},{6,4},{7,5},{8,10},{9,11},{10,... | collective-permute-start | bytes 1351688 | tf_op jit(solution)/shard_map/ppermute | solution.py:483
  20.6 9.0 %collective-permute-start.6 = (bf16[384,384]{1,0:T(8,128)(2,1)S(1)}, bf16[384,384]{1,0:T(8,128)(2,1)S(1)}, u32[]{:S(2)}, u32[]{:S(2)}) collective-permute-start(bf16[384,384]{1,0:T(8,128)(2,1)S(1)} %constant_dynamic-update-slice_fusion), channel_id=1, source_target_pairs={{0,1},{1,0},{2,3},{3,2},{4,5},{5,4},{6,7},{7,6},{8,9},{9,8},{10,11... | collective-permute-start | bytes 884744 | tf_op jit(solution)/shard_map/ppermute | solution.py:483
  29.6 8.1 %collective-permute-start.7 = (bf16[320,640]{1,0:T(8,128)(2,1)S(1)}, bf16[320,640]{1,0:T(8,128)(2,1)S(1)}, u32[]{:S(2)}, u32[]{:S(2)}) collective-permute-start(bf16[320,640]{1,0:T(8,128)(2,1)S(1)} %pad_maximum_fusion.3), channel_id=1, source_target_pairs={{0,1},{1,0},{2,3},{3,2},{4,5},{5,4},{6,7},{7,6},{8,24},{9,25},{10,... | collective-permute-start | bytes 1228808 | tf_op jit(solution)/shard_map/ppermute | solution.py:483
  31.5 8.1 %collective-permute-start.8 = (bf16[192,640]{1,0:T(8,128)(2,1)S(1)}, bf16[192,640]{1,0:T(8,128)(2,1)S(1)}, u32[]{:S(2)}, u32[]{:S(2)}) collective-permute-start(bf16[192,640]{1,0:T(8,128)(2,1)S(1)} %copy-done), channel_id=1, source_target_pairs={{0,6},{1,7},{2,4},{3,5},{4,2},{5,3},{6,0},{7,1},{8,14},{9,15},{10,... | collective-permute-start | bytes 737288 | tf_op jit(solution)/shard_map/ppermute | solution.py:483
  39.6 14.8 %collective-permute-start.9 = (bf16[640,640]{1,0:T(8,128)(2,1)S(1)}, bf16[640,640]{1,0:T(8,128)(2,1)S(1)}, u32[]{:S(2)}, u32[]{:S(2)}) collective-permute-start(bf16[640,640]{1,0:T(8,128)(2,1)S(1)} %pad_maximum_fusion.1), channel_id=1, source_target_pairs={{0,16},{1,17},{2,18},{3,19},{4,20},{5,21},{6,22},{7,23},{8,9},{9,8... | collective-permute-start | bytes 2457608 | tf_op jit(solution)/shard_map/ppermute | solution.py:483
  41.4 8.7 %collective-permute-start.10 = (bf16[192,640]{1,0:T(8,128)(2,1)S(1)}, bf16[192,640]{1,0:T(8,128)(2,1)S(1)}, u32[]{:S(2)}, u32[]{:S(2)}) collective-permute-start(bf16[192,640]{1,0:T(8,128)(2,1)S(1)} %collective-permute-done.8.refs_2_), channel_id=1, source_target_pairs={{0,2},{1,3},{2,0},{3,1},{4,6},{5,7},{6,4},{7,5},{8,10},{9,11},{10,... | collective-permute-start | bytes 737288 | tf_op jit(solution)/shard_map/ppermute | solution.py:483
  52.6 1.6 %collective-permute-start.11 = (bf16[4,96,320]{2,1,0:T(8,128)(2,1)S(1)}, bf16[4,96,320]{2,1,0:T(8,128)(2,1)S(1)}, u32[]{:S(2)}, u32[]{:S(2)}) collective-permute-start(bf16[4,96,320]{2,1,0:T(8,128)(2,1)S(1)} %get-tuple-element.35), channel_id=1, source_target_pairs={{0,8},{1,9},{2,10},{3,11},{4,12},{5,13},{6,14},{7,15},{8,0},{9,1},... | collective-permute-start | bytes 737288 | tf_op jit(solution)/shard_map/ppermute | solution.py:483
  54.5 3.7 %collective-permute-start.12 = (bf16[1280,640]{1,0:T(8,128)(2,1)S(1)}, bf16[1280,640]{1,0:T(8,128)(2,1)S(1)}, u32[]{:S(2)}, u32[]{:S(2)}) collective-permute-start(bf16[1280,640]{1,0:T(8,128)(2,1)S(1)} %pad_maximum_fusion.refs_0_), channel_id=1, source_target_pairs={{0,8},{1,9},{2,10},{3,11},{4,12},{5,13},{6,14},{7,15},{8,0},{9,1},... | collective-permute-start | bytes 4915208 | tf_op jit(solution)/shard_map/ppermute | solution.py:483
  54.7 5.0 %collective-permute-start.13 = (bf16[96,320]{1,0:T(8,128)(2,1)S(1)}, bf16[96,320]{1,0:T(8,128)(2,1)S(1)}, u32[]{:S(2)}, u32[]{:S(2)}) collective-permute-start(bf16[96,320]{1,0:T(8,128)(2,1)S(1)} %get-tuple-element.40), channel_id=1, source_target_pairs={{0,1},{1,0},{2,3},{3,2},{4,5},{5,4},{6,7},{7,6},{8,9},{9,8},{10,11... | collective-permute-start | bytes 184328 | tf_op jit(solution)/shard_map/ppermute | solution.py:483
  55.0 4.7 %collective-permute-start.14 = (bf16[96,320]{1,0:T(8,128)(2,1)S(1)}, bf16[96,320]{1,0:T(8,128)(2,1)S(1)}, u32[]{:S(2)}, u32[]{:S(2)}) collective-permute-start(bf16[96,320]{1,0:T(8,128)(2,1)S(1)} %get-tuple-element.41), channel_id=1, source_target_pairs={{0,16},{1,17},{2,18},{3,19},{4,20},{5,21},{6,22},{7,23},{8,24},{9,... | collective-permute-start | bytes 184328 | tf_op jit(solution)/shard_map/ppermute | solution.py:483
  56.4 5.3 %copy-start.1 = (bf16[6,2,8,640]{3,2,1,0:T(8,128)(2,1)S(1)}, bf16[6,2,8,640]{3,2,1,0:T(8,128)(2,1)}, u32[]{:S(2)}) copy-start(bf16[6,2,8,640]{3,2,1,0:T(8,128)(2,1)} %refs_0_.3) | copy-start | bytes 368644
  56.4 5.3 %copy-start.3 = (f32[1280]{0:T(1024)S(1)}, f32[1280]{0:T(1024)}, u32[]{:S(2)}) copy-start(f32[1280]{0:T(1024)} %refs_1_.2) | copy-start | bytes 15364
  56.4 5.3 %collective-permute-start.15 = (bf16[96,320]{1,0:T(8,128)(2,1)S(1)}, bf16[96,320]{1,0:T(8,128)(2,1)S(1)}, u32[]{:S(2)}, u32[]{:S(2)}) collective-permute-start(bf16[96,320]{1,0:T(8,128)(2,1)S(1)} %get-tuple-element.42), channel_id=1, source_target_pairs={{0,17},{1,16},{2,19},{3,18},{4,21},{5,20},{6,23},{7,22},{8,25},{9,... | collective-permute-start | bytes 184328 | tf_op jit(solution)/shard_map/ppermute | solution.py:483

commit v5 on v4

--- a/solution.py
+++ b/solution.py
@@ -526,7 +526,7 @@
     own = jnp.concatenate([piece[: p.body] for piece in pieces], axis=0)
     far = move(own, lambda i, j: (i, j + 2 if j % 2 else j - 2))
     both = move(jnp.concatenate([own, far], axis=0), lambda i, j: (i, j ^ 1))
-    contracted = contract(p, own, far, both, pieces)
+    contracted = contract(p, own, far, after(both, turned), pieces)
 
     near = jnp.concatenate([mlp_pack, move(mlp_pack, mirror), mix_pack], axis=0)
     next_to = move(after(near, far), beside)

time: 63.5 us -> 67.2 us (1.058)
  waiting for transfers between devices: 24.4 us -> 28 us
    ppermute x16, waiting for transfers between devices: 24.4 us -> 28 us  [move(): return lax.ppermute(value, AXES, pairs)]
  transfers between devices with their start and end apart: 16 -> 16, of which waited for: 8 -> 8; matrix products, arithmetic and copies ran while one was open for 3% -> 3% of each run, Pallas kernels for 15% -> 14%
where the time goes in v5:
time: 67.2 us; the launch traced here: 66.9 us
  waiting for transfers between devices  28 us (42%)
  starting transfers between devices  23.6 us (35%)
  Pallas kernels  12.9 us (19%)
  other arithmetic  1.33 us (2%)
  local copies, waits for them, and re-layouts  0.88 us (1%)
    ppermute x16, waiting for transfers between devices, move(): return lax.ppermute(value, AXES, pairs)  28 us
    ppermute x16, starting transfers between devices, move(): return lax.ppermute(value, AXES, pairs)  23.6 us
    pallas_call x1, Pallas kernels, contract(): pl.pallas_call(lambda *refs: contract_kernel(p, *refs), out_shape=shape_o...  3.47 us
    pallas_call x1, Pallas kernels, mix_basis(): pl.pallas_call(lambda *refs: mix_kernel(p, *refs), out_shape=[shape_of((2...  2.59 us
    pallas_call x1, Pallas kernels, pack_weights(): pl.pallas_call(lambda *refs: pack_kernel(p, *refs), out_shape=[shape_of((...  2.01 us
    pallas_call x1, Pallas kernels, normal_pieces(): pl.pallas_call(lambda *refs: normal_kernel(p, *refs), out_shape=[shape_of...  1.93 us
    pallas_call x1, Pallas kernels, mlp(): pl.pallas_call(lambda *refs: mlp_kernel(p, *refs), out_shape=shape_of(lat...  1.67 us
  transfers between devices with their start and end apart: 16, of which 8 were waited for; matrix products, arithmetic and copies ran while one was open for 3% of the time, Pallas kernels for 14%

profile of v5, /device:TPU:0, one launch (start us, length us, event | category | flops | bytes accessed | tf_op | source)
XLA Modules:
  0.0 66.9 jit_solution(3431782003100866886)
XLA Ops:
  0.0 1.9 %normalize.1 = (bf16[80,384]{1,0:T(8,128)(2,1)}, bf16[80,384]{1,0:T(8,128)(2,1)}, bf16[80,384]{1,0:T(8,128)(2,1)}, bf16[80,384]{1,0:T(8,128)(2,1)}) custom-call(s32[4,6]{1,0:T(4,128)} %bitcast.8, s32[4,6]{1,0:T(4,128)} %bitcast.9, bf16[6,2,8,640]{3,2,1,0:T(8,128)(2,1)} %refs_0_.3, f32[640]{0:T(1024)} %refs_3_.1, bf16[6,32,9]{2,1,0:T(8,128)(2,1)} %bitcast.7), custom_call_target="tpu_custom_call" | custom-call | tf_op jit(solution)/shard_map/normalize/pallas_call | solution.py:149
  1.9 0.5 collective-permute-start.1
  2.4 2.6 %collective-permute-start.2 = (bf16[80,384]{1,0:T(8,128)(2,1)}, bf16[80,384]{1,0:T(8,128)(2,1)S(1)}, u32[]{:S(2)}, u32[]{:S(2)}) collective-permute-start(bf16[80,384]{1,0:T(8,128)(2,1)} %get-tuple-element.30), channel_id=1, source_target_pairs={{0,16},{1,17},{2,18},{3,19},{4,20},{5,21},{6,22},{7,23},{8,24},{9,... | collective-permute-start | bytes 184328 | tf_op jit(solution)/shard_map/ppermute | solution.py:483
  5.0 1.4 %collective-permute-start.3 = (bf16[80,384]{1,0:T(8,128)(2,1)}, bf16[80,384]{1,0:T(8,128)(2,1)S(1)}, u32[]{:S(2)}, u32[]{:S(2)}) collective-permute-start(bf16[80,384]{1,0:T(8,128)(2,1)} %get-tuple-element.31), channel_id=1, source_target_pairs={{0,24},{1,25},{2,26},{3,27},{4,28},{5,29},{6,30},{7,31},{8,0},{9,1... | collective-permute-start | bytes 184328 | tf_op jit(solution)/shard_map/ppermute | solution.py:483
  6.4 2.0 %pack_weights.1 = (bf16[80,640]{1,0:T(8,128)(2,1)}, bf16[192,640]{1,0:T(8,128)(2,1)}) custom-call(bf16[9,160,80]{2,1,0:T(8,128)(2,1)} %refs_0_.2, bf16[160,160]{1,0:T(8,128)(2,1)} %refs_1_.1, bf16[80,320]{1,0:T(8,128)(2,1)} %bitcast.6), custom_call_target="tpu_custom_call" | custom-call | tf_op jit(solution)/shard_map/pack_weights/pallas_call | solution.py:179
  8.4 3.7 %collective-permute-start = (bf16[80,640]{1,0:T(8,128)(2,1)}, bf16[80,640]{1,0:T(8,128)(2,1)S(1)}, u32[]{:S(2)}, u32[]{:S(2)}) collective-permute-start(bf16[80,640]{1,0:T(8,128)(2,1)} %get-tuple-element.27), channel_id=1, source_target_pairs={{0,6},{1,7},{2,4},{3,5},{4,2},{5,3},{6,0},{7,1},{8,14},{9,15},{10,... | collective-permute-start | bytes 307208 | tf_op jit(solution)/shard_map/ppermute | solution.py:483
  12.0 0.8 %constant_dynamic-update-slice_fusion.4 = (bf16[384,384]{1,0:T(8,128)(2,1)S(1)}, bf16[48,384]{1,0:T(8,128)(2,1)S(1)}) fusion(bf16[80,384]{1,0:T(8,128)(2,1)} %get-tuple-element.25.refs_3_), kind=kLoop, calls=%fused_computation.9 | loop fusion | bytes 110592
  12.9 0.3 collective-permute-start.4
  13.2 3.0 %collective-permute-done = bf16[80,640]{1,0:T(8,128)(2,1)S(1)} collective-permute-done((bf16[80,640]{1,0:T(8,128)(2,1)}, bf16[80,640]{1,0:T(8,128)(2,1)S(1)}, u32[]{:S(2)}, u32[]{:S(2)}) %collective-permute-start) | collective-permute-done | bytes 102432 | tf_op jit(solution)/shard_map/ppermute | solution.py:483
  16.2 1.1 %pad_maximum_fusion.2 = bf16[352,640]{1,0:T(8,128)(2,1)S(1)} fusion(bf16[192,640]{1,0:T(8,128)(2,1)} %get-tuple-element.28.refs_1_, bf16[80,640]{1,0:T(8,128)(2,1)S(1)} %collective-permute-done, bf16[80,640]{1,0:T(8,128)(2,1)} %get-tuple-element.27), kind=kLoop, calls=%fused_computation.2 | loop fusion | flops 1351680 | bytes 901120 | tf_op jit(solution)/shard_map/concatenate | solution.py:531
  17.3 1.2 %collective-permute-done.4.refs_1_ = bf16[192,384]{1,0:T(8,128)(2,1)S(1)} collective-permute-done((bf16[192,384]{1,0:T(8,128)(2,1)S(1)}, bf16[192,384]{1,0:T(8,128)(2,1)S(1)}, u32[]{:S(2)}, u32[]{:S(2)}) %collective-permute-start.4) | collective-permute-done | bytes 147488 | tf_op jit(solution)/shard_map/ppermute | solution.py:483
  18.5 2.1 %collective-permute-start.5 = (bf16[352,640]{1,0:T(8,128)(2,1)S(1)}, bf16[352,640]{1,0:T(8,128)(2,1)S(1)}, u32[]{:S(2)}, u32[]{:S(2)}) collective-permute-start(bf16[352,640]{1,0:T(8,128)(2,1)S(1)} %pad_maximum_fusion.2), channel_id=1, source_target_pairs={{0,2},{1,3},{2,0},{3,1},{4,6},{5,7},{6,4},{7,5},{8,10},{9,11},{10,... | collective-permute-start | bytes 1351688 | tf_op jit(solution)/shard_map/ppermute | solution.py:483
  20.6 0.9 %collective-permute-start.6 = (bf16[384,384]{1,0:T(8,128)(2,1)S(1)}, bf16[384,384]{1,0:T(8,128)(2,1)S(1)}, u32[]{:S(2)}, u32[]{:S(2)}) collective-permute-start(bf16[384,384]{1,0:T(8,128)(2,1)S(1)} %constant_dynamic-update-slice_fusion), channel_id=1, source_target_pairs={{0,1},{1,0},{2,3},{3,2},{4,5},{5,4},{6,7},{7,6},{8,9},{9,8},{10,11... | collective-permute-start | bytes 884744 | tf_op jit(solution)/shard_map/ppermute | solution.py:483
  21.5 8.0 %collective-permute-done.5.refs_3_ = bf16[352,640]{1,0:T(8,128)(2,1)S(1)} collective-permute-done((bf16[352,640]{1,0:T(8,128)(2,1)S(1)}, bf16[352,640]{1,0:T(8,128)(2,1)S(1)}, u32[]{:S(2)}, u32[]{:S(2)}) %collective-permute-start.5) | collective-permute-done | bytes 450592 | tf_op jit(solution)/shard_map/ppermute | solution.py:483
  29.6 1.9 %collective-permute-start.7 = (bf16[320,640]{1,0:T(8,128)(2,1)S(1)}, bf16[320,640]{1,0:T(8,128)(2,1)S(1)}, u32[]{:S(2)}, u32[]{:S(2)}) collective-permute-start(bf16[320,640]{1,0:T(8,128)(2,1)S(1)} %pad_maximum_fusion.3), channel_id=1, source_target_pairs={{0,1},{1,0},{2,3},{3,2},{4,5},{5,4},{6,7},{7,6},{8,24},{9,25},{10,... | collective-permute-start | bytes 1228808 | tf_op jit(solution)/shard_map/ppermute | solution.py:483
  31.5 2.7 %collective-permute-start.8 = (bf16[192,640]{1,0:T(8,128)(2,1)S(1)}, bf16[192,640]{1,0:T(8,128)(2,1)S(1)}, u32[]{:S(2)}, u32[]{:S(2)}) collective-permute-start(bf16[192,640]{1,0:T(8,128)(2,1)S(1)} %copy-done), channel_id=1, source_target_pairs={{0,6},{1,7},{2,4},{3,5},{4,2},{5,3},{6,0},{7,1},{8,14},{9,15},{10,... | collective-permute-start | bytes 737288 | tf_op jit(solution)/shard_map/ppermute | solution.py:483
  34.2 5.4 %collective-permute-done.8.refs_2_ = bf16[192,640]{1,0:T(8,128)(2,1)S(1)} collective-permute-done((bf16[192,640]{1,0:T(8,128)(2,1)S(1)}, bf16[192,640]{1,0:T(8,128)(2,1)S(1)}, u32[]{:S(2)}, u32[]{:S(2)}) %collective-permute-start.8) | collective-permute-done | bytes 245792 | tf_op jit(solution)/shard_map/ppermute | solution.py:483
  39.6 3.5 %contract.1.refs_0_ = bf16[768,2304]{1,0:T(8,128)(2,1)S(1)} custom-call(bf16[192,384]{1,0:T(8,128)(2,1)S(1)} %pad_maximum_fusion.4.refs_0_, bf16[192,384]{1,0:T(8,128)(2,1)S(1)} %collective-permute-done.4.refs_1_, bf16[384,384]{1,0:T(8,128)(2,1)S(1)} %collective-permute-done.6.refs_2_, bf16[80,384]{1,0:T(8,128)(2,1)S(1)} %copy-done.2, ...), custom_call_target="tpu_custom_call" | custom-call | tf_op jit(solution)/shard_map/contract/pallas_call | solution.py:288
  43.2 1.8 %collective-permute-start.9 = (bf16[640,640]{1,0:T(8,128)(2,1)S(1)}, bf16[640,640]{1,0:T(8,128)(2,1)S(1)}, u32[]{:S(2)}, u32[]{:S(2)}) collective-permute-start(bf16[640,640]{1,0:T(8,128)(2,1)S(1)} %pad_maximum_fusion.1), channel_id=1, source_target_pairs={{0,16},{1,17},{2,18},{3,19},{4,20},{5,21},{6,22},{7,23},{8,9},{9,8... | collective-permute-start | bytes 2457608 | tf_op jit(solution)/shard_map/ppermute | solution.py:483
  45.0 2.0 %collective-permute-start.10 = (bf16[192,640]{1,0:T(8,128)(2,1)S(1)}, bf16[192,640]{1,0:T(8,128)(2,1)S(1)}, u32[]{:S(2)}, u32[]{:S(2)}) collective-permute-start(bf16[192,640]{1,0:T(8,128)(2,1)S(1)} %collective-permute-done.8.refs_2_), channel_id=1, source_target_pairs={{0,2},{1,3},{2,0},{3,1},{4,6},{5,7},{6,4},{7,5},{8,10},{9,11},{10,... | collective-permute-start | bytes 737288 | tf_op jit(solution)/shard_map/ppermute | solution.py:483
  47.0 6.7 %collective-permute-done.10.refs_4_ = bf16[192,640]{1,0:T(8,128)(2,1)S(1)} collective-permute-done((bf16[192,640]{1,0:T(8,128)(2,1)S(1)}, bf16[192,640]{1,0:T(8,128)(2,1)S(1)}, u32[]{:S(2)}, u32[]{:S(2)}) %collective-permute-start.10) | collective-permute-done | bytes 245792 | tf_op jit(solution)/shard_map/ppermute | solution.py:483
  53.7 2.6 %mix_basis.1 = (f32[4,96,320]{2,1,0:T(8,128)S(1)}, bf16[4,96,320]{2,1,0:T(8,128)(2,1)S(1)}) custom-call(bf16[768,2304]{1,0:T(8,128)(2,1)S(1)} %contract.1.refs_0_, bf16[192,640]{1,0:T(8,128)(2,1)S(1)} %copy-done, bf16[192,640]{1,0:T(8,128)(2,1)S(1)} %collective-permute-done.8.refs_2_, bf16[352,640]{1,0:T(8,128)(2,1)S(1)} %collective-permute-done.5.refs_3_, ...), custom_call_target="tpu_custom_call" | custom-call | tf_op jit(solution)/shard_map/mix_basis/pallas_call | solution.py:350
  56.4 1.6 %collective-permute-done.11.arrived = bf16[4,96,320]{2,1,0:T(8,128)(2,1)S(1)} collective-permute-done((bf16[4,96,320]{2,1,0:T(8,128)(2,1)S(1)}, bf16[4,96,320]{2,1,0:T(8,128)(2,1)S(1)}, u32[]{:S(2)}, u32[]{:S(2)}) %collective-permute-start.11) | collective-permute-done | bytes 245792 | tf_op jit(solution)/shard_map/ppermute | solution.py:483
  58.0 0.1 pad_maximum_fusion.refs_0_
  58.2 0.2 collective-permute-start.12
  58.4 0.4 collective-permute-start.13
  58.7 1.3 %collective-permute-start.14 = (bf16[96,320]{1,0:T(8,128)(2,1)S(1)}, bf16[96,320]{1,0:T(8,128)(2,1)S(1)}, u32[]{:S(2)}, u32[]{:S(2)}) collective-permute-start(bf16[96,320]{1,0:T(8,128)(2,1)S(1)} %get-tuple-element.43), channel_id=1, source_target_pairs={{0,16},{1,17},{2,18},{3,19},{4,20},{5,21},{6,22},{7,23},{8,24},{9,... | collective-permute-start | bytes 184328 | tf_op jit(solution)/shard_map/ppermute | solution.py:483
  60.0 1.9 %collective-permute-start.15 = (bf16[96,320]{1,0:T(8,128)(2,1)S(1)}, bf16[96,320]{1,0:T(8,128)(2,1)S(1)}, u32[]{:S(2)}, u32[]{:S(2)}) collective-permute-start(bf16[96,320]{1,0:T(8,128)(2,1)S(1)} %get-tuple-element.44), channel_id=1, source_target_pairs={{0,17},{1,16},{2,19},{3,18},{4,21},{5,20},{6,23},{7,22},{8,25},{9,... | collective-permute-start | bytes 184328 | tf_op jit(solution)/shard_map/ppermute | solution.py:483
  61.9 1.2 %mlp_weights.1 = (bf16[640,1280]{1,0:T(8,128)(2,1)S(1)}, bf16[640,1280]{1,0:T(8,128)(2,1)S(1)}) custom-call(bf16[1280,640]{1,0:T(8,128)(2,1)S(1)} %pad_maximum_fusion.refs_0_, bf16[1280,640]{1,0:T(8,128)(2,1)S(1)} %collective-permute-done.12.refs_1_), custom_call_target="tpu_custom_call" | custom-call | tf_op jit(solution)/shard_map/mlp_weights/pallas_call | solution.py:419
  63.1 0.2 collective-permute-done.13.refs_5_
  63.3 2.0 %collective-permute-done.15.refs_7_ = bf16[96,320]{1,0:T(8,128)(2,1)S(1)} collective-permute-done((bf16[96,320]{1,0:T(8,128)(2,1)S(1)}, bf16[96,320]{1,0:T(8,128)(2,1)S(1)}, u32[]{:S(2)}, u32[]{:S(2)}) %collective-permute-start.15) | collective-permute-done | bytes 61472 | tf_op jit(solution)/shard_map/ppermute | solution.py:483
  65.3 1.7 %sum_mlp.1 = bf16[6,2,8,640]{3,2,1,0:T(8,128)(2,1)} custom-call(bf16[6,2,8,640]{3,2,1,0:T(8,128)(2,1)S(1)} %copy-done.1, f32[1280]{0:T(1024)S(1)} %copy-done.3, bf16[640,1280]{1,0:T(8,128)(2,1)S(1)} %get-tuple-element.40.refs_2_, bf16[640,1280]{1,0:T(8,128)(2,1)S(1)} %get-tuple-element.41.refs_3_, f32[96,320]{1,0:T(8,128)S(1)} %get-tuple-element.38.refs_4_, ...), custom_call_target="tpu_custom_call" | custom-call | tf_op jit(solution)/shard_map/sum_mlp/pallas_call | solution.py:463
  (28 shorter events, 0.4 us)
Async XLA Ops:
  1.9 10.9 %collective-permute-start.1 = (bf16[80,384]{1,0:T(8,128)(2,1)}, bf16[80,384]{1,0:T(8,128)(2,1)S(1)}, u32[]{:S(2)}, u32[]{:S(2)}) collective-permute-start(bf16[80,384]{1,0:T(8,128)(2,1)} %get-tuple-element.29), channel_id=1, source_target_pairs={{0,8},{1,9},{2,10},{3,11},{4,12},{5,13},{6,14},{7,15},{8,16},{9,17... | collective-permute-start | bytes 184328 | tf_op jit(solution)/shard_map/ppermute | solution.py:483
  2.4 10.5 %collective-permute-start.2 = (bf16[80,384]{1,0:T(8,128)(2,1)}, bf16[80,384]{1,0:T(8,128)(2,1)S(1)}, u32[]{:S(2)}, u32[]{:S(2)}) collective-permute-start(bf16[80,384]{1,0:T(8,128)(2,1)} %get-tuple-element.30), channel_id=1, source_target_pairs={{0,16},{1,17},{2,18},{3,19},{4,20},{5,21},{6,22},{7,23},{8,24},{9,... | collective-permute-start | bytes 184328 | tf_op jit(solution)/shard_map/ppermute | solution.py:483
  5.0 7.9 %collective-permute-start.3 = (bf16[80,384]{1,0:T(8,128)(2,1)}, bf16[80,384]{1,0:T(8,128)(2,1)S(1)}, u32[]{:S(2)}, u32[]{:S(2)}) collective-permute-start(bf16[80,384]{1,0:T(8,128)(2,1)} %get-tuple-element.31), channel_id=1, source_target_pairs={{0,24},{1,25},{2,26},{3,27},{4,28},{5,29},{6,30},{7,31},{8,0},{9,1... | collective-permute-start | bytes 184328 | tf_op jit(solution)/shard_map/ppermute | solution.py:483
  8.4 21.2 %copy-start.4 = (bf16[80,640]{1,0:T(8,128)(2,1)S(1)}, bf16[80,640]{1,0:T(8,128)(2,1)}, u32[]{:S(2)}) copy-start(bf16[80,640]{1,0:T(8,128)(2,1)} %get-tuple-element.27) | copy-start | bytes 307204
  8.4 23.1 %copy-start = (bf16[192,640]{1,0:T(8,128)(2,1)S(1)}, bf16[192,640]{1,0:T(8,128)(2,1)}, u32[]{:S(2)}) copy-start(bf16[192,640]{1,0:T(8,128)(2,1)} %get-tuple-element.28.refs_1_) | copy-start | bytes 737284
  8.4 31.2 %copy-start.2 = (bf16[80,384]{1,0:T(8,128)(2,1)S(1)}, bf16[80,384]{1,0:T(8,128)(2,1)}, u32[]{:S(2)}) copy-start(bf16[80,384]{1,0:T(8,128)(2,1)} %get-tuple-element.25.refs_3_) | copy-start | bytes 184324
  8.4 7.8 %collective-permute-start = (bf16[80,640]{1,0:T(8,128)(2,1)}, bf16[80,640]{1,0:T(8,128)(2,1)S(1)}, u32[]{:S(2)}, u32[]{:S(2)}) collective-permute-start(bf16[80,640]{1,0:T(8,128)(2,1)} %get-tuple-element.27), channel_id=1, source_target_pairs={{0,6},{1,7},{2,4},{3,5},{4,2},{5,3},{6,0},{7,1},{8,14},{9,15},{10,... | collective-permute-start | bytes 307208 | tf_op jit(solution)/shard_map/ppermute | solution.py:483
  12.9 5.5 %collective-permute-start.4 = (bf16[192,384]{1,0:T(8,128)(2,1)S(1)}, bf16[192,384]{1,0:T(8,128)(2,1)S(1)}, u32[]{:S(2)}, u32[]{:S(2)}) collective-permute-start(bf16[192,384]{1,0:T(8,128)(2,1)S(1)} %pad_maximum_fusion.4.refs_0_), channel_id=1, source_target_pairs={{0,6},{1,3},{2,0},{3,5},{4,2},{5,7},{6,4},{7,1},{8,14},{9,11},{10,... | collective-permute-start | bytes 442376 | tf_op jit(solution)/shard_map/ppermute | solution.py:483
  18.5 11.0 %collective-permute-start.5 = (bf16[352,640]{1,0:T(8,128)(2,1)S(1)}, bf16[352,640]{1,0:T(8,128)(2,1)S(1)}, u32[]{:S(2)}, u32[]{:S(2)}) collective-permute-start(bf16[352,640]{1,0:T(8,128)(2,1)S(1)} %pad_maximum_fusion.2), channel_id=1, source_target_pairs={{0,2},{1,3},{2,0},{3,1},{4,6},{5,7},{6,4},{7,5},{8,10},{9,11},{10,... | collective-permute-start | bytes 1351688 | tf_op jit(solution)/shard_map/ppermute | solution.py:483
  20.6 9.0 %collective-permute-start.6 = (bf16[384,384]{1,0:T(8,128)(2,1)S(1)}, bf16[384,384]{1,0:T(8,128)(2,1)S(1)}, u32[]{:S(2)}, u32[]{:S(2)}) collective-permute-start(bf16[384,384]{1,0:T(8,128)(2,1)S(1)} %constant_dynamic-update-slice_fusion), channel_id=1, source_target_pairs={{0,1},{1,0},{2,3},{3,2},{4,5},{5,4},{6,7},{7,6},{8,9},{9,8},{10,11... | collective-permute-start | bytes 884744 | tf_op jit(solution)/shard_map/ppermute | solution.py:483
  29.6 13.5 %collective-permute-start.7 = (bf16[320,640]{1,0:T(8,128)(2,1)S(1)}, bf16[320,640]{1,0:T(8,128)(2,1)S(1)}, u32[]{:S(2)}, u32[]{:S(2)}) collective-permute-start(bf16[320,640]{1,0:T(8,128)(2,1)S(1)} %pad_maximum_fusion.3), channel_id=1, source_target_pairs={{0,1},{1,0},{2,3},{3,2},{4,5},{5,4},{6,7},{7,6},{8,24},{9,25},{10,... | collective-permute-start | bytes 1228808 | tf_op jit(solution)/shard_map/ppermute | solution.py:483
  31.5 8.1 %collective-permute-start.8 = (bf16[192,640]{1,0:T(8,128)(2,1)S(1)}, bf16[192,640]{1,0:T(8,128)(2,1)S(1)}, u32[]{:S(2)}, u32[]{:S(2)}) collective-permute-start(bf16[192,640]{1,0:T(8,128)(2,1)S(1)} %copy-done), channel_id=1, source_target_pairs={{0,6},{1,7},{2,4},{3,5},{4,2},{5,3},{6,0},{7,1},{8,14},{9,15},{10,... | collective-permute-start | bytes 737288 | tf_op jit(solution)/shard_map/ppermute | solution.py:483
  43.2 14.8 %collective-permute-start.9 = (bf16[640,640]{1,0:T(8,128)(2,1)S(1)}, bf16[640,640]{1,0:T(8,128)(2,1)S(1)}, u32[]{:S(2)}, u32[]{:S(2)}) collective-permute-start(bf16[640,640]{1,0:T(8,128)(2,1)S(1)} %pad_maximum_fusion.1), channel_id=1, source_target_pairs={{0,16},{1,17},{2,18},{3,19},{4,20},{5,21},{6,22},{7,23},{8,9},{9,8... | collective-permute-start | bytes 2457608 | tf_op jit(solution)/shard_map/ppermute | solution.py:483
  45.0 8.7 %collective-permute-start.10 = (bf16[192,640]{1,0:T(8,128)(2,1)S(1)}, bf16[192,640]{1,0:T(8,128)(2,1)S(1)}, u32[]{:S(2)}, u32[]{:S(2)}) collective-permute-start(bf16[192,640]{1,0:T(8,128)(2,1)S(1)} %collective-permute-done.8.refs_2_), channel_id=1, source_target_pairs={{0,2},{1,3},{2,0},{3,1},{4,6},{5,7},{6,4},{7,5},{8,10},{9,11},{10,... | collective-permute-start | bytes 737288 | tf_op jit(solution)/shard_map/ppermute | solution.py:483
  56.3 1.6 %collective-permute-start.11 = (bf16[4,96,320]{2,1,0:T(8,128)(2,1)S(1)}, bf16[4,96,320]{2,1,0:T(8,128)(2,1)S(1)}, u32[]{:S(2)}, u32[]{:S(2)}) collective-permute-start(bf16[4,96,320]{2,1,0:T(8,128)(2,1)S(1)} %get-tuple-element.37), channel_id=1, source_target_pairs={{0,8},{1,9},{2,10},{3,11},{4,12},{5,13},{6,14},{7,15},{8,0},{9,1},... | collective-permute-start | bytes 737288 | tf_op jit(solution)/shard_map/ppermute | solution.py:483
  58.2 3.7 %collective-permute-start.12 = (bf16[1280,640]{1,0:T(8,128)(2,1)S(1)}, bf16[1280,640]{1,0:T(8,128)(2,1)S(1)}, u32[]{:S(2)}, u32[]{:S(2)}) collective-permute-start(bf16[1280,640]{1,0:T(8,128)(2,1)S(1)} %pad_maximum_fusion.refs_0_), channel_id=1, source_target_pairs={{0,8},{1,9},{2,10},{3,11},{4,12},{5,13},{6,14},{7,15},{8,0},{9,1},... | collective-permute-start | bytes 4915208 | tf_op jit(solution)/shard_map/ppermute | solution.py:483
  58.4 4.9 %collective-permute-start.13 = (bf16[96,320]{1,0:T(8,128)(2,1)S(1)}, bf16[96,320]{1,0:T(8,128)(2,1)S(1)}, u32[]{:S(2)}, u32[]{:S(2)}) collective-permute-start(bf16[96,320]{1,0:T(8,128)(2,1)S(1)} %get-tuple-element.42), channel_id=1, source_target_pairs={{0,1},{1,0},{2,3},{3,2},{4,5},{5,4},{6,7},{7,6},{8,9},{9,8},{10,11... | collective-permute-start | bytes 184328 | tf_op jit(solution)/shard_map/ppermute | solution.py:483
  58.7 4.5 %collective-permute-start.14 = (bf16[96,320]{1,0:T(8,128)(2,1)S(1)}, bf16[96,320]{1,0:T(8,128)(2,1)S(1)}, u32[]{:S(2)}, u32[]{:S(2)}) collective-permute-start(bf16[96,320]{1,0:T(8,128)(2,1)S(1)} %get-tuple-element.43), channel_id=1, source_target_pairs={{0,16},{1,17},{2,18},{3,19},{4,20},{5,21},{6,22},{7,23},{8,24},{9,... | collective-permute-start | bytes 184328 | tf_op jit(solution)/shard_map/ppermute | solution.py:483
  60.0 5.3 %copy-start.1 = (bf16[6,2,8,640]{3,2,1,0:T(8,128)(2,1)S(1)}, bf16[6,2,8,640]{3,2,1,0:T(8,128)(2,1)}, u32[]{:S(2)}) copy-start(bf16[6,2,8,640]{3,2,1,0:T(8,128)(2,1)} %refs_0_.3) | copy-start | bytes 368644
  60.0 5.3 %copy-start.3 = (f32[1280]{0:T(1024)S(1)}, f32[1280]{0:T(1024)}, u32[]{:S(2)}) copy-start(f32[1280]{0:T(1024)} %refs_1_.2) | copy-start | bytes 15364
  60.0 5.3 %collective-permute-start.15 = (bf16[96,320]{1,0:T(8,128)(2,1)S(1)}, bf16[96,320]{1,0:T(8,128)(2,1)S(1)}, u32[]{:S(2)}, u32[]{:S(2)}) collective-permute-start(bf16[96,320]{1,0:T(8,128)(2,1)S(1)} %get-tuple-element.44), channel_id=1, source_target_pairs={{0,17},{1,16},{2,19},{3,18},{4,21},{5,20},{6,23},{7,22},{8,25},{9,... | collective-permute-start | bytes 184328 | tf_op jit(solution)/shard_map/ppermute | solution.py:483
